TPU v7x, 32 devices: a whole 2x2x4 slice. The times are simulated.
32 devices in a mesh: dp: 4 (over y, core), expert: 8 (over z, x).
Axes of the slice: x: 2, y: 2, z: 4, core: 2. Of those that a mesh axis runs over, the one named last changes fastest.
Arguments:
- tokens: bfloat16 [8192, 1536], P(('dp', 'expert')), may hold values from -6 to 6
- seq_lengths: int32 [32, 4], P(('dp', 'expert')), may hold values from 1 to 128, 256 in all within a row
- routes: int32 [8192, 8], P(('dp', 'expert')), may hold values from 0 to 15, all different within a row; in each aligned block of 256 rows (0 to 255, 256 to 511, ...) at most 160 rows name the same one
- w_query: bfloat16 [1536, 1536], P('dp'), may hold values from -0.15625 to 0.15625
- w_key: bfloat16 [1536, 512], P('dp'), may hold values from -0.15625 to 0.15625
- w_value: bfloat16 [1536, 512], P('dp'), may hold values from -0.15625 to 0.15625
- w_output: bfloat16 [1536, 1536], P('dp'), may hold values from -0.625 to 0.625
- w_router: bfloat16 [1536, 16], P('dp'), may hold values from -0.078125 to 0.078125
- attn_gain: bfloat16 [1536], P('dp'), may hold values from 0.099609375 to 1.8984375
- moe_gain: bfloat16 [1536], P('dp'), may hold values from 0.099609375 to 1.8984375
- expert_gate: bfloat16 [16, 1536, 512], P('expert'), may hold values from -0.15625 to 0.15625
- expert_up: bfloat16 [16, 1536, 512], P('expert'), may hold values from -0.15625 to 0.15625
- expert_down: bfloat16 [16, 1536, 512], P('expert'), may hold values from -1 to 1
- out_grad: bfloat16 [8192, 1536], P(('dp', 'expert')), may hold values from -6 to 6
Outputs:
- layer_out: bfloat16 [8192, 1536], P(('dp', 'expert'))
- in_grad: float32 [8192, 1536], P(('dp', 'expert'))
- grad_query: float32 [1536, 1536], P('dp')
- grad_key: float32 [1536, 512], P('dp')
- grad_value: float32 [1536, 512], P('dp')
- grad_output: float32 [1536, 1536], P('dp')
- grad_router: float32 [1536, 16], P('dp')
- grad_attn_gain: float32 [1536], P('dp')
- grad_moe_gain: float32 [1536], P('dp')
- grad_gate: float32 [16, 1536, 512], P('expert', 'dp')
- grad_up: float32 [16, 1536, 512], P('expert', 'dp')
- grad_down: float32 [16, 1536, 512], P('expert', 'dp')
Inputs may be any that keep to these rules, and one draw needn't show every extreme that they name: `seq_lengths`: row b gives the lengths of the sequences of block b; they sum to 256, and the longest is 128. `routes`: each row names 8 different experts. In the rows of one block no expert is named more than 160 times, and in some block some expert is named exactly 160 times.
All inputs are finite; a program needn't handle non-finite values.
Results may differ from a plain program's by a relative error of at most 0.022.
Values may be sent and summed in bfloat16 or wider, within the bound.
A program may use at most 256 MiB of HBM per device.

v0:
```python
import jax
import jax.numpy as jnp
from jax import lax
from jax.sharding import PartitionSpec as P

QH = 24
KVH = 8
HD = 64
TOP = 8


eps = 1e-06
rope_base = 10000.0
masked_score = -1e30


def shortened(value):
    return jax.tree.map(lambda a: a.astype(jnp.bfloat16) if a.dtype == jnp.float32 else a, value)


def rms_scale(values):
    return lax.rsqrt(jnp.mean(values * values, axis=-1, keepdims=True) + eps)


def token_layout(lengths_row, row_count):
    token_index = jnp.arange(row_count, dtype=jnp.int32)
    seq_ends = jnp.cumsum(lengths_row)
    passed = (token_index[:, None] >= seq_ends[None, :]).astype(jnp.int32)
    doc_id = jnp.sum(passed, axis=1)
    seq_start = jnp.sum(passed * lengths_row[None, :], axis=1)
    return (doc_id, token_index - seq_start)


def rope_tables(position):
    half_size = HD // 2
    frequency = rope_base ** (-2.0 * jnp.arange(half_size, dtype=jnp.float32) / HD)
    angles = position.astype(jnp.float32)[:, None] * frequency[None, :]
    return (jnp.cos(angles)[:, None, :], jnp.sin(angles)[:, None, :])


def rotate(values, cos_table, sin_table, head_count):
    half_size = HD // 2
    shaped = values.reshape(values.shape[0], head_count, HD)
    front_half = shaped[..., :half_size]
    back_half = shaped[..., half_size:]
    turned = jnp.concatenate(
        [
            front_half * cos_table - back_half * sin_table,
            back_half * cos_table + front_half * sin_table,
        ],
        axis=-1,
    )
    return turned.reshape(values.shape[0], head_count * HD)


def unrotate(values, cos_table, sin_table, head_count):
    half_size = HD // 2
    shaped = values.reshape(values.shape[0], head_count, HD)
    front_half = shaped[..., :half_size]
    back_half = shaped[..., half_size:]
    turned = jnp.concatenate(
        [
            front_half * cos_table + back_half * sin_table,
            back_half * cos_table - front_half * sin_table,
        ],
        axis=-1,
    )
    return turned.reshape(values.shape[0], head_count * HD)


def expert_slots(route_rows, expert_count, capacity):
    flat_routes = route_rows.reshape(-1)
    pair_count = flat_routes.shape[0]
    matches = (flat_routes[:, None] == jnp.arange(expert_count, dtype=jnp.int32)[None, :]).astype(
        jnp.int32
    )
    earlier = jnp.cumsum(matches, axis=0) - matches
    slot_rank = jnp.sum(earlier * matches, axis=1)
    slot_table = jnp.full((expert_count, capacity), pair_count, jnp.int32)
    slot_table = slot_table.at[flat_routes, slot_rank].set(jnp.arange(pair_count, dtype=jnp.int32))
    return (slot_table, slot_rank)


def body(
    tokens,
    seq_lengths,
    routes,
    w_query,
    w_key,
    w_value,
    w_output,
    w_router,
    attn_gain,
    moe_gain,
    expert_gate,
    expert_up,
    expert_down,
    out_grad,
):
    shards = (w_query, w_key, w_value, w_output, w_router, attn_gain, moe_gain)
    gathered = (
        lax.all_gather(shards[0], "dp", axis=0, tiled=True),
        lax.all_gather(shards[1], "dp", axis=0, tiled=True),
        lax.all_gather(shards[2], "dp", axis=0, tiled=True),
        lax.all_gather(shards[3], "dp", axis=0, tiled=True),
        lax.all_gather(shards[4], "dp", axis=0, tiled=True),
        lax.all_gather(shards[5], "dp", axis=0, tiled=True),
        lax.all_gather(shards[6], "dp", axis=0, tiled=True),
    )
    query_w, key_w, value_w, output_w, router_w, gain_one, gain_two = gathered
    row_count = tokens.shape[0]
    width = tokens.shape[1]
    expert_count = w_router.shape[1]
    capacity = 5 * row_count * TOP // (4 * expert_count)
    group_size = QH // KVH
    block_rows = min(512, row_count)
    block_total = row_count // block_rows
    score_scale = HD ** (-0.5)
    doc_id, position = token_layout(seq_lengths[0], row_count)
    cos_table, sin_table = rope_tables(position)
    token_index = jnp.arange(row_count, dtype=jnp.int32)
    block_starts = jnp.arange(block_total, dtype=jnp.int32) * block_rows
    inputs = tokens.astype(jnp.float32)
    scale_one = rms_scale(inputs)
    normed_one = inputs * scale_one
    hidden_one = (normed_one * gain_one.astype(jnp.float32)).astype(jnp.bfloat16)
    query_rot = rotate(
        jnp.dot(hidden_one, query_w, preferred_element_type=jnp.float32), cos_table, sin_table, QH
    ).astype(jnp.bfloat16)
    key_rot = rotate(
        jnp.dot(hidden_one, key_w, preferred_element_type=jnp.float32), cos_table, sin_table, KVH
    ).astype(jnp.bfloat16)
    value_rows = jnp.dot(hidden_one, value_w, preferred_element_type=jnp.float32).astype(
        jnp.bfloat16
    )
    key_heads = key_rot.reshape(row_count, KVH, HD)
    value_heads = value_rows.reshape(row_count, KVH, HD)

    def block_scores(block_start):
        query_block = query_rot.reshape(block_rows, KVH, group_size, HD)
        raw_scores = (
            jnp.einsum("tkgd,ukd->kgtu", query_block, key_heads, preferred_element_type=jnp.float32)
            * score_scale
        )
        block_index = block_start + jnp.arange(block_rows, dtype=jnp.int32)
        allowed = (doc_id[:, None] == doc_id[None, :]) & (
            token_index[None, :] <= block_index[:, None]
        )
        return (query_block, jnp.where(allowed, raw_scores, masked_score))

    def attend_block(block_start):
        query_block, scores = block_scores(block_start)
        row_top = jnp.max(scores, axis=-1, keepdims=True)
        exp_terms = jnp.exp(scores - row_top)
        row_total = jnp.sum(exp_terms, axis=-1, keepdims=True)
        probs_low = (exp_terms / row_total).astype(jnp.bfloat16)
        attended_block = jnp.einsum(
            "kgtu,ukd->tkgd", probs_low, value_heads, preferred_element_type=jnp.float32
        )
        log_total = (row_top + jnp.log(row_total))[..., 0]
        return (attended_block.reshape(block_rows, QH * HD).astype(jnp.bfloat16), log_total)

    attended_blocks, log_blocks = lax.map(attend_block, block_starts)
    attended = attended_blocks.reshape(row_count, QH * HD)
    residual = inputs + jnp.dot(attended, output_w, preferred_element_type=jnp.float32)
    scale_two = rms_scale(residual)
    normed_two = residual * scale_two
    hidden_two = (normed_two * gain_two.astype(jnp.float32)).astype(jnp.bfloat16)
    logits = jnp.dot(hidden_two, router_w, preferred_element_type=jnp.float32)
    expert_ids = jnp.arange(expert_count, dtype=jnp.int32)
    route_hot = (routes[:, :, None] == expert_ids[None, None, :]).astype(jnp.float32)
    chosen = jnp.sum(route_hot * logits[:, None, :], axis=-1)
    gate_probs = jax.nn.softmax(chosen, axis=-1)
    slot_table, slot_rank = expert_slots(routes, expert_count, capacity)
    flat_routes = routes.reshape(-1)
    zero_row = jnp.zeros((1, width), jnp.bfloat16)
    padded = jnp.concatenate([hidden_two, zero_row], axis=0)
    outgoing = padded[slot_table // TOP]
    arrived = lax.all_to_all(outgoing, "expert", split_axis=0, concat_axis=1, tiled=True)
    gate_pre = jnp.einsum("erd,edf->erf", arrived, expert_gate, preferred_element_type=jnp.float32)
    up_pre = jnp.einsum("erd,edf->erf", arrived, expert_up, preferred_element_type=jnp.float32)
    gate_sig = jax.nn.sigmoid(gate_pre)
    gate_act = gate_pre * gate_sig
    activation = (gate_act * up_pre).astype(jnp.bfloat16)
    expert_out = jnp.einsum(
        "erf,edf->erd", activation, expert_down, preferred_element_type=jnp.float32
    ).astype(jnp.bfloat16)
    returned = lax.all_to_all(expert_out, "expert", split_axis=1, concat_axis=0, tiled=True)
    per_pair = returned[flat_routes, slot_rank].reshape(row_count, TOP, width)
    mixture = jnp.sum(gate_probs[:, :, None] * per_pair, axis=1)
    layer_out = (residual + mixture).astype(jnp.bfloat16)
    upstream = out_grad.astype(jnp.float32)
    pair_grad = (gate_probs[:, :, None] * upstream[:, None, :]).astype(jnp.bfloat16)
    gate_grad = jnp.sum(upstream[:, None, :] * per_pair, axis=-1)
    flat_grad = jnp.concatenate([pair_grad.reshape(row_count * TOP, width), zero_row], axis=0)
    slot_grads = flat_grad[slot_table]
    grad_arrived = lax.all_to_all(slot_grads, "expert", split_axis=0, concat_axis=1, tiled=True)
    act_grad = jnp.einsum(
        "erd,edf->erf", grad_arrived, expert_down, preferred_element_type=jnp.float32
    )
    gate_pre_grad = (act_grad * up_pre * gate_sig * (1.0 + gate_pre * (1.0 - gate_sig))).astype(
        jnp.bfloat16
    )
    up_pre_grad = (act_grad * gate_act).astype(jnp.bfloat16)
    down_partial = jnp.einsum(
        "erd,erf->edf", grad_arrived, activation, preferred_element_type=jnp.float32
    )
    gate_partial = jnp.einsum(
        "erd,erf->edf", arrived, gate_pre_grad, preferred_element_type=jnp.float32
    )
    up_partial = jnp.einsum(
        "erd,erf->edf", arrived, up_pre_grad, preferred_element_type=jnp.float32
    )
    row_grad = jnp.einsum(
        "erf,edf->erd", gate_pre_grad, expert_gate, preferred_element_type=jnp.float32
    )
    row_grad = (
        row_grad
        + jnp.einsum("erf,edf->erd", up_pre_grad, expert_up, preferred_element_type=jnp.float32)
    ).astype(jnp.bfloat16)
    grad_returned = lax.all_to_all(row_grad, "expert", split_axis=1, concat_axis=0, tiled=True)
    pair_rows = grad_returned[flat_routes, slot_rank].reshape(row_count, TOP, width)
    hidden_two_grad = jnp.sum(pair_rows.astype(jnp.float32), axis=1)
    chosen_grad = gate_probs * (gate_grad - jnp.sum(gate_probs * gate_grad, axis=-1, keepdims=True))
    logit_grad = jnp.sum(route_hot * chosen_grad[:, :, None], axis=1).astype(jnp.bfloat16)
    hidden_two_grad = hidden_two_grad + jnp.dot(
        logit_grad, router_w.T, preferred_element_type=jnp.float32
    )
    gain_two_partial = jnp.sum(hidden_two_grad * normed_two, axis=0)
    normed_two_grad = hidden_two_grad * gain_two.astype(jnp.float32)
    residual_grad = upstream + scale_two * (
        normed_two_grad
        - normed_two * jnp.mean(normed_two_grad * normed_two, axis=-1, keepdims=True)
    )
    branch_grad = residual_grad.astype(jnp.bfloat16)
    attended_grad = jnp.dot(branch_grad, output_w.T, preferred_element_type=jnp.float32).astype(
        jnp.bfloat16
    )

    def attend_back(carry, block_data):
        key_acc, value_acc = carry
        block_start, log_total = block_data
        query_block, scores = block_scores(block_start)
        attn_probs = jnp.exp(scores - log_total[..., None])
        probs_low = attn_probs.astype(jnp.bfloat16)
        grad_block = attended_grad.reshape(block_rows, KVH, group_size, HD)
        prob_grad = jnp.einsum(
            "tkgd,ukd->kgtu", grad_block, value_heads, preferred_element_type=jnp.float32
        )
        score_grad = (
            attn_probs * (prob_grad - jnp.sum(attn_probs * prob_grad, axis=-1, keepdims=True))
        ).astype(jnp.bfloat16)
        query_part = (
            jnp.einsum("kgtu,ukd->tkgd", score_grad, key_heads, preferred_element_type=jnp.float32)
            * score_scale
        )
        key_acc = (
            key_acc
            + jnp.einsum(
                "kgtu,tkgd->ukd", score_grad, query_block, preferred_element_type=jnp.float32
            )
            * score_scale
        )
        value_acc = value_acc + jnp.einsum(
            "kgtu,tkgd->ukd", probs_low, grad_block, preferred_element_type=jnp.float32
        )
        return ((key_acc, value_acc), query_part.reshape(block_rows, QH * HD))

    zero_heads = jnp.zeros((row_count, KVH, HD), jnp.float32)
    (key_sums, value_sums), query_blocks = lax.scan(
        attend_back, (zero_heads, zero_heads), (block_starts, log_blocks)
    )
    query_grad = unrotate(
        query_blocks.reshape(row_count, QH * HD), cos_table, sin_table, QH
    ).astype(jnp.bfloat16)
    key_grad = unrotate(key_sums.reshape(row_count, KVH * HD), cos_table, sin_table, KVH).astype(
        jnp.bfloat16
    )
    value_grad = value_sums.reshape(row_count, KVH * HD).astype(jnp.bfloat16)
    hidden_one_grad = jnp.dot(query_grad, query_w.T, preferred_element_type=jnp.float32)
    hidden_one_grad = hidden_one_grad + jnp.dot(
        key_grad, key_w.T, preferred_element_type=jnp.float32
    )
    hidden_one_grad = hidden_one_grad + jnp.dot(
        value_grad, value_w.T, preferred_element_type=jnp.float32
    )
    gain_one_partial = jnp.sum(hidden_one_grad * normed_one, axis=0)
    normed_one_grad = hidden_one_grad * gain_one.astype(jnp.float32)
    in_grad = residual_grad + scale_one * (
        normed_one_grad
        - normed_one * jnp.mean(normed_one_grad * normed_one, axis=-1, keepdims=True)
    )
    query_partial = jnp.dot(hidden_one.T, query_grad, preferred_element_type=jnp.float32)
    key_partial = jnp.dot(hidden_one.T, key_grad, preferred_element_type=jnp.float32)
    value_partial = jnp.dot(hidden_one.T, value_grad, preferred_element_type=jnp.float32)
    output_partial = jnp.dot(attended.T, branch_grad, preferred_element_type=jnp.float32)
    router_partial = jnp.dot(hidden_two.T, logit_grad, preferred_element_type=jnp.float32)
    pieces = jax.tree.map(
        lambda part: part.astype(jnp.float32),
        lax.psum_scatter(
            shortened(
                (
                    query_partial,
                    key_partial,
                    value_partial,
                    output_partial,
                    router_partial,
                    gain_one_partial,
                    gain_two_partial,
                )
            ),
            "dp",
            scatter_dimension=0,
            tiled=True,
        ),
    )
    totals = (
        lax.psum(pieces[0].astype(jnp.bfloat16), "expert").astype(jnp.float32),
        lax.psum(pieces[1].astype(jnp.bfloat16), "expert").astype(jnp.float32),
        lax.psum(pieces[2].astype(jnp.bfloat16), "expert").astype(jnp.float32),
        lax.psum(pieces[3].astype(jnp.bfloat16), "expert").astype(jnp.float32),
        lax.psum(pieces[4].astype(jnp.bfloat16), "expert").astype(jnp.float32),
        lax.psum(pieces[5].astype(jnp.bfloat16), "expert").astype(jnp.float32),
        lax.psum(pieces[6].astype(jnp.bfloat16), "expert").astype(jnp.float32),
    )
    expert_totals = (
        lax.psum_scatter(
            gate_partial.astype(jnp.bfloat16), "dp", scatter_dimension=1, tiled=True
        ).astype(jnp.float32),
        lax.psum_scatter(
            up_partial.astype(jnp.bfloat16), "dp", scatter_dimension=1, tiled=True
        ).astype(jnp.float32),
        lax.psum_scatter(
            down_partial.astype(jnp.bfloat16), "dp", scatter_dimension=1, tiled=True
        ).astype(jnp.float32),
    )
    return (
        layer_out,
        in_grad,
        totals[0],
        totals[1],
        totals[2],
        totals[3],
        totals[4],
        totals[5],
        totals[6],
        expert_totals[0],
        expert_totals[1],
        expert_totals[2],
    )


def solution(mesh):
    placed = (
        P(("dp", "expert"), None),
        P(("dp", "expert"), None),
        P(("dp", "expert"), None),
        P("dp", None),
        P("dp", None),
        P("dp", None),
        P("dp", None),
        P("dp", None),
        P("dp"),
        P("dp"),
        P("expert", None, None),
        P("expert", None, None),
        P("expert", None, None),
        P(("dp", "expert"), None),
    )
    return jax.shard_map(
        body,
        mesh=mesh,
        in_specs=placed,
        out_specs=(
            P(("dp", "expert"), None),
            P(("dp", "expert"), None),
            P("dp", None),
            P("dp", None),
            P("dp", None),
            P("dp", None),
            P("dp", None),
            P("dp"),
            P("dp"),
            P("expert", "dp", None),
            P("expert", "dp", None),
            P("expert", "dp", None),
        ),
        check_vma=False,
    )
```

profile of v0, /device:TPU:0, one launch (start us, length us, event | category | flops | bytes accessed | tf_op | source)
XLA Modules:
  0.0 1480.4 jit_solution(6461521647750548897)
XLA Ops:
  56.2 36.5 %all-gather.11.cloned.1.call-done = bf16[1536,1536]{1,0:T(8,128)(2,1)} async-done(((bf16[384,1536]{1,0:T(8,128)(2,1)}), bf16[1536,1536]{1,0:T(8,128)(2,1)}) %all-gather.11.cloned.1.call-update) | async-done | bytes 4718608 | tf_op jit(solution)/shard_map/all_gather | solution.py:102
  104.2 27.4 %all-gather.13.cloned.1.call-done = bf16[1536,1536]{1,0:T(8,128)(2,1)} async-done(((bf16[384,1536]{1,0:T(8,128)(2,1)}), bf16[1536,1536]{1,0:T(8,128)(2,1)}) %all-gather.13.cloned.1.call-update) | async-done | bytes 4718608 | tf_op jit(solution)/shard_map/all_gather | solution.py:105
  146.5 20.0 %gather_fusion.2 = bf16[2560,1536]{1,0:T(8,128)(2,1)} fusion(bf16[2049,1536]{1,0:T(8,128)(2,1)} %concatenate.31, s32[3072]{0:T(1024)S(1)} %copy-done.47), kind=kCustom, calls=%fused_computation.2 | custom fusion | bytes 15738880 | tf_op jit(solution)/shard_map/gather | solution.py:196
  174.3 17.6 %gather_fusion = bf16[2560,1536]{1,0:T(8,128)(2,1)} fusion(bf16[257,1536]{1,0:T(8,128)(2,1)} %concatenate.29, s32[3072]{0:T(1024)S(1)} %pad_clamp_fusion.1), kind=kCustom, calls=%fused_computation | custom fusion | bytes 15738880 | tf_op jit(solution)/shard_map/gather | solution.py:178
  192.0 152.6 %all-to-all-done.2 = bf16[16,160,1536]{2,1,0:T(8,128)(2,1)} async-done(((bf16[16,160,1536]{2,1,0:T(8,128)(2,1)}), bf16[16,160,1536]{2,1,0:T(8,128)(2,1)}, u32[]{:S(2)}, u32[]{:S(2)}) %all-to-all-start.2) | async-done | bytes 7864352 | tf_op jit(solution)/shard_map/all_to_all | solution.py:197
  357.0 164.3 %all-to-all-done = bf16[16,160,1536]{2,1,0:T(8,128)(2,1)} async-done(((bf16[16,160,1536]{2,1,0:T(8,128)(2,1)}), bf16[16,160,1536]{2,1,0:T(8,128)(2,1)}, u32[]{:S(2)}, u32[]{:S(2)}) %all-to-all-start) | async-done | bytes 7864352 | tf_op jit(solution)/shard_map/all_to_all | solution.py:179
  544.1 10.8 multiply_convert_fusion
  559.4 43.7 %copy.121 = bf16[2,1280,1536]{2,0,1:T(2,128)(2,1)} copy(bf16[2,1280,1536]{2,1,0:T(8,128)(2,1)S(1)} %convolution_convert_fusion) | data formatting | bytes 15728640 | tf_op jit(solution)/shard_map/convert_element_type | solution.py:187
  618.0 14.7 add_convert_fusion
  632.7 15.6 %copy.125 = bf16[2,1280,1536]{2,0,1:T(2,128)(2,1)} copy(bf16[2,1280,1536]{2,1,0:T(8,128)(2,1)} %add_convert_fusion) | data formatting | bytes 15728640 | tf_op jit(solution)/shard_map/convert_element_type | solution.py:220
  648.3 130.9 %all-to-all-done.1 = bf16[2,1280,1536]{2,0,1:T(2,128)(2,1)} async-done(((bf16[2,1280,1536]{2,0,1:T(2,128)(2,1)}), bf16[2,1280,1536]{2,0,1:T(2,128)(2,1)}, u32[]{:S(2)}, u32[]{:S(2)}) %all-to-all-start.1) | async-done | bytes 7864352 | tf_op jit(solution)/shard_map/all_to_all | solution.py:188
  792.3 46.3 %gather_fusion.1 = bf16[2048,1536]{1,0:T(8,128)(2,1)} fusion(bf16[16,160,1536]{2,1,0:T(8,128)(2,1)} %bitcast.158, s32[2048]{0:T(1024)S(1)} %bitcast.156), kind=kCustom, calls=%fused_computation.1 | custom fusion | bytes 12599296 | tf_op jit(solution)/shard_map/gather | solution.py:189
  848.4 106.6 %all-to-all-done.3 = bf16[2,1280,1536]{2,0,1:T(2,128)(2,1)} async-done(((bf16[2,1280,1536]{2,0,1:T(2,128)(2,1)}), bf16[2,1280,1536]{2,0,1:T(2,128)(2,1)}, u32[]{:S(2)}, u32[]{:S(2)}) %all-to-all-start.3) | async-done | bytes 7864352 | tf_op jit(solution)/shard_map/all_to_all | solution.py:221
  962.9 46.5 %gather_fusion.3 = bf16[2048,1536]{1,0:T(8,128)(2,1)} fusion(bf16[16,160,1536]{2,1,0:T(8,128)(2,1)} %bitcast.159, s32[2048]{0:T(1024)S(1)} %bitcast.157), kind=kCustom, calls=%fused_computation.3 | custom fusion | bytes 12599296 | tf_op jit(solution)/shard_map/gather | solution.py:222
  1053.2 9.9 convolution_convert_fusion.3
  1063.2 10.2 convolution_convert_fusion.4
  1073.7 10.0 convolution_convert_fusion.5
  1086.1 48.8 %reduce-scatter.17.cloned.1.call-done = bf16[384,1536]{1,0:T(8,128)(2,1)} async-done(((bf16[1536,1536]{1,0:T(8,128)(2,1)}), bf16[384,1536]{1,0:T(8,128)(2,1)}) %reduce-scatter.17.cloned.1.call-update) | async-done | bytes 1179664 | tf_op jit(solution)/shard_map/reduce_scatter | solution.py:300
  1134.8 50.6 %reduce-scatter.11.cloned.1.call-done = bf16[384,1536]{1,0:T(8,128)(2,1)} async-done(((bf16[1536,1536]{1,0:T(8,128)(2,1)}), bf16[384,1536]{1,0:T(8,128)(2,1)}) %reduce-scatter.11.cloned.1.call-update) | async-done | bytes 1179664 | tf_op jit(solution)/shard_map/reduce_scatter | solution.py:300
  1186.7 39.2 %reduce-scatter.23.cloned.1.call-done = bf16[2,384,512]{2,1,0:T(8,128)(2,1)} async-done(((bf16[2,1536,512]{2,1,0:T(8,128)(2,1)}), bf16[2,384,512]{2,1,0:T(8,128)(2,1)}) %reduce-scatter.23.cloned.1.call-update) | async-done | bytes 786448 | tf_op jit(solution)/shard_map/reduce_scatter | solution.py:333
  1228.5 38.0 %reduce-scatter.21.cloned.1.call-done = bf16[2,384,512]{2,1,0:T(8,128)(2,1)} async-done(((bf16[2,1536,512]{2,1,0:T(8,128)(2,1)}), bf16[2,384,512]{2,1,0:T(8,128)(2,1)}) %reduce-scatter.21.cloned.1.call-update) | async-done | bytes 786448 | tf_op jit(solution)/shard_map/reduce_scatter | solution.py:330
  1269.0 38.1 %reduce-scatter.19.cloned.1.call-done = bf16[2,384,512]{2,1,0:T(8,128)(2,1)} async-done(((bf16[2,1536,512]{2,1,0:T(8,128)(2,1)}), bf16[2,384,512]{2,1,0:T(8,128)(2,1)}) %reduce-scatter.19.cloned.1.call-update) | async-done | bytes 786448 | tf_op jit(solution)/shard_map/reduce_scatter | solution.py:327
  1331.9 39.1 %all-reduce.4 = (bf16[384,16]{0,1:T(8,128)(2,1)S(1)}, bf16[384]{0:T(512)(128)(2,1)S(1)}, bf16[384]{0:T(512)(128)(2,1)S(1)}) all-reduce(bf16[384,16]{0,1:T(8,128)(2,1)S(1)} %copy.150, bf16[384]{0:T(512)(128)(2,1)S(1)} %dynamic-slice.1, bf16[384]{0:T(512)(128)(2,1)S(1)} %dynamic-slice.3), channel_id=1, replica_groups=mesh['dp'=4,'expert'=8] {'expert'}, use_global_device_ids=true, to_apply=%region_31.32 | all-reduce | flops 6912 | bytes 27648 | tf_op jit(solution)/shard_map/psum | solution.py:322
  1372.7 93.4 %all-reduce.9.cloned.1.call-done = (bf16[384,1536]{1,0:T(8,128)(2,1)}, bf16[384,512]{1,0:T(8,128)(2,1)}, bf16[384,512]{1,0:T(8,128)(2,1)}, bf16[384,1536]{1,0:T(8,128)(2,1)}) async-done(((bf16[384,1536]{1,0:T(8,128)(2,1)}, bf16[384,512]{1,0:T(8,128)(2,1)}, bf16[384,512]{1,0:T(8,128)(2,1)}, bf16[384,1536]{1,0:T(8,128)(2,1)}), (bf16[384,1536]{1,0:T(8,128)(2,1)}, bf16[384,512]{1,0:T(8,128)(2,1)}, ...) | async-done | bytes 3145744 | tf_op jit(solution)/shard_map/psum | solution.py:318
  (299 shorter events, 253.9 us)
Async XLA Ops:
  7.2 536.9 %copy-start = (bf16[2,1536,512]{2,1,0:T(8,128)(2,1)S(1)}, bf16[2,1536,512]{2,1,0:T(8,128)(2,1)}, u32[]{:S(2)}) copy-start(bf16[2,1536,512]{2,1,0:T(8,128)(2,1)} %param.26) | copy-start | bytes 9437188
  7.3 41.2 %all-gather.7.cloned.1.call-start = ((), (), s32[]{:S(2)}) async-start(), calls=%async_computation.12 | async-start | bytes 1966080 | tf_op jit(solution)/shard_map/all_gather | solution.py:104
  8.0 45.6 %all-gather.9.cloned.1.call-start = ((), (), s32[]{:S(2)}) async-start(), calls=%async_computation.13 | async-start | bytes 1966080 | tf_op jit(solution)/shard_map/all_gather | solution.py:103
  8.8 83.9 %all-gather.11.cloned.1.call-start = ((), (), s32[]{:S(2)}) async-start(), calls=%async_computation.14 | async-start | bytes 5898240 | tf_op jit(solution)/shard_map/all_gather | solution.py:102
  9.5 122.1 %all-gather.13.cloned.1.call-start = ((), (), s32[]{:S(2)}) async-start(), calls=%async_computation.15 | async-start | bytes 5898240 | tf_op jit(solution)/shard_map/all_gather | solution.py:105
  16.8 119.1 %copy-start.43 = (f32[1536]{0:T(1024)}, f32[1536]{0:T(1024)S(1)}, u32[]{:S(2)}) copy-start(f32[1536]{0:T(1024)S(1)} %reshape.423) | copy-start | bytes 18436
  22.2 70.4 %copy-start.36 = (f32[1536]{0:T(1024)}, f32[1536]{0:T(1024)S(1)}, u32[]{:S(2)}) copy-start(f32[1536]{0:T(1024)S(1)} %reshape.422) | copy-start | bytes 18436
  45.4 91.8 %copy-start.38 = (bf16[1536,16]{0,1:T(8,128)(2,1)}, bf16[1536,16]{0,1:T(8,128)(2,1)S(1)}, u32[]{:S(2)}) copy-start(bf16[1536,16]{0,1:T(8,128)(2,1)S(1)} %all_gather.27) | copy-start | bytes 147460
  47.7 49.6 %copy-start.32 = (f32[256,32]{0,1:T(8,128)}, f32[256,32]{0,1:T(8,128)S(1)}, u32[]{:S(2)}) copy-start(f32[256,32]{0,1:T(8,128)S(1)} %get-tuple-element.104) | copy-start | bytes 98308
  166.5 178.0 %all-to-all-start.2 = ((bf16[16,160,1536]{2,1,0:T(8,128)(2,1)}), bf16[16,160,1536]{2,1,0:T(8,128)(2,1)}, u32[]{:S(2)}, u32[]{:S(2)}) async-start(bf16[16,160,1536]{2,1,0:T(8,128)(2,1)} %bitcast.160), calls=%async_computation.2 | async-start | bytes 15728640 | tf_op jit(solution)/shard_map/all_to_all | solution.py:197
  344.5 176.8 %all-to-all-start = ((bf16[16,160,1536]{2,1,0:T(8,128)(2,1)}), bf16[16,160,1536]{2,1,0:T(8,128)(2,1)}, u32[]{:S(2)}, u32[]{:S(2)}) async-start(bf16[16,160,1536]{2,1,0:T(8,128)(2,1)} %bitcast.161), calls=%async_computation | async-start | bytes 15728640 | tf_op jit(solution)/shard_map/all_to_all | solution.py:179
  603.1 176.2 %all-to-all-start.1 = ((bf16[2,1280,1536]{2,0,1:T(2,128)(2,1)}), bf16[2,1280,1536]{2,0,1:T(2,128)(2,1)}, u32[]{:S(2)}, u32[]{:S(2)}) async-start(bf16[2,1280,1536]{2,0,1:T(2,128)(2,1)} %copy.121), calls=%async_computation.1 | async-start | bytes 15728640 | tf_op jit(solution)/shard_map/all_to_all | solution.py:188
  779.2 175.8 %all-to-all-start.3 = ((bf16[2,1280,1536]{2,0,1:T(2,128)(2,1)}), bf16[2,1280,1536]{2,0,1:T(2,128)(2,1)}, u32[]{:S(2)}, u32[]{:S(2)}) async-start(bf16[2,1280,1536]{2,0,1:T(2,128)(2,1)} %copy.125), calls=%async_computation.3 | async-start | bytes 15728640 | tf_op jit(solution)/shard_map/all_to_all | solution.py:221
  784.2 301.8 %reduce-scatter.15.cloned.1.call-start = ((), (), s32[]{:S(2)}) async-start(), calls=%async_computation.18 | async-start | bytes 1966080 | tf_op jit(solution)/shard_map/reduce_scatter | solution.py:300
  1026.5 59.5 %reduce-scatter.13.cloned.1.call-start = ((), (), s32[]{:S(2)}) async-start(), calls=%async_computation.17 | async-start | bytes 1966080 | tf_op jit(solution)/shard_map/reduce_scatter | solution.py:300
  1041.7 93.2 %reduce-scatter.17.cloned.1.call-start = ((), (), s32[]{:S(2)}) async-start(), calls=%async_computation.19 | async-start | bytes 5898240 | tf_op jit(solution)/shard_map/reduce_scatter | solution.py:300
  1045.3 140.1 %reduce-scatter.11.cloned.1.call-start = ((), (), s32[]{:S(2)}) async-start(), calls=%async_computation.16 | async-start | bytes 5898240 | tf_op jit(solution)/shard_map/reduce_scatter | solution.py:300
  1052.9 173.0 %reduce-scatter.23.cloned.1.call-start = ((), (), s32[]{:S(2)}) async-start(), calls=%async_computation.22 | async-start | bytes 3932160 | tf_op jit(solution)/shard_map/reduce_scatter | solution.py:333
  1063.1 203.4 %reduce-scatter.21.cloned.1.call-start = ((), (), s32[]{:S(2)}) async-start(), calls=%async_computation.21 | async-start | bytes 3932160 | tf_op jit(solution)/shard_map/reduce_scatter | solution.py:330
  1073.4 233.6 %reduce-scatter.19.cloned.1.call-start = ((), (), s32[]{:S(2)}) async-start(), calls=%async_computation.20 | async-start | bytes 3932160 | tf_op jit(solution)/shard_map/reduce_scatter | solution.py:327
  1083.7 101.8 %copy-start.66 = (u32[32]{0:T(128)S(1)}, u32[32]{0:T(128)}, u32[]{:S(2)}) copy-start(u32[32]{0:T(128)} %constant.150) | copy-start | bytes 388
  1083.7 247.2 %reduce-scatter.25.cloned.1.call-start = ((), (), s32[]{:S(2)}) async-start(), calls=%async_computation.23 | async-start | bytes 491520
  1086.0 380.1 %all-reduce.9.cloned.1.call-start = ((), (), s32[]{:S(2)}) async-start(), calls=%async_computation.24 | async-start | bytes 6291456 | tf_op jit(solution)/shard_map/psum | solution.py:318
  1186.7 122.8 %copy-start.17 = (bf16[256,24,64]{0,2,1:T(8,128)(2,1)S(1)}, bf16[256,24,64]{0,2,1:T(8,128)(2,1)}, u32[]{:S(2)}) copy-start(bf16[256,24,64]{0,2,1:T(8,128)(2,1)} %copy-done.16) | copy-start | bytes 2359300
  (65 other events, 616.2 us)
Sparse Core Ops, SparseCore 0:
  9.7 22.3 all-gather.6
  33.6 19.9 all-gather.8
  55.2 37.4 all-gather.10
  94.1 37.4 all-gather.12
  1026.6 26.4 reduce-scatter.14
  1056.2 28.1 reduce-scatter.12
  1087.0 47.8 reduce-scatter.16
  1137.5 47.8 reduce-scatter.10
  1188.0 37.9 reduce-scatter.22
  1228.5 37.9 reduce-scatter.20
  1269.0 37.9 reduce-scatter.18
  1310.1 20.7 reduce-scatter.24
  1335.3 130.7 all-reduce.8
where the time goes:
time: 1490 us; the launch traced here: 1480 us
  waiting for transfers between devices  936 us (63%)
  local copies, waits for them, and re-layouts  249 us (17%)
  matrix products  134 us (9%)
  blocking collectives  61.9 us (4%)
  other arithmetic  60.7 us (4%)
  starting transfers between devices  22.7 us (2%)
  between operations  15.9 us (1%)
    all_to_all x1, waiting for transfers between devices, body(): lax.all_to_all(outgoing, 'expert', split_axis=0, concat_axis=1, tiled=True)  164 us
    all_to_all x1, waiting for transfers between devices, body(): lax.all_to_all(slot_grads, 'expert', split_axis=0, concat_axis=1, tiled=T...  153 us
    all_to_all x1, waiting for transfers between devices, body(): lax.all_to_all(expert_out, 'expert', split_axis=1, concat_axis=0, tiled=T...  131 us
    all_to_all x1, waiting for transfers between devices, body(): lax.all_to_all(row_grad, 'expert', split_axis=1, concat_axis=0, tiled=True)  107 us
    reduce_scatter x4, waiting for transfers between devices, body(): lax.psum_scatter(shortened((query_partial, key_partial, value_partial, ou...  99.4 us
    psum x1, waiting for transfers between devices, body(): lax.psum(pieces[0].astype(jnp.bfloat16), 'expert').astype(jnp.float32)  93.4 us
    gather x1, local copies, waits for them, and re-layouts, body(): grad_returned[flat_routes, slot_rank].reshape(row_count, TOP, width)  46.5 us
    gather x1, local copies, waits for them, and re-layouts, body(): per_pair = returned[flat_routes, slot_rank].reshape(row_count, TOP, width)  46.3 us
  transfers between devices with their start and end apart: 17, of which 14 were waited for; matrix products, arithmetic and copies ran while one was open for 16% of the time, Pallas kernels for 0%

commit v1 on v0

--- a/solution.py
+++ b/solution.py
@@ -68,17 +68,9 @@
     return turned.reshape(values.shape[0], head_count * HD)
 
 
-def expert_slots(route_rows, expert_count, capacity):
-    flat_routes = route_rows.reshape(-1)
-    pair_count = flat_routes.shape[0]
-    matches = (flat_routes[:, None] == jnp.arange(expert_count, dtype=jnp.int32)[None, :]).astype(
-        jnp.int32
-    )
-    earlier = jnp.cumsum(matches, axis=0) - matches
-    slot_rank = jnp.sum(earlier * matches, axis=1)
-    slot_table = jnp.full((expert_count, capacity), pair_count, jnp.int32)
-    slot_table = slot_table.at[flat_routes, slot_rank].set(jnp.arange(pair_count, dtype=jnp.int32))
-    return (slot_table, slot_rank)
+def own_columns(values, local_count):
+    start = lax.axis_index("expert") * local_count
+    return lax.dynamic_slice_in_dim(values, start, local_count, axis=1)
 
 
 def body(
@@ -109,9 +101,7 @@
     )
     query_w, key_w, value_w, output_w, router_w, gain_one, gain_two = gathered
     row_count = tokens.shape[0]
-    width = tokens.shape[1]
     expert_count = w_router.shape[1]
-    capacity = 5 * row_count * TOP // (4 * expert_count)
     group_size = QH // KVH
     block_rows = min(512, row_count)
     block_total = row_count // block_rows
@@ -171,56 +161,56 @@
     route_hot = (routes[:, :, None] == expert_ids[None, None, :]).astype(jnp.float32)
     chosen = jnp.sum(route_hot * logits[:, None, :], axis=-1)
     gate_probs = jax.nn.softmax(chosen, axis=-1)
-    slot_table, slot_rank = expert_slots(routes, expert_count, capacity)
-    flat_routes = routes.reshape(-1)
-    zero_row = jnp.zeros((1, width), jnp.bfloat16)
-    padded = jnp.concatenate([hidden_two, zero_row], axis=0)
-    outgoing = padded[slot_table // TOP]
-    arrived = lax.all_to_all(outgoing, "expert", split_axis=0, concat_axis=1, tiled=True)
-    gate_pre = jnp.einsum("erd,edf->erf", arrived, expert_gate, preferred_element_type=jnp.float32)
-    up_pre = jnp.einsum("erd,edf->erf", arrived, expert_up, preferred_element_type=jnp.float32)
-    gate_sig = jax.nn.sigmoid(gate_pre)
-    gate_act = gate_pre * gate_sig
-    activation = (gate_act * up_pre).astype(jnp.bfloat16)
-    expert_out = jnp.einsum(
-        "erf,edf->erd", activation, expert_down, preferred_element_type=jnp.float32
-    ).astype(jnp.bfloat16)
-    returned = lax.all_to_all(expert_out, "expert", split_axis=1, concat_axis=0, tiled=True)
-    per_pair = returned[flat_routes, slot_rank].reshape(row_count, TOP, width)
-    mixture = jnp.sum(gate_probs[:, :, None] * per_pair, axis=1)
+    dense_probs = jnp.sum(route_hot * gate_probs[:, :, None], axis=1)
+    upstream = out_grad.astype(jnp.float32)
+    local_count = expert_gate.shape[0]
+    all_hidden = lax.all_gather(hidden_two, "expert", axis=0, tiled=True)
+    all_probs = own_columns(lax.all_gather(dense_probs, "expert", axis=0, tiled=True), local_count)
+    all_upstream = lax.all_gather(out_grad, "expert", axis=0, tiled=True)
+    mix_part = jnp.zeros(all_hidden.shape, jnp.float32)
+    row_part = jnp.zeros(all_hidden.shape, jnp.float32)
+    grad_columns, down_parts, gate_parts, up_parts = [], [], [], []
+    for e in range(local_count):
+        prob = all_probs[:, e : e + 1]
+        gate_pre = jnp.dot(all_hidden, expert_gate[e], preferred_element_type=jnp.float32)
+        up_pre = jnp.dot(all_hidden, expert_up[e], preferred_element_type=jnp.float32)
+        raw_grad = jnp.dot(all_upstream, expert_down[e], preferred_element_type=jnp.float32)
+        gate_sig = jax.nn.sigmoid(gate_pre)
+        gate_act = gate_pre * gate_sig
+        activation = gate_act * up_pre
+        grad_columns.append(jnp.sum(activation * raw_grad, axis=-1, keepdims=True))
+        weighted = (activation * prob).astype(jnp.bfloat16)
+        act_grad = raw_grad * prob
+        gate_pre_grad = (act_grad * up_pre * gate_sig * (1.0 + gate_pre * (1.0 - gate_sig))).astype(
+            jnp.bfloat16
+        )
+        up_pre_grad = (act_grad * gate_act).astype(jnp.bfloat16)
+        mix_part = mix_part + jnp.dot(
+            weighted, expert_down[e].T, preferred_element_type=jnp.float32
+        )
+        row_part = row_part + jnp.dot(
+            gate_pre_grad, expert_gate[e].T, preferred_element_type=jnp.float32
+        )
+        row_part = row_part + jnp.dot(
+            up_pre_grad, expert_up[e].T, preferred_element_type=jnp.float32
+        )
+        down_parts.append(jnp.dot(all_upstream.T, weighted, preferred_element_type=jnp.float32))
+        gate_parts.append(jnp.dot(all_hidden.T, gate_pre_grad, preferred_element_type=jnp.float32))
+        up_parts.append(jnp.dot(all_hidden.T, up_pre_grad, preferred_element_type=jnp.float32))
+    down_partial = jnp.stack(down_parts)
+    gate_partial = jnp.stack(gate_parts)
+    up_partial = jnp.stack(up_parts)
+    grad_dense = lax.all_to_all(
+        jnp.concatenate(grad_columns, axis=1), "expert", split_axis=0, concat_axis=1, tiled=True
+    )
+    gate_grad = jnp.sum(route_hot * grad_dense[:, None, :], axis=-1)
+    mixture = lax.psum_scatter(
+        mix_part.astype(jnp.bfloat16), "expert", scatter_dimension=0, tiled=True
+    ).astype(jnp.float32)
     layer_out = (residual + mixture).astype(jnp.bfloat16)
-    upstream = out_grad.astype(jnp.float32)
-    pair_grad = (gate_probs[:, :, None] * upstream[:, None, :]).astype(jnp.bfloat16)
-    gate_grad = jnp.sum(upstream[:, None, :] * per_pair, axis=-1)
-    flat_grad = jnp.concatenate([pair_grad.reshape(row_count * TOP, width), zero_row], axis=0)
-    slot_grads = flat_grad[slot_table]
-    grad_arrived = lax.all_to_all(slot_grads, "expert", split_axis=0, concat_axis=1, tiled=True)
-    act_grad = jnp.einsum(
-        "erd,edf->erf", grad_arrived, expert_down, preferred_element_type=jnp.float32
-    )
-    gate_pre_grad = (act_grad * up_pre * gate_sig * (1.0 + gate_pre * (1.0 - gate_sig))).astype(
-        jnp.bfloat16
-    )
-    up_pre_grad = (act_grad * gate_act).astype(jnp.bfloat16)
-    down_partial = jnp.einsum(
-        "erd,erf->edf", grad_arrived, activation, preferred_element_type=jnp.float32
-    )
-    gate_partial = jnp.einsum(
-        "erd,erf->edf", arrived, gate_pre_grad, preferred_element_type=jnp.float32
-    )
-    up_partial = jnp.einsum(
-        "erd,erf->edf", arrived, up_pre_grad, preferred_element_type=jnp.float32
-    )
-    row_grad = jnp.einsum(
-        "erf,edf->erd", gate_pre_grad, expert_gate, preferred_element_type=jnp.float32
-    )
-    row_grad = (
-        row_grad
-        + jnp.einsum("erf,edf->erd", up_pre_grad, expert_up, preferred_element_type=jnp.float32)
-    ).astype(jnp.bfloat16)
-    grad_returned = lax.all_to_all(row_grad, "expert", split_axis=1, concat_axis=0, tiled=True)
-    pair_rows = grad_returned[flat_routes, slot_rank].reshape(row_count, TOP, width)
-    hidden_two_grad = jnp.sum(pair_rows.astype(jnp.float32), axis=1)
+    hidden_two_grad = lax.psum_scatter(
+        row_part.astype(jnp.bfloat16), "expert", scatter_dimension=0, tiled=True
+    ).astype(jnp.float32)
     chosen_grad = gate_probs * (gate_grad - jnp.sum(gate_probs * gate_grad, axis=-1, keepdims=True))
     logit_grad = jnp.sum(route_hot * chosen_grad[:, :, None], axis=1).astype(jnp.bfloat16)
     hidden_two_grad = hidden_two_grad + jnp.dot(

time: 1490 us -> 1180 us (0.79)
  local copies, waits for them, and re-layouts: 249 us -> 33.3 us
  waiting for transfers between devices: 936 us -> 773 us
  matrix products: 134 us -> 200 us
  blocking collectives: 61.9 us -> 92.9 us
  starting transfers between devices: 22.7 us -> 5.51 us
    all_to_all x4 -> x1, waiting for transfers between devices: 554 us -> 6.17 us  [body(): lax.all_to_all(jnp.concatenate(grad_columns, axis=1), 'expert', split_axi...]
    all_gather x0 -> x2, waiting for transfers between devices: none -> 178 us  [the longest x1 93.1 us: body(): all_hidden = lax.all_gather(hidden_two, 'expert', axis=0, tiled=True)]
    reduce_scatter x1 -> x2, waiting for transfers between devices: 39.2 us -> 214 us  [the longest x1 117 us: body(): lax.psum_scatter(mix_part.astype(jnp.bfloat16), 'expert', scatter_dimensi...]
    gather x4 -> x0, local copies, waits for them, and re-layouts: 130 us -> none  [the longest x1 46.5 us: body(): grad_returned[flat_routes, slot_rank].reshape(row_count, TOP, width)]
    dot_general x9 -> x18, matrix products: 85.2 us -> 146 us  [the longest x2 24.4 us: body(): jnp.dot(up_pre_grad, expert_up[e].T, preferred_element_type=jnp.float32)]
    convert_element_type x2 -> x0, local copies, waits for them, and re-layouts: 59.3 us -> none  [the longest x1 43.7 us: body(): expert_out = jnp.einsum('erf,edf->erd', activation, expert_down, preferre...]
    unnamed x14 -> x19, waiting for transfers between devices: 7.75 us -> 65.4 us
    reduce_scatter x4, waiting for transfers between devices: 99.4 us -> 68.8 us  [body(): lax.psum_scatter(shortened((query_partial, key_partial, value_partial, ou...]
  transfers between devices with their start and end apart: 17 -> 18, of which waited for: 14 -> 16; matrix products, arithmetic and copies ran while one was open for 16% -> 14% of each run, Pallas kernels for 0% -> 0%
where the time goes in v1:
time: 1180 us; the launch traced here: 1170 us
  waiting for transfers between devices  773 us (66%)
  matrix products  200 us (17%)
  blocking collectives  92.9 us (8%)
  other arithmetic  47.1 us (4%)
  local copies, waits for them, and re-layouts  33.3 us (3%)
  between operations  15.8 us (1%)
    reduce_scatter x1, waiting for transfers between devices, body(): lax.psum_scatter(mix_part.astype(jnp.bfloat16), 'expert', scatter_dimensi...  117 us
    reduce_scatter x1, waiting for transfers between devices, body(): lax.psum_scatter(row_part.astype(jnp.bfloat16), 'expert', scatter_dimensi...  96.4 us
    all_gather x1, waiting for transfers between devices, body(): all_hidden = lax.all_gather(hidden_two, 'expert', axis=0, tiled=True)  93.1 us
    all_gather x1, waiting for transfers between devices, body(): all_upstream = lax.all_gather(out_grad, 'expert', axis=0, tiled=True)  85.3 us
    psum x1, waiting for transfers between devices, body(): lax.psum(pieces[0].astype(jnp.bfloat16), 'expert').astype(jnp.float32)  74.8 us
    reduce_scatter x4, waiting for transfers between devices, body(): lax.psum_scatter(shortened((query_partial, key_partial, value_partial, ou...  68.8 us
    unnamed x19, waiting for transfers between devices  65.4 us
    psum x1, blocking collectives, body(): lax.psum(pieces[4].astype(jnp.bfloat16), 'expert').astype(jnp.float32)  39.3 us
  transfers between devices with their start and end apart: 18, of which 16 were waited for; matrix products, arithmetic and copies ran while one was open for 14% of the time, Pallas kernels for 0%

profile of v1, /device:TPU:0, one launch (start us, length us, event | category | flops | bytes accessed | tf_op | source)
XLA Modules:
  0.0 1167.0 jit_solution(14045744881273360889)
XLA Ops:
  22.6 9.4 all-gather.9.cloned.1.call-done
  34.2 19.1 %all-gather.11.cloned.1.call-done = bf16[1536,512]{1,0:T(8,128)(2,1)} async-done(((bf16[384,512]{1,0:T(8,128)(2,1)}), bf16[1536,512]{1,0:T(8,128)(2,1)}) %all-gather.11.cloned.1.call-update) | async-done | bytes 1572880 | tf_op jit(solution)/shard_map/all_gather | solution.py:95
  55.6 36.7 %all-gather.13.cloned.1.call-done = bf16[1536,1536]{1,0:T(8,128)(2,1)} async-done(((bf16[384,1536]{1,0:T(8,128)(2,1)}), bf16[1536,1536]{1,0:T(8,128)(2,1)}) %all-gather.13.cloned.1.call-update) | async-done | bytes 4718608 | tf_op jit(solution)/shard_map/all_gather | solution.py:94
  102.1 29.1 %all-gather.15.cloned.1.call-done = bf16[1536,1536]{1,0:T(8,128)(2,1)} async-done(((bf16[384,1536]{1,0:T(8,128)(2,1)}), bf16[1536,1536]{1,0:T(8,128)(2,1)}) %all-gather.15.cloned.1.call-update) | async-done | bytes 4718608 | tf_op jit(solution)/shard_map/all_gather | solution.py:97
  142.2 93.1 %all-gather.17.cloned.1.call-done = bf16[2048,1536]{1,0:T(8,128)(2,1)} async-done(((bf16[256,1536]{1,0:T(8,128)(2,1)}), bf16[2048,1536]{1,0:T(8,128)(2,1)}) %all-gather.17.cloned.1.call-update) | async-done | bytes 6291472 | tf_op jit(solution)/shard_map/all_gather | solution.py:167
  235.4 8.8 fusion.44
  249.3 85.3 %all-gather.19.cloned.1.call-done = bf16[2048,1536]{1,0:T(8,128)(2,1)} async-done(((bf16[256,1536]{1,0:T(8,128)(2,1)}), bf16[2048,1536]{1,0:T(8,128)(2,1)}) %all-gather.19.cloned.1.call-update) | async-done | bytes 6291472 | tf_op jit(solution)/shard_map/all_gather | solution.py:169
  334.6 11.8 %multiply_reduce_fusion.1 = (f32[2048]{0:T(1024)S(1)}, f32[2048,512]{0,1:T(8,128)}) fusion(f32[2048,512]{0,1:T(8,128)} %fusion.44, f32[2048,512]{0,1:T(8,128)} %fusion.48, bf16[2048,1536]{1,0:T(8,128)(2,1)} %all-gather.19.cloned.1.call-done, bf16[2,1536,512]{2,1,0:T(8,128)(2,1)} %param.26), kind=kOutput, calls=%fused_computation.16 | convolution fusion | flops 3228563456 | bytes 20455424 | tf_op jit(solution)/shard_map/dot_general | solution.py:177
  360.0 8.5 multiply_reduce_fusion
  379.2 30.5 %all_gather.38 = f32[2048,16]{0,1:T(8,128)S(1)} all-gather(f32[256,16]{0,1:T(8,128)S(1)} %get-tuple-element.122), channel_id=1, replica_groups=mesh['dp'=4,'expert'=8] {'expert'}, dimensions={0}, use_global_device_ids=true | all-gather | bytes 147456 | tf_op jit(solution)/shard_map/all_gather | solution.py:168
  444.5 17.9 %add_convert_fusion = bf16[2048,1536]{1,0:T(8,128)(2,1)} fusion(f32[2048,1536]{1,0:T(8,128)} %fusion.34, f32[2048,1536]{1,0:T(8,128)} %fusion.46, f32[2048,1536]{1,0:T(8,128)} %fusion.42, bf16[2048,512]{0,1:T(8,128)(2,1)} %get-tuple-element.138, bf16[2,1536,512]{2,1,0:T(8,128)(2,1)} %param.25), kind=kOutput, calls=%fused_computation | convolution fusion | flops 3233808384 | bytes 47710208 | tf_op jit(solution)/shard_map/dot_general | solution.py:194
  462.7 10.2 fusion.40
  472.9 8.5 add_convert_fusion.1
  481.5 96.4 %reduce-scatter.17.cloned.1.call-done = bf16[256,1536]{1,0:T(8,128)(2,1)} async-done(((bf16[2048,1536]{1,0:T(8,128)(2,1)}), bf16[256,1536]{1,0:T(8,128)(2,1)}) %reduce-scatter.17.cloned.1.call-update) | async-done | bytes 786448 | tf_op jit(solution)/shard_map/reduce_scatter | solution.py:211
  581.4 117.2 %reduce-scatter.15.cloned.1.call-done = bf16[256,1536]{1,0:T(8,128)(2,1)} async-done(((bf16[2048,1536]{1,0:T(8,128)(2,1)}), bf16[256,1536]{1,0:T(8,128)(2,1)}) %reduce-scatter.15.cloned.1.call-update) | async-done | bytes 786448 | tf_op jit(solution)/shard_map/reduce_scatter | solution.py:207
  758.1 8.7 copy.92
  803.7 18.4 %reduce-scatter.25.cloned.1.call-done = bf16[384,1536]{1,0:T(8,128)(2,1)} async-done(((bf16[1536,1536]{1,0:T(8,128)(2,1)}), bf16[384,1536]{1,0:T(8,128)(2,1)}) %reduce-scatter.25.cloned.1.call-update) | async-done | bytes 1179664 | tf_op jit(solution)/shard_map/reduce_scatter | solution.py:290
  822.1 50.4 %reduce-scatter.19.cloned.1.call-done = bf16[384,1536]{1,0:T(8,128)(2,1)} async-done(((bf16[1536,1536]{1,0:T(8,128)(2,1)}), bf16[384,1536]{1,0:T(8,128)(2,1)}) %reduce-scatter.19.cloned.1.call-update) | async-done | bytes 1179664 | tf_op jit(solution)/shard_map/reduce_scatter | solution.py:290
  873.8 22.6 %reduce-scatter.31.cloned.1.call-done = bf16[384,16]{1,0:T(8,128)(2,1)} async-done(((bf16[1536,16]{1,0:T(8,128)(2,1)}), bf16[384,16]{1,0:T(8,128)(2,1)}) %reduce-scatter.31.cloned.1.call-update) | async-done | bytes 12304
  897.4 39.4 %reduce-scatter.33.cloned.1.call-done = bf16[384,1024]{1,0:T(8,128)(2,1)} async-done(((bf16[1536,1024]{1,0:T(8,128)(2,1)}), bf16[384,1024]{1,0:T(8,128)(2,1)}) %reduce-scatter.33.cloned.1.call-update) | async-done | bytes 786448
  943.8 33.6 %reduce-scatter.27.cloned.1.call-done = bf16[2,384,512]{2,1,0:T(8,128)(2,1)} async-done(((bf16[2,1536,512]{2,1,0:T(8,128)(2,1)}), bf16[2,384,512]{2,1,0:T(8,128)(2,1)}) %reduce-scatter.27.cloned.1.call-update) | async-done | bytes 786448 | tf_op jit(solution)/shard_map/reduce_scatter | solution.py:317
  979.8 37.9 %reduce-scatter.29.cloned.1.call-done = bf16[2,384,512]{2,1,0:T(8,128)(2,1)} async-done(((bf16[2,1536,512]{2,1,0:T(8,128)(2,1)}), bf16[2,384,512]{2,1,0:T(8,128)(2,1)}) %reduce-scatter.29.cloned.1.call-update) | async-done | bytes 786448 | tf_op jit(solution)/shard_map/reduce_scatter | solution.py:320
  1033.9 39.3 %all-reduce.2 = (bf16[384,16]{0,1:T(8,128)(2,1)S(1)}, bf16[384]{0:T(512)(128)(2,1)S(1)}, bf16[384]{0:T(512)(128)(2,1)S(1)}) all-reduce(bf16[384,16]{0,1:T(8,128)(2,1)S(1)} %copy.91, bf16[384]{0:T(512)(128)(2,1)S(1)} %dynamic-slice.1, bf16[384]{0:T(512)(128)(2,1)S(1)} %dynamic-slice.3), channel_id=1, replica_groups=mesh['dp'=4,'expert'=8] {'expert'}, use_global_device_ids=true, to_apply=%region_30.31 | all-reduce | flops 6912 | bytes 27648 | tf_op jit(solution)/shard_map/psum | solution.py:312
  1077.9 74.8 %all-reduce.7.cloned.1.call-done = (bf16[384,1536]{1,0:T(8,128)(2,1)}, bf16[384,512]{1,0:T(8,128)(2,1)}, bf16[384,512]{1,0:T(8,128)(2,1)}, bf16[384,1536]{1,0:T(8,128)(2,1)}) async-done(((bf16[384,1536]{1,0:T(8,128)(2,1)}, bf16[384,512]{1,0:T(8,128)(2,1)}, bf16[384,512]{1,0:T(8,128)(2,1)}, bf16[384,1536]{1,0:T(8,128)(2,1)}), (bf16[384,1536]{1,0:T(8,128)(2,1)}, bf16[384,512]{1,0:T(8,128)(2,1)}, ...) | async-done | bytes 3145744 | tf_op jit(solution)/shard_map/psum | solution.py:308
  (265 shorter events, 243.5 us)
Async XLA Ops:
  7.2 24.8 %all-gather.9.cloned.1.call-start = ((), (), s32[]{:S(2)}) async-start(), calls=%async_computation.11 | async-start | bytes 1966080 | tf_op jit(solution)/shard_map/all_gather | solution.py:96
  8.0 45.3 %all-gather.11.cloned.1.call-start = ((), (), s32[]{:S(2)}) async-start(), calls=%async_computation.12 | async-start | bytes 1966080 | tf_op jit(solution)/shard_map/all_gather | solution.py:95
  8.7 83.6 %all-gather.13.cloned.1.call-start = ((), (), s32[]{:S(2)}) async-start(), calls=%async_computation.13 | async-start | bytes 5898240 | tf_op jit(solution)/shard_map/all_gather | solution.py:94
  9.4 121.8 %all-gather.15.cloned.1.call-start = ((), (), s32[]{:S(2)}) async-start(), calls=%async_computation.14 | async-start | bytes 5898240 | tf_op jit(solution)/shard_map/all_gather | solution.py:97
  10.0 225.4 %all-gather.17.cloned.1.call-start = ((), (), s32[]{:S(2)}) async-start(), calls=%async_computation.15 | async-start | bytes 7077888 | tf_op jit(solution)/shard_map/all_gather | solution.py:167
  21.7 70.6 %copy-start.41 = (f32[1536]{0:T(1024)}, f32[1536]{0:T(1024)S(1)}, u32[]{:S(2)}) copy-start(f32[1536]{0:T(1024)S(1)} %reshape.292) | copy-start | bytes 18436
  22.3 70.1 %copy-start.43 = (f32[256]{0:T(256)}, f32[256]{0:T(256)S(1)}, u32[]{:S(2)}) copy-start(f32[256]{0:T(256)S(1)} %add_rsqrt_fusion.1) | copy-start | bytes 3076
  22.5 74.2 %copy-start.34 = (f32[256,32]{0,1:T(8,128)}, f32[256,32]{0,1:T(8,128)S(1)}, u32[]{:S(2)}) copy-start(f32[256,32]{0,1:T(8,128)S(1)} %get-tuple-element.156) | copy-start | bytes 98308
  22.5 74.2 %copy-start.37 = (f32[256,32]{0,1:T(8,128)}, f32[256,32]{0,1:T(8,128)S(1)}, u32[]{:S(2)}) copy-start(f32[256,32]{0,1:T(8,128)S(1)} %get-tuple-element.157) | copy-start | bytes 98308
  136.2 198.5 %all-gather.19.cloned.1.call-start = ((), (), s32[]{:S(2)}) async-start(), calls=%async_computation.17 | async-start | bytes 7077888 | tf_op jit(solution)/shard_map/all_gather | solution.py:169
  369.1 9.9 all-to-all-start
  372.5 205.4 %reduce-scatter.17.cloned.1.call-start = ((), (), s32[]{:S(2)}) async-start(), calls=%async_computation.18 | async-start | bytes 7077888 | tf_op jit(solution)/shard_map/reduce_scatter | solution.py:211
  462.5 236.1 %reduce-scatter.15.cloned.1.call-start = ((), (), s32[]{:S(2)}) async-start(), calls=%async_computation.16 | async-start | bytes 7077888 | tf_op jit(solution)/shard_map/reduce_scatter | solution.py:207
  481.4 322.2 %reduce-scatter.23.cloned.1.call-start = ((), (), s32[]{:S(2)}) async-start(), calls=%async_computation.21 | async-start | bytes 1966080 | tf_op jit(solution)/shard_map/reduce_scatter | solution.py:290
  712.8 90.9 %reduce-scatter.21.cloned.1.call-start = ((), (), s32[]{:S(2)}) async-start(), calls=%async_computation.20 | async-start | bytes 1966080 | tf_op jit(solution)/shard_map/reduce_scatter | solution.py:290
  727.6 94.5 %reduce-scatter.25.cloned.1.call-start = ((), (), s32[]{:S(2)}) async-start(), calls=%async_computation.22 | async-start | bytes 5898240 | tf_op jit(solution)/shard_map/reduce_scatter | solution.py:290
  732.4 140.1 %reduce-scatter.19.cloned.1.call-start = ((), (), s32[]{:S(2)}) async-start(), calls=%async_computation.19 | async-start | bytes 5898240 | tf_op jit(solution)/shard_map/reduce_scatter | solution.py:290
  741.0 155.5 %reduce-scatter.31.cloned.1.call-start = ((), (), s32[]{:S(2)}) async-start(), calls=%async_computation.25 | async-start | bytes 491520
  742.2 194.6 %reduce-scatter.33.cloned.1.call-start = ((), (), s32[]{:S(2)}) async-start(), calls=%async_computation.26 | async-start | bytes 3932160
  771.2 206.2 %reduce-scatter.27.cloned.1.call-start = ((), (), s32[]{:S(2)}) async-start(), calls=%async_computation.23 | async-start | bytes 3932160 | tf_op jit(solution)/shard_map/reduce_scatter | solution.py:317
  787.9 229.8 %reduce-scatter.29.cloned.1.call-start = ((), (), s32[]{:S(2)}) async-start(), calls=%async_computation.24 | async-start | bytes 3932160 | tf_op jit(solution)/shard_map/reduce_scatter | solution.py:320
  803.4 69.2 %copy-start.58 = (u32[32]{0:T(128)S(1)}, u32[32]{0:T(128)}, u32[]{:S(2)}) copy-start(u32[32]{0:T(128)} %constant.89) | copy-start | bytes 388
  803.4 349.4 %all-reduce.7.cloned.1.call-start = ((), (), s32[]{:S(2)}) async-start(), calls=%async_computation.27 | async-start | bytes 6291456 | tf_op jit(solution)/shard_map/psum | solution.py:308
  941.2 79.0 %copy-start.16 = (bf16[256,24,64]{0,2,1:T(8,128)(2,1)S(1)}, bf16[256,24,64]{0,2,1:T(8,128)(2,1)}, u32[]{:S(2)}) copy-start(bf16[256,24,64]{0,2,1:T(8,128)(2,1)} %copy-done.15) | copy-start | bytes 2359300
  (55 other events, 473.5 us)
Sparse Core Ops, SparseCore 0:
  9.6 22.3 all-gather.8
  33.6 19.6 all-gather.10
  54.8 37.4 all-gather.12
  93.7 37.4 all-gather.14
  136.3 99.0 all-gather.16
  237.4 97.1 all-gather.18
  462.6 115.2 reduce-scatter.16
  581.5 117.0 reduce-scatter.14
  713.0 27.3 reduce-scatter.22
  743.4 28.1 reduce-scatter.20
  774.2 47.8 reduce-scatter.24
  824.6 47.8 reduce-scatter.18
  875.6 20.7 reduce-scatter.30
  898.8 37.9 reduce-scatter.32
  939.3 37.9 reduce-scatter.26
  979.7 37.9 reduce-scatter.28
  1021.9 130.8 all-reduce.6

commit v2 on v1

--- a/solution.py
+++ b/solution.py
@@ -1,8 +1,13 @@
+import functools
+
 import jax
 import jax.numpy as jnp
 from jax import lax
+from jax.experimental import pallas as pl
+from jax.experimental.pallas import tpu as pltpu
 from jax.sharding import PartitionSpec as P
 
+MESH = pl.DeviceIdType.MESH
 QH = 24
 KVH = 8
 HD = 64
@@ -71,6 +76,508 @@
 def own_columns(values, local_count):
     start = lax.axis_index("expert") * local_count
     return lax.dynamic_slice_in_dim(values, start, local_count, axis=1)
+
+
+NT = (((1,), (1,)), ((), ()))
+TN = (((0,), (0,)), ((), ()))
+
+
+def dot_f32(left, right, dims=(((1,), (0,)), ((), ()))):
+    return lax.dot_general(left, right, dims, preferred_element_type=jnp.float32)
+
+
+def packed(rows, index, step, base=8):
+    value = 0
+    for place, row in enumerate(rows):
+        number = sum(digit * base**power for power, digit in enumerate(row))
+        value = value + jnp.where(index == place, number, 0)
+    scale = 1
+    for power in range(1, len(rows[0])):
+        scale = jnp.where(step == power, base**power, scale)
+    return (value // scale) % base
+
+
+BLOCK_ORDER = (
+    (0, 4, 1, 5, 2, 6, 3, 7),
+    (1, 5, 0, 2, 4, 3, 6, 7),
+    (2, 6, 3, 1, 7, 0, 5, 4),
+    (3, 7, 2, 6, 1, 5, 0, 4),
+)
+TAKE_FIRST = (
+    (7, 1, 7, 2, 7, 3, 7, 7),
+    (7, 0, 7, 7, 3, 7, 7, 7),
+    (7, 3, 7, 7, 0, 7, 7, 7),
+    (7, 2, 7, 1, 7, 0, 7, 7),
+)
+TAKE_SECOND = (
+    (7, 7, 7, 7, 7, 7, 7, 7),
+    (7, 2, 7, 7, 7, 7, 7, 7),
+    (7, 1, 7, 7, 7, 7, 7, 7),
+    (7, 7, 7, 7, 7, 7, 7, 7),
+)
+SUM_ORDER = ((3, 2, 1, 0), (3, 2, 0, 1), (0, 1, 3, 2), (0, 1, 2, 3))
+
+
+def moe_kernel(
+    h_in, u_in, p_in, wg_in, wu_in, wd_in,
+    d_out, e_out, gg_out, grads_out, core_got, y_got,
+    h_all, u_all, p_all, wg, wu, wd, act, gu, ex, ez, rx, rz, d_stage, gg_stage, tile_bf, tile_f32, got_tile, got_y,
+    load_sem, h_up, h_down, h_across, h_recv, p_send, p_recv, g_send, g_recv,
+    x_send, x_recv, z_send, z_recv, d_sem, c_send, c_recv, y_send, y_recv, tile_sem, out_sem,
+    *, comm
+):
+    A, B, n = 4, 2, 8
+    R, D = h_in.shape
+    F = wg.shape[2]
+    shard = D // 4
+    me = lax.axis_index("expert")
+    dp = lax.axis_index("dp")
+    a, b = me // B, me % B
+    y, c = dp // 2, dp % 2
+    partner_x = a * B + (1 - b)
+    core_peer = 2 * y + (1 - c)
+    y_peer = 2 * (1 - y) + c
+
+    def copy(src, dst, send, recv, **target):
+        return pltpu.make_async_remote_copy(
+            src_ref=src, dst_ref=dst, send_sem=send, recv_sem=recv, device_id=target, device_id_type=MESH
+        )
+
+    loads = [
+        pltpu.make_async_copy(h_in, h_all.at[me], load_sem.at[0]),
+        pltpu.make_async_copy(u_in, u_all, load_sem.at[1]),
+        pltpu.make_async_copy(wg_in, wg, load_sem.at[2]),
+        pltpu.make_async_copy(wu_in, wu, load_sem.at[3]),
+        pltpu.make_async_copy(wd_in, wd, load_sem.at[4]),
+        pltpu.make_async_copy(p_in.at[me], p_all.at[me], load_sem.at[5]),
+    ]
+    for load in loads:
+        load.start()
+
+    barrier = pltpu.get_barrier_semaphore()
+    for k in range(1, n):
+        pl.semaphore_signal(barrier, inc=1, device_id={"expert": (me + k) % n}, device_id_type=MESH)
+    pl.semaphore_signal(barrier, inc=1, device_id={"dp": core_peer}, device_id_type=MESH)
+    pl.semaphore_signal(barrier, inc=1, device_id={"dp": y_peer}, device_id_type=MESH)
+    pl.semaphore_wait(barrier, n + 1)
+    loads[0].wait()
+    loads[5].wait()
+
+    def send_up(s):
+        return copy(h_all.at[s], h_all.at[s], h_up.at[s], h_recv.at[s], expert=me + B)
+
+    def send_down(s):
+        return copy(h_all.at[s], h_all.at[s], h_down.at[s], h_recv.at[s], expert=me - B)
+
+    def send_across(s):
+        return copy(h_all.at[s], h_all.at[s], h_across.at[s], h_recv.at[s], expert=partner_x)
+
+    def p_copy(peer):
+        return copy(p_in.at[peer], p_all.at[me], p_send.at[peer], p_recv.at[me], expert=peer)
+
+    @pl.when(a < A - 1)
+    def _():
+        send_up(me).start()
+
+    @pl.when(a > 0)
+    def _():
+        send_down(me).start()
+
+    send_across(me).start()
+    for k in range(1, n):
+        p_copy((me + k) % n).start()
+    for k in range(1, n):
+        s = (me + k) % n
+        copy(p_in.at[s], p_all.at[s], p_send.at[s], p_recv.at[s], expert=s).wait_recv()
+    for load in loads[1:5]:
+        load.wait()
+
+    def recv_block(s):
+        send_across(s).wait_recv()
+
+    def take(row):
+        @pl.when(row < A)
+        def _():
+            s = row * B + b
+            recv_block(s)
+            send_across(s).start()
+
+            @pl.when((row < a) & (a < A - 1))
+            def _():
+                send_up(s).start()
+
+            @pl.when((row > a) & (a > 0))
+            def _():
+                send_down(s).start()
+
+    def d_copy(s, slot):
+        return pltpu.make_async_copy(d_stage.at[slot], d_out.at[s], d_sem.at[slot])
+
+    def g_copy(s):
+        return copy(gg_stage.at[s], gg_out.at[me], g_send.at[s], g_recv.at[me], expert=s)
+
+    def compute(step, s, row, across):
+        rows = pl.ds(pl.multiple_of(s * R, R), R)
+        probs = jnp.transpose(p_all[s])
+        grad_cols = []
+        for e in range(2):
+            gate_pre = dot_f32(h_all[s], wg[e])
+            up_pre = dot_f32(h_all[s], wu[e])
+            raw = dot_f32(u_all[s], wd[e])
+            prob = probs[:, e : e + 1]
+            sig = 1.0 / (1.0 + jnp.exp(-gate_pre))
+            gate_act = gate_pre * sig
+            activation = gate_act * up_pre
+            grad_cols.append(jnp.sum(activation * raw, axis=1, keepdims=True))
+            act[rows, e * F : (e + 1) * F] = (activation * prob).astype(jnp.bfloat16)
+            act_grad = raw * prob
+            gate_grad = act_grad * up_pre * sig * (1.0 + gate_pre * (1.0 - sig))
+            gu[rows, 2 * e * F : (2 * e + 1) * F] = gate_grad.astype(jnp.bfloat16)
+            gu[rows, (2 * e + 1) * F : (2 * e + 2) * F] = (act_grad * gate_act).astype(jnp.bfloat16)
+        column = lax.broadcasted_iota(jnp.int32, (R, 128), 1)
+        both = jnp.where(column == 0, grad_cols[0], jnp.where(column == 1, grad_cols[1], 0.0))
+        gg_stage[s] = jnp.transpose(both)[:8]
+        slot = step % 2
+
+        @pl.when(step >= 2)
+        def _():
+            d_copy(s, slot).wait()
+
+        def columns(tile, _):
+            cols = pl.ds(pl.multiple_of(tile * 512, 512), 512)
+            mixed = dot_f32(act[rows, 0:F], wd[0, cols, :], NT) + dot_f32(act[rows, F : 2 * F], wd[1, cols, :], NT)
+            d_stage[slot, :, cols] = mixed.astype(jnp.bfloat16)
+            back = dot_f32(gu[rows, 0:F], wg[0, cols, :], NT)
+            back += dot_f32(gu[rows, F : 2 * F], wu[0, cols, :], NT)
+            back += dot_f32(gu[rows, 2 * F : 3 * F], wg[1, cols, :], NT)
+            back += dot_f32(gu[rows, 3 * F : 4 * F], wu[1, cols, :], NT)
+
+            @pl.when(across)
+            def _():
+                ex[row, :, cols] = back.astype(jnp.bfloat16)
+
+            @pl.when(jnp.logical_not(across))
+            def _():
+                ez[row, :, cols] = back.astype(jnp.bfloat16)
+
+            return 0
+
+        lax.fori_loop(0, D // 512, columns, 0)
+        d_copy(s, slot).start()
+
+        @pl.when(s != me)
+        def _():
+            g_copy(s).start()
+
+        @pl.when(s == me)
+        def _():
+            pltpu.make_async_copy(gg_stage.at[s], gg_out.at[me], g_send.at[s]).start()
+
+    def block_step(step, _):
+        take(packed(TAKE_FIRST, a, step))
+        take(packed(TAKE_SECOND, a, step))
+        code = packed(BLOCK_ORDER, a, step)
+        across = code >= A
+        row = code % A
+        s = row * B + jnp.where(across, 1 - b, b)
+
+        @pl.when(across)
+        def _():
+            recv_block(s)
+
+        compute(step, s, row, across)
+        return 0
+
+    lax.fori_loop(0, n, block_step, 0)
+
+    def x_copy(row):
+        return copy(ex.at[row], rx.at[row], x_send.at[row], x_recv.at[row], expert=partner_x)
+
+    def z_up(row):
+        return copy(ez.at[row], rz.at[row + 1], z_send.at[row], z_recv.at[row + 1], expert=me + B)
+
+    def z_down(row):
+        return copy(ez.at[row], rz.at[row], z_send.at[row], z_recv.at[row], expert=me - B)
+
+    for place in range(A):
+        x_copy(packed(SUM_ORDER, a, place)).start()
+
+    def core_copy(slot, which, index):
+        return copy(tile_bf.at[slot], core_got.at[which, index], c_send.at[slot], c_recv.at[which, index], dp=core_peer)
+
+    def y_copy(slot, index):
+        return copy(tile_bf.at[slot], y_got.at[index], y_send.at[slot], y_recv.at[index], dp=y_peer)
+
+    def weight_tile(group, e, kind, left, right):
+        owner = jnp.where(group == 0, core_peer, jnp.where(group == 1, 2 * (1 - y) + 1 - c, jnp.where(group == 2, y_peer, dp)))
+        cols = pl.ds(pl.multiple_of(owner * shard, 128), shard)
+        total = dot_f32(left[:, :, cols].reshape(n * R, shard), right, TN)
+        index = kind * 2 + e
+        slot = kind
+
+        @pl.when(group < 2)
+        def _():
+            @pl.when((group > 0) | (e > 0))
+            def _():
+                core_copy(slot, 0, index).wait_send()
+
+            tile_bf[slot] = total.astype(jnp.bfloat16)
+            core_copy(slot, group, index).start()
+
+        @pl.when(group == 2)
+        def _():
+            @pl.when(e == 0)
+            def _():
+                core_copy(slot, 0, index).wait_send()
+
+            @pl.when(e > 0)
+            def _():
+                y_copy(slot, index).wait_send()
+
+            core_copy(slot, 1, index).wait_recv()
+            got = pltpu.make_async_copy(core_got.at[1, index], got_tile, tile_sem)
+            got.start()
+            got.wait()
+            tile_bf[slot] = (total + got_tile[...].astype(jnp.float32)).astype(jnp.bfloat16)
+            y_copy(slot, index).start()
+
+        @pl.when(group == 3)
+        def _():
+            core_copy(slot, 0, index).wait_recv()
+            got = pltpu.make_async_copy(core_got.at[0, index], got_tile, tile_sem)
+            got.start()
+            got.wait()
+            tile_f32[index] = total + got_tile[...].astype(jnp.float32)
+
+    def sum_step(place, _):
+        def pair(e, _):
+            weight_tile(place, e, 0, h_all, gu[:, pl.ds(pl.multiple_of(2 * e * F, 128), F)])
+            weight_tile(place, e, 1, h_all, gu[:, pl.ds(pl.multiple_of((2 * e + 1) * F, 128), F)])
+            weight_tile(place, e, 2, u_all, act[:, pl.ds(pl.multiple_of(e * F, 128), F)])
+            return 0
+
+        lax.fori_loop(0, 2, pair, 0)
+        row = packed(SUM_ORDER, a, place)
+        x_copy(row).wait_recv()
+        below = (a > 0) & (row >= a)
+        above = (a < A - 1) & (row <= a)
+
+        @pl.when(below)
+        def _():
+            z_up(row).wait_recv()
+
+        @pl.when(above)
+        def _():
+            z_down(row).wait_recv()
+
+        def chunk(index, _):
+            part = pl.ds(pl.multiple_of(index * 64, 64), 64)
+            total = ez[row, part, :].astype(jnp.float32) + rx[row, part, :].astype(jnp.float32)
+
+            @pl.when(row != a)
+            def _():
+                @pl.when(below)
+                def _():
+                    ez[row, part, :] = (total + rz[row + 1, part, :].astype(jnp.float32)).astype(jnp.bfloat16)
+
+                @pl.when(above)
+                def _():
+                    ez[row, part, :] = (total + rz[row, part, :].astype(jnp.float32)).astype(jnp.bfloat16)
+
+                @pl.when(jnp.logical_not(below | above))
+                def _():
+                    ez[row, part, :] = total.astype(jnp.bfloat16)
+
+            @pl.when(row == a)
+            def _():
+                @pl.when(below & above)
+                def _():
+                    e_out[part, :] = total + rz[row + 1, part, :].astype(jnp.float32) + rz[row, part, :].astype(jnp.float32)
+
+                @pl.when(below & jnp.logical_not(above))
+                def _():
+                    e_out[part, :] = total + rz[row + 1, part, :].astype(jnp.float32)
+
+                @pl.when(above & jnp.logical_not(below))
+                def _():
+                    e_out[part, :] = total + rz[row, part, :].astype(jnp.float32)
+
+            return 0
+
+        lax.fori_loop(0, R // 64, chunk, 0)
+
+        @pl.when(row > a)
+        def _():
+            z_up(row).start()
+
+        @pl.when(row < a)
+        def _():
+            z_down(row).start()
+
+        return 0
+
+    lax.fori_loop(0, A, sum_step, 0)
+
+    def finish(index, _):
+        y_copy(0, index).wait_recv()
+        got = pltpu.make_async_copy(y_got.at[index], got_y, tile_sem)
+        got.start()
+        got.wait()
+        tile_f32[index] = tile_f32[index] + got_y[...].astype(jnp.float32)
+        out = pltpu.make_async_copy(tile_f32.at[index], grads_out.at[index], out_sem.at[index])
+        out.start()
+        return 0
+
+    lax.fori_loop(0, 6, finish, 0)
+
+    for kind in range(3):
+        y_copy(kind, 0).wait_send()
+    for row in range(A):
+        x_copy(row).wait_send()
+
+        @pl.when(row != a)
+        def _():
+            z_up(row).wait_send()
+
+    @pl.when(a < A - 1)
+    def _():
+        send_up(me).wait_send()
+
+    @pl.when(a > 0)
+    def _():
+        send_down(me).wait_send()
+
+    for row in range(A):
+        s = row * B + b
+        send_across(s).wait_send()
+
+        @pl.when((row < a) & (a < A - 1))
+        def _():
+            send_up(s).wait_send()
+
+        @pl.when((row > a) & (a > 0))
+        def _():
+            send_down(s).wait_send()
+
+    for k in range(1, n):
+        s = (me + k) % n
+        p_copy(s).wait_send()
+        g_copy(s).wait_send()
+        copy(gg_stage.at[s], gg_out.at[s], g_send.at[s], g_recv.at[s], expert=s).wait_recv()
+    pltpu.make_async_copy(gg_stage.at[me], gg_out.at[me], g_send.at[me]).wait()
+    for slot in range(2):
+        d_copy(0, slot).wait()
+    for index in range(6):
+        pltpu.make_async_copy(tile_f32.at[index], grads_out.at[index], out_sem.at[index]).wait()
+
+
+def moe_call(hidden, all_upstream, probs, expert_gate, expert_up, expert_down):
+    R, D = hidden.shape
+    F = expert_gate.shape[2]
+    A, n = 4, 8
+    shard = D // 4
+    bf, f32 = jnp.bfloat16, jnp.float32
+    any_spec = pl.BlockSpec(memory_space=pl.ANY)
+    vmem = pl.BlockSpec(memory_space=pltpu.VMEM)
+    dma = pltpu.SemaphoreType.DMA
+    out_shape = (
+        jax.ShapeDtypeStruct((n, R, D), bf),
+        jax.ShapeDtypeStruct((R, D), f32),
+        jax.ShapeDtypeStruct((n, 8, R), f32),
+        jax.ShapeDtypeStruct((6, shard, F), f32),
+        jax.ShapeDtypeStruct((2, 6, shard, F), bf),
+        jax.ShapeDtypeStruct((6, shard, F), bf),
+    )
+    return pl.pallas_call(
+        functools.partial(moe_kernel, comm=True),
+        out_shape=out_shape,
+        in_specs=[any_spec] * 6,
+        out_specs=(any_spec, vmem, any_spec, any_spec, any_spec, any_spec),
+        scratch_shapes=[
+            pltpu.VMEM((n, R, D), bf),
+            pltpu.VMEM((n, R, D), bf),
+            pltpu.VMEM((n, 8, R), f32),
+            pltpu.VMEM((2, D, F), bf),
+            pltpu.VMEM((2, D, F), bf),
+            pltpu.VMEM((2, D, F), bf),
+            pltpu.VMEM((n * R, 2 * F), bf),
+            pltpu.VMEM((n * R, 4 * F), bf),
+            pltpu.VMEM((A, R, D), bf),
+            pltpu.VMEM((A, R, D), bf),
+            pltpu.VMEM((A, R, D), bf),
+            pltpu.VMEM((A + 1, R, D), bf),
+            pltpu.VMEM((2, R, D), bf),
+            pltpu.VMEM((n, 8, R), f32),
+            pltpu.VMEM((3, shard, F), bf),
+            pltpu.VMEM((6, shard, F), f32),
+            pltpu.VMEM((shard, F), bf),
+            pltpu.VMEM((shard, F), bf),
+            dma((6,)), dma((n,)), dma((n,)), dma((n,)), dma((n,)), dma((n,)), dma((n,)), dma((n,)), dma((n,)),
+            dma((A,)), dma((A,)), dma((A,)), dma((A + 1,)), dma((2,)),
+            dma((3,)), dma((2, 6)), dma((3,)), dma((6,)), dma, dma((6,)),
+        ],
+        compiler_params=pltpu.CompilerParams(
+            collective_id=1, has_side_effects=True, vmem_limit_bytes=64 * 1024 * 1024 - 65536
+        ),
+        cost_estimate=pl.CostEstimate(flops=58 * 10**9, bytes_accessed=60 * 10**6, transcendentals=2 * 10**6),
+        name="experts",
+    )(hidden, all_upstream, probs, expert_gate, expert_up, expert_down)
+
+
+def moe_by_collectives(hidden_two, all_upstream, dense_probs, expert_gate, expert_up, expert_down):
+    local_count = expert_gate.shape[0]
+    all_hidden = lax.all_gather(hidden_two, "expert", axis=0, tiled=True)
+    all_probs = own_columns(lax.all_gather(dense_probs, "expert", axis=0, tiled=True), local_count)
+    mix_part = jnp.zeros(all_hidden.shape, jnp.float32)
+    row_part = jnp.zeros(all_hidden.shape, jnp.float32)
+    grad_columns, down_parts, gate_parts, up_parts = [], [], [], []
+    for e in range(local_count):
+        prob = all_probs[:, e : e + 1]
+        gate_pre = jnp.dot(all_hidden, expert_gate[e], preferred_element_type=jnp.float32)
+        up_pre = jnp.dot(all_hidden, expert_up[e], preferred_element_type=jnp.float32)
+        raw_grad = jnp.dot(all_upstream, expert_down[e], preferred_element_type=jnp.float32)
+        gate_sig = jax.nn.sigmoid(gate_pre)
+        gate_act = gate_pre * gate_sig
+        activation = gate_act * up_pre
+        grad_columns.append(jnp.sum(activation * raw_grad, axis=-1, keepdims=True))
+        weighted = (activation * prob).astype(jnp.bfloat16)
+        act_grad = raw_grad * prob
+        gate_pre_grad = (act_grad * up_pre * gate_sig * (1.0 + gate_pre * (1.0 - gate_sig))).astype(
+            jnp.bfloat16
+        )
+        up_pre_grad = (act_grad * gate_act).astype(jnp.bfloat16)
+        mix_part = mix_part + jnp.dot(
+            weighted, expert_down[e].T, preferred_element_type=jnp.float32
+        )
+        row_part = row_part + jnp.dot(
+            gate_pre_grad, expert_gate[e].T, preferred_element_type=jnp.float32
+        )
+        row_part = row_part + jnp.dot(
+            up_pre_grad, expert_up[e].T, preferred_element_type=jnp.float32
+        )
+        down_parts.append(jnp.dot(all_upstream.T, weighted, preferred_element_type=jnp.float32))
+        gate_parts.append(jnp.dot(all_hidden.T, gate_pre_grad, preferred_element_type=jnp.float32))
+        up_parts.append(jnp.dot(all_hidden.T, up_pre_grad, preferred_element_type=jnp.float32))
+    down_partial = jnp.stack(down_parts)
+    gate_partial = jnp.stack(gate_parts)
+    up_partial = jnp.stack(up_parts)
+    grad_dense = lax.all_to_all(
+        jnp.concatenate(grad_columns, axis=1), "expert", split_axis=0, concat_axis=1, tiled=True
+    )
+    hidden_two_grad = lax.psum_scatter(
+        row_part.astype(jnp.bfloat16), "expert", scatter_dimension=0, tiled=True
+    ).astype(jnp.float32)
+    expert_totals = tuple(
+        lax.psum_scatter(part.astype(jnp.bfloat16), "dp", scatter_dimension=1, tiled=True).astype(
+            jnp.float32
+        )
+        for part in (gate_partial, up_partial, down_partial)
+    )
+    return (mix_part.astype(jnp.bfloat16), hidden_two_grad, grad_dense, expert_totals)
+
+
+def fits_fused(dp_size, group, row_count):
+    return dp_size == 4 and group == 8 and row_count == 256
 
 
 def body(
@@ -164,53 +671,31 @@
     dense_probs = jnp.sum(route_hot * gate_probs[:, :, None], axis=1)
     upstream = out_grad.astype(jnp.float32)
     local_count = expert_gate.shape[0]
-    all_hidden = lax.all_gather(hidden_two, "expert", axis=0, tiled=True)
-    all_probs = own_columns(lax.all_gather(dense_probs, "expert", axis=0, tiled=True), local_count)
+    group = lax.axis_size("expert")
     all_upstream = lax.all_gather(out_grad, "expert", axis=0, tiled=True)
-    mix_part = jnp.zeros(all_hidden.shape, jnp.float32)
-    row_part = jnp.zeros(all_hidden.shape, jnp.float32)
-    grad_columns, down_parts, gate_parts, up_parts = [], [], [], []
-    for e in range(local_count):
-        prob = all_probs[:, e : e + 1]
-        gate_pre = jnp.dot(all_hidden, expert_gate[e], preferred_element_type=jnp.float32)
-        up_pre = jnp.dot(all_hidden, expert_up[e], preferred_element_type=jnp.float32)
-        raw_grad = jnp.dot(all_upstream, expert_down[e], preferred_element_type=jnp.float32)
-        gate_sig = jax.nn.sigmoid(gate_pre)
-        gate_act = gate_pre * gate_sig
-        activation = gate_act * up_pre
-        grad_columns.append(jnp.sum(activation * raw_grad, axis=-1, keepdims=True))
-        weighted = (activation * prob).astype(jnp.bfloat16)
-        act_grad = raw_grad * prob
-        gate_pre_grad = (act_grad * up_pre * gate_sig * (1.0 + gate_pre * (1.0 - gate_sig))).astype(
-            jnp.bfloat16
-        )
-        up_pre_grad = (act_grad * gate_act).astype(jnp.bfloat16)
-        mix_part = mix_part + jnp.dot(
-            weighted, expert_down[e].T, preferred_element_type=jnp.float32
-        )
-        row_part = row_part + jnp.dot(
-            gate_pre_grad, expert_gate[e].T, preferred_element_type=jnp.float32
-        )
-        row_part = row_part + jnp.dot(
-            up_pre_grad, expert_up[e].T, preferred_element_type=jnp.float32
-        )
-        down_parts.append(jnp.dot(all_upstream.T, weighted, preferred_element_type=jnp.float32))
-        gate_parts.append(jnp.dot(all_hidden.T, gate_pre_grad, preferred_element_type=jnp.float32))
-        up_parts.append(jnp.dot(all_hidden.T, up_pre_grad, preferred_element_type=jnp.float32))
-    down_partial = jnp.stack(down_parts)
-    gate_partial = jnp.stack(gate_parts)
-    up_partial = jnp.stack(up_parts)
-    grad_dense = lax.all_to_all(
-        jnp.concatenate(grad_columns, axis=1), "expert", split_axis=0, concat_axis=1, tiled=True
-    )
+    if fits_fused(lax.axis_size("dp"), group, row_count):
+        by_owner = jnp.pad(
+            dense_probs.T.reshape(group, local_count, row_count), ((0, 0), (0, 8 - local_count), (0, 0))
+        )
+        mix_part, row_sum, grad_rows, expert_grads, _, _ = moe_call(
+            hidden_two,
+            all_upstream.reshape(group, row_count, -1),
+            by_owner,
+            expert_gate,
+            expert_up,
+            expert_down,
+        )
+        mix_part = mix_part.reshape(all_upstream.shape)
+        hidden_two_grad = row_sum
+        grad_dense = grad_rows[:, :local_count].reshape(expert_count, row_count).T
+        expert_totals = tuple(expert_grads[2 * kind : 2 * kind + 2] for kind in range(3))
+    else:
+        mix_part, hidden_two_grad, grad_dense, expert_totals = moe_by_collectives(
+            hidden_two, all_upstream, dense_probs, expert_gate, expert_up, expert_down
+        )
     gate_grad = jnp.sum(route_hot * grad_dense[:, None, :], axis=-1)
-    mixture = lax.psum_scatter(
-        mix_part.astype(jnp.bfloat16), "expert", scatter_dimension=0, tiled=True
-    ).astype(jnp.float32)
-    layer_out = (residual + mixture).astype(jnp.bfloat16)
-    hidden_two_grad = lax.psum_scatter(
-        row_part.astype(jnp.bfloat16), "expert", scatter_dimension=0, tiled=True
-    ).astype(jnp.float32)
+    mixture = lax.psum_scatter(mix_part, "expert", scatter_dimension=0, tiled=True)
+    layer_out = (residual + mixture.astype(jnp.float32)).astype(jnp.bfloat16)
     chosen_grad = gate_probs * (gate_grad - jnp.sum(gate_probs * gate_grad, axis=-1, keepdims=True))
     logit_grad = jnp.sum(route_hot * chosen_grad[:, :, None], axis=1).astype(jnp.bfloat16)
     hidden_two_grad = hidden_two_grad + jnp.dot(
@@ -313,17 +798,6 @@
         lax.psum(pieces[5].astype(jnp.bfloat16), "expert").astype(jnp.float32),
         lax.psum(pieces[6].astype(jnp.bfloat16), "expert").astype(jnp.float32),
     )
-    expert_totals = (
-        lax.psum_scatter(
-            gate_partial.astype(jnp.bfloat16), "dp", scatter_dimension=1, tiled=True
-        ).astype(jnp.float32),
-        lax.psum_scatter(
-            up_partial.astype(jnp.bfloat16), "dp", scatter_dimension=1, tiled=True
-        ).astype(jnp.float32),
-        lax.psum_scatter(
-            down_partial.astype(jnp.bfloat16), "dp", scatter_dimension=1, tiled=True
-        ).astype(jnp.float32),
-    )
     return (
         layer_out,
         in_grad,

time: 1180 us -> 894 us (0.76)
  waiting for transfers between devices: 773 us -> 527 us
  Pallas kernels: 0 us -> 193 us
  matrix products: 200 us -> 50.1 us
  blocking collectives: 92.9 us -> 62.1 us
  other arithmetic: 47.1 us -> 23.4 us
  local copies, waits for them, and re-layouts: 33.3 us -> 20 us
    pallas_call x0 -> x1, Pallas kernels: none -> 193 us  [moe_call(): pl.pallas_call(functools.partial(moe_kernel, comm=True), out_shape=out_sh...]
    reduce_scatter x4 -> x1, waiting for transfers between devices: 285 us -> 117 us  [body(): lax.psum_scatter(mix_part, 'expert', scatter_dimension=0, tiled=True)]
    dot_general x18 -> x0, matrix products: 146 us -> none  [the longest x2 24.4 us: body(): jnp.dot(up_pre_grad, expert_up[e].T, preferred_element_type=jnp.float32)]
    all_gather x1 -> x0, waiting for transfers between devices: 93.1 us -> none  [body(): all_hidden = lax.all_gather(hidden_two, 'expert', axis=0, tiled=True)]
    reduce_scatter x4, waiting for transfers between devices: 68.8 us -> 132 us  [body(): lax.psum_scatter(shortened((query_partial, key_partial, value_partial, ou...]
    unnamed x19 -> x13, waiting for transfers between devices: 65.4 us -> 20.5 us
    all_gather x1 -> x0, blocking collectives: 30.5 us -> none  [body(): lax.all_gather(dense_probs, 'expert', axis=0, tiled=True)]
    unnamed x134 -> x121, local copies, waits for them, and re-layouts: 32.2 us -> 13.1 us
  transfers between devices with their start and end apart: 18 -> 12, of which waited for: 16 -> 11; matrix products, arithmetic and copies ran while one was open for 14% -> 7% of each run, Pallas kernels for 0% -> 0%
where the time goes in v2:
time: 894 us; the launch traced here: 893 us
  waiting for transfers between devices  527 us (59%)
  Pallas kernels  193 us (22%)
  blocking collectives  62.1 us (7%)
  matrix products  50.1 us (6%)
  other arithmetic  23.4 us (3%)
  local copies, waits for them, and re-layouts  20 us (2%)
  between operations  15.8 us (2%)
    pallas_call x1, Pallas kernels, moe_call(): pl.pallas_call(functools.partial(moe_kernel, comm=True), out_shape=out_sh...  193 us
    reduce_scatter x4, waiting for transfers between devices, body(): lax.psum_scatter(shortened((query_partial, key_partial, value_partial, ou...  132 us
    reduce_scatter x1, waiting for transfers between devices, body(): lax.psum_scatter(mix_part, 'expert', scatter_dimension=0, tiled=True)  117 us
    all_gather x1, waiting for transfers between devices, body(): all_upstream = lax.all_gather(out_grad, 'expert', axis=0, tiled=True)  93.3 us
    psum x1, waiting for transfers between devices, body(): lax.psum(pieces[0].astype(jnp.bfloat16), 'expert').astype(jnp.float32)  76.2 us
    psum x1, blocking collectives, body(): lax.psum(pieces[4].astype(jnp.bfloat16), 'expert').astype(jnp.float32)  39 us
    all_gather x1, waiting for transfers between devices, body(): lax.all_gather(shards[0], 'dp', axis=0, tiled=True)  36.7 us
    all_gather x1, waiting for transfers between devices, body(): lax.all_gather(shards[3], 'dp', axis=0, tiled=True)  29.1 us
  transfers between devices with their start and end apart: 12, of which 11 were waited for; matrix products, arithmetic and copies ran while one was open for 7% of the time, Pallas kernels for 0%

profile of v2, /device:TPU:0, one launch (start us, length us, event | category | flops | bytes accessed | tf_op | source)
XLA Modules:
  0.0 892.6 jit_solution(76613384111537401)
XLA Ops:
  10.7 6.1 all-gather.1
  16.9 5.4 all-gather
  22.5 5.5 all_gather.31
  34.4 19.1 %all-gather.10.cloned.1.call-done = bf16[1536,512]{1,0:T(8,128)(2,1)} async-done(((bf16[384,512]{1,0:T(8,128)(2,1)}), bf16[1536,512]{1,0:T(8,128)(2,1)}) %all-gather.10.cloned.1.call-update) | async-done | bytes 1572880 | tf_op jit(solution)/shard_map/all_gather | solution.py:602
  55.8 36.7 %all-gather.12.cloned.1.call-done = bf16[1536,1536]{1,0:T(8,128)(2,1)} async-done(((bf16[384,1536]{1,0:T(8,128)(2,1)}), bf16[1536,1536]{1,0:T(8,128)(2,1)}) %all-gather.12.cloned.1.call-update) | async-done | bytes 4718608 | tf_op jit(solution)/shard_map/all_gather | solution.py:601
  92.6 4.3 fusion.41
  102.4 29.1 %all-gather.14.cloned.1.call-done = bf16[1536,1536]{1,0:T(8,128)(2,1)} async-done(((bf16[384,1536]{1,0:T(8,128)(2,1)}), bf16[1536,1536]{1,0:T(8,128)(2,1)}) %all-gather.14.cloned.1.call-update) | async-done | bytes 4718608 | tf_op jit(solution)/shard_map/all_gather | solution.py:604
  131.5 3.8 multiply_reduce_fusion.2
  139.2 93.3 %all-gather.16.cloned.1.call-done = bf16[2048,1536]{1,0:T(8,128)(2,1)} async-done(((bf16[256,1536]{1,0:T(8,128)(2,1)}), bf16[2048,1536]{1,0:T(8,128)(2,1)}) %all-gather.16.cloned.1.call-update) | async-done | bytes 6291472 | tf_op jit(solution)/shard_map/all_gather | solution.py:675
  232.6 193.2 %experts.1 = (bf16[8,256,1536]{2,1,0:T(8,128)(2,1)}, f32[256,1536]{1,0:T(8,128)}, f32[8,8,256]{2,1,0:T(8,128)}, f32[6,384,512]{2,1,0:T(8,128)}, bf16[2,6,384,512...) custom-call(bf16[256,1536]{1,0:T(8,128)(2,1)} %copy-done.8, bf16[8,256,1536]{2,1,0:T(8,128)(2,1)} %bitcast.115, ...), custom_call_target="tpu_custom_call" | custom-call | flops 57999998976 | bytes 60000000 | tf_op jit(solution)/shard_map/experts/pallas_call | solution.py:491
  429.7 117.1 %reduce-scatter.9.cloned.1.call-done = bf16[256,1536]{1,0:T(8,128)(2,1)} async-done(((bf16[2048,1536]{1,0:T(8,128)(2,1)}), bf16[256,1536]{1,0:T(8,128)(2,1)}) %reduce-scatter.9.cloned.1.call-update) | async-done | bytes 786448 | tf_op jit(solution)/shard_map/reduce_scatter | solution.py:697
  550.0 3.7 convolution_convert_fusion.4
  554.0 3.9 fusion.26
  560.2 4.2 fusion
  564.4 4.8 fusion.2
  588.1 30.8 %reduce-scatter.13.cloned.1.call-done = bf16[384,512]{1,0:T(8,128)(2,1)} async-done(((bf16[1536,512]{1,0:T(8,128)(2,1)}), bf16[384,512]{1,0:T(8,128)(2,1)}) %reduce-scatter.13.cloned.1.call-update) | async-done | bytes 393232 | tf_op jit(solution)/shard_map/reduce_scatter | solution.py:775
  618.9 50.4 %reduce-scatter.17.cloned.1.call-done = bf16[384,1536]{1,0:T(8,128)(2,1)} async-done(((bf16[1536,1536]{1,0:T(8,128)(2,1)}), bf16[384,1536]{1,0:T(8,128)(2,1)}) %reduce-scatter.17.cloned.1.call-update) | async-done | bytes 1179664 | tf_op jit(solution)/shard_map/reduce_scatter | solution.py:775
  669.3 50.4 %reduce-scatter.11.cloned.1.call-done = bf16[384,1536]{1,0:T(8,128)(2,1)} async-done(((bf16[1536,1536]{1,0:T(8,128)(2,1)}), bf16[384,1536]{1,0:T(8,128)(2,1)}) %reduce-scatter.11.cloned.1.call-update) | async-done | bytes 1179664 | tf_op jit(solution)/shard_map/reduce_scatter | solution.py:775
  721.6 4.7 fusion.46
  726.3 17.3 %reduce-scatter.19.cloned.1.call-done = bf16[384,16]{1,0:T(8,128)(2,1)} async-done(((bf16[1536,16]{1,0:T(8,128)(2,1)}), bf16[384,16]{1,0:T(8,128)(2,1)}) %reduce-scatter.19.cloned.1.call-update) | async-done | bytes 12304
  744.7 3.9 fusion.49
  752.1 6.1 all-reduce.5
  758.4 39.0 %all-reduce.3 = (bf16[384,16]{0,1:T(8,128)(2,1)S(1)}, bf16[384]{0:T(512)(128)(2,1)S(1)}, bf16[384]{0:T(512)(128)(2,1)S(1)}) all-reduce(bf16[384,16]{0,1:T(8,128)(2,1)S(1)} %copy.85, bf16[384]{0:T(512)(128)(2,1)S(1)} %dynamic-slice.1, bf16[384]{0:T(512)(128)(2,1)S(1)} %dynamic-slice.3), channel_id=1, replica_groups=mesh['dp'=4,'expert'=8] {'expert'}, use_global_device_ids=true, to_apply=%region_27.28 | all-reduce | flops 6912 | bytes 27648 | tf_op jit(solution)/shard_map/psum | solution.py:797
  802.1 76.2 %all-reduce.8.cloned.1.call-done = (bf16[384,1536]{1,0:T(8,128)(2,1)}, bf16[384,512]{1,0:T(8,128)(2,1)}, bf16[384,512]{1,0:T(8,128)(2,1)}, bf16[384,1536]{1,0:T(8,128)(2,1)}) async-done(((bf16[384,1536]{1,0:T(8,128)(2,1)}, bf16[384,512]{1,0:T(8,128)(2,1)}, bf16[384,512]{1,0:T(8,128)(2,1)}, bf16[384,1536]{1,0:T(8,128)(2,1)}), (bf16[384,1536]{1,0:T(8,128)(2,1)}, bf16[384,512]{1,0:T(8,128)(2,1)}, ...) | async-done | bytes 3145744 | tf_op jit(solution)/shard_map/psum | solution.py:793
  (211 shorter events, 67.4 us)
Async XLA Ops:
  7.2 25.1 %all-gather.8.cloned.1.call-start = ((), (), s32[]{:S(2)}) async-start(), calls=%async_computation.6 | async-start | bytes 1966080 | tf_op jit(solution)/shard_map/all_gather | solution.py:603
  7.9 45.6 %all-gather.10.cloned.1.call-start = ((), (), s32[]{:S(2)}) async-start(), calls=%async_computation.7 | async-start | bytes 1966080 | tf_op jit(solution)/shard_map/all_gather | solution.py:602
  8.7 19.4 %copy-start.1 = (bf16[256,1536]{1,0:T(8,128)(2,1)S(1)}, bf16[256,1536]{1,0:T(8,128)(2,1)}, u32[]{:S(2)}) copy-start(bf16[256,1536]{1,0:T(8,128)(2,1)} %param.14) | copy-start | bytes 2359300
  8.7 83.8 %all-gather.12.cloned.1.call-start = ((), (), s32[]{:S(2)}) async-start(), calls=%async_computation.8 | async-start | bytes 5898240 | tf_op jit(solution)/shard_map/all_gather | solution.py:601
  9.4 122.0 %all-gather.14.cloned.1.call-start = ((), (), s32[]{:S(2)}) async-start(), calls=%async_computation.9 | async-start | bytes 5898240 | tf_op jit(solution)/shard_map/all_gather | solution.py:604
  10.0 222.5 %all-gather.16.cloned.1.call-start = ((), (), s32[]{:S(2)}) async-start(), calls=%async_computation.10 | async-start | bytes 7077888 | tf_op jit(solution)/shard_map/all_gather | solution.py:675
  10.6 536.1 %reduce-scatter.9.cloned.1.call-start = ((), (), s32[]{:S(2)}) async-start(), calls=%async_computation.11 | async-start | bytes 7077888 | tf_op jit(solution)/shard_map/reduce_scatter | solution.py:697
  16.9 118.5 %copy-start.38 = (f32[1536]{0:T(1024)}, f32[1536]{0:T(1024)S(1)}, u32[]{:S(2)}) copy-start(f32[1536]{0:T(1024)S(1)} %reshape.301) | copy-start | bytes 18436
  22.3 70.2 %copy-start.30 = (f32[1536]{0:T(1024)}, f32[1536]{0:T(1024)S(1)}, u32[]{:S(2)}) copy-start(f32[1536]{0:T(1024)S(1)} %reshape.300) | copy-start | bytes 18436
  28.0 108.2 %copy-start.32 = (bf16[1536,16]{0,1:T(8,128)(2,1)}, bf16[1536,16]{0,1:T(8,128)(2,1)S(1)}, u32[]{:S(2)}) copy-start(bf16[1536,16]{0,1:T(8,128)(2,1)S(1)} %all_gather.31) | copy-start | bytes 147460
  28.3 64.2 %copy-start.44 = (f32[256]{0:T(256)}, f32[256]{0:T(256)S(1)}, u32[]{:S(2)}) copy-start(f32[256]{0:T(256)S(1)} %add_rsqrt_fusion.1) | copy-start | bytes 3076
  28.6 68.4 %copy-start.26 = (f32[256,32]{0,1:T(8,128)}, f32[256,32]{0,1:T(8,128)S(1)}, u32[]{:S(2)}) copy-start(f32[256,32]{0,1:T(8,128)S(1)} %get-tuple-element.105) | copy-start | bytes 98308
  28.6 68.4 %copy-start.28 = (f32[256,32]{0,1:T(8,128)}, f32[256,32]{0,1:T(8,128)S(1)}, u32[]{:S(2)}) copy-start(f32[256,32]{0,1:T(8,128)S(1)} %get-tuple-element.106) | copy-start | bytes 98308
  34.4 65.1 %copy-start.25 = (bf16[256,512]{0,1:T(8,128)(2,1)}, bf16[256,512]{0,1:T(8,128)(2,1)S(1)}, u32[]{:S(2)}) copy-start(bf16[256,512]{0,1:T(8,128)(2,1)S(1)} %copy.66) | copy-start | bytes 786436
  55.8 41.5 %copy-start.19 = (bf16[256,8,32]{0,2,1:T(8,128)(2,1)}, bf16[256,8,32]{0,2,1:T(8,128)(2,1)S(1)}, u32[]{:S(2)}) copy-start(bf16[256,8,32]{0,2,1:T(8,128)(2,1)S(1)} %get-tuple-element.103) | copy-start | bytes 393220
  55.8 41.5 %copy-start.21 = (bf16[256,8,32]{0,2,1:T(8,128)(2,1)}, bf16[256,8,32]{0,2,1:T(8,128)(2,1)S(1)}, u32[]{:S(2)}) copy-start(bf16[256,8,32]{0,2,1:T(8,128)(2,1)S(1)} %get-tuple-element.104) | copy-start | bytes 393220
  102.4 32.9 %copy-start.6 = (bf16[8,64,3,256]{3,1,2,0:T(8,128)(2,1)}, bf16[8,64,3,256]{3,1,2,0:T(8,128)(2,1)S(1)}, u32[]{:S(2)}) copy-start(bf16[8,64,3,256]{3,1,2,0:T(8,128)(2,1)S(1)} %fusion.20) | copy-start | bytes 2359300
  425.9 162.1 %reduce-scatter.15.cloned.1.call-start = ((), (), s32[]{:S(2)}) async-start(), calls=%async_computation.14 | async-start | bytes 1966080 | tf_op jit(solution)/shard_map/reduce_scatter | solution.py:775
  559.9 59.0 %reduce-scatter.13.cloned.1.call-start = ((), (), s32[]{:S(2)}) async-start(), calls=%async_computation.13 | async-start | bytes 1966080 | tf_op jit(solution)/shard_map/reduce_scatter | solution.py:775
  573.6 95.7 %reduce-scatter.17.cloned.1.call-start = ((), (), s32[]{:S(2)}) async-start(), calls=%async_computation.15 | async-start | bytes 5898240 | tf_op jit(solution)/shard_map/reduce_scatter | solution.py:775
  577.3 142.5 %reduce-scatter.11.cloned.1.call-start = ((), (), s32[]{:S(2)}) async-start(), calls=%async_computation.12 | async-start | bytes 5898240 | tf_op jit(solution)/shard_map/reduce_scatter | solution.py:775
  585.7 157.9 %reduce-scatter.19.cloned.1.call-start = ((), (), s32[]{:S(2)}) async-start(), calls=%async_computation.16 | async-start | bytes 491520
  588.0 290.3 %all-reduce.8.cloned.1.call-start = ((), (), s32[]{:S(2)}) async-start(), calls=%async_computation.17 | async-start | bytes 6291456 | tf_op jit(solution)/shard_map/psum | solution.py:793
  721.6 23.0 %copy-start.13 = (bf16[256,24,64]{0,2,1:T(8,128)(2,1)S(1)}, bf16[256,24,64]{0,2,1:T(8,128)(2,1)}, u32[]{:S(2)}) copy-start(bf16[256,24,64]{0,2,1:T(8,128)(2,1)} %copy-done.12) | copy-start | bytes 2359300
  (45 other events, 109.6 us)
Sparse Core Ops, SparseCore 0:
  9.6 22.6 all-gather.7
  33.8 19.6 all-gather.9
  55.1 37.4 all-gather.11
  94.0 37.4 all-gather.13
  133.5 99.0 all-gather.15
  426.1 120.6 reduce-scatter.8
  560.0 27.3 reduce-scatter.14
  590.6 28.1 reduce-scatter.12
  621.4 47.8 reduce-scatter.16
  671.8 47.8 reduce-scatter.10
  722.8 20.8 reduce-scatter.18
  747.4 130.8 all-reduce.7

commit v3 on v2

--- a/solution.py
+++ b/solution.py
@@ -524,6 +524,361 @@
     )(hidden, all_upstream, probs, expert_gate, expert_up, expert_down)
 
 
+def reduce_kernel(
+    left, right, extra, out,
+    core_out, core_in, y_out, y_in, half, x_out, x_in, own, z_out, z_in, full,
+    core_send, core_recv, y_send, y_recv, x_send, x_recv, zs_send, zs_recv, zg_send, zg_recv, xg_send, xg_recv,
+):
+    A, B = 4, 2
+    W = core_out.shape[3]
+    shard = core_out.shape[2]
+    half_rows, piece = shard // B, shard // (A * B)
+    chunks = y_in.shape[0]
+    me = lax.axis_index("expert")
+    dp = lax.axis_index("dp")
+    a, b = me // B, me % B
+    y, c = dp // 2, dp % 2
+    partner_x = a * B + (1 - b)
+    core_peer = 2 * y + (1 - c)
+    y_peer = 2 * (1 - y) + c
+
+    def copy(src, dst, send, recv, **target):
+        return pltpu.make_async_remote_copy(
+            src_ref=src, dst_ref=dst, send_sem=send, recv_sem=recv, device_id=target, device_id_type=MESH
+        )
+
+    barrier = pltpu.get_barrier_semaphore()
+    for target in [{"dp": core_peer}, {"dp": y_peer}, {"expert": partner_x}] + [
+        {"expert": (a + k) % A * B + b} for k in range(1, A)
+    ]:
+        pl.semaphore_signal(barrier, inc=1, device_id=target, device_id_type=MESH)
+    pl.semaphore_wait(barrier, 2 + A)
+
+    def partial(chunk, owner):
+        rows = pl.ds(pl.multiple_of(owner * shard, 128), shard)
+        cols = pl.ds(pl.multiple_of(chunk * W, 128), W)
+        which = jnp.where(chunk < 4, 0, 1)
+        total = dot_f32(left[which, :, rows], right[:, cols], TN)
+        share = extra[pl.ds(pl.multiple_of(owner * shard, 128), shard), :].astype(jnp.float32)
+        share = jnp.where(chunk == chunks - 1, share, 0.0)
+        return jnp.concatenate([total[:, : W - 128], total[:, W - 128 :] + share], axis=1)
+
+    def core_copy(chunk, which):
+        slot = chunk % 2
+        return copy(core_out.at[slot, which], core_in.at[chunk, which], core_send.at[slot, which], core_recv.at[chunk, which], dp=core_peer)
+
+    def y_copy(chunk):
+        slot = chunk % 2
+        return copy(y_out.at[slot], y_in.at[chunk], y_send.at[slot], y_recv.at[chunk], dp=y_peer)
+
+    def x_copy(chunk):
+        slot = chunk % 2
+        return copy(x_out.at[slot], x_in.at[chunk], x_send.at[slot], x_recv.at[chunk], expert=partner_x)
+
+    def z_scatter(chunk, to, source):
+        slot = chunk % 2
+        return copy(
+            z_out.at[slot, pl.ds(pl.multiple_of(to * piece, 16), piece)], z_in.at[chunk, source],
+            zs_send.at[slot, to], zs_recv.at[chunk, source], expert=to * B + b,
+        )
+
+    def z_gather(chunk, to, source):
+        rows = pl.ds(pl.multiple_of(b * half_rows + source * piece, 16), piece)
+        return copy(full.at[chunk, rows], full.at[chunk, rows], zg_send.at[chunk, to], zg_recv.at[chunk, source], expert=to * B + b)
+
+    def x_gather(chunk, side):
+        rows = pl.ds(pl.multiple_of(side * half_rows, 16), half_rows)
+        return copy(full.at[chunk, rows], full.at[chunk, rows], xg_send.at[chunk], xg_recv.at[chunk], expert=partner_x)
+
+    def to_core(chunk):
+        for which, owner in ((0, core_peer), (1, 2 * (1 - y) + 1 - c)):
+            value = partial(chunk, owner).astype(jnp.bfloat16)
+
+            @pl.when(chunk >= 2)
+            def _():
+                core_copy(chunk, which).wait_send()
+
+            core_out[chunk % 2, which] = value
+            core_copy(chunk, which).start()
+
+    def to_y(chunk):
+        value = partial(chunk, y_peer)
+        core_copy(chunk, 1).wait_recv()
+
+        @pl.when(chunk >= 2)
+        def _():
+            y_copy(chunk).wait_send()
+
+        y_out[chunk % 2] = (value + core_in[chunk, 1].astype(jnp.float32)).astype(jnp.bfloat16)
+        y_copy(chunk).start()
+
+    def to_x(chunk):
+        value = partial(chunk, dp)
+        core_copy(chunk, 0).wait_recv()
+        y_copy(chunk).wait_recv()
+        value = value + core_in[chunk, 0].astype(jnp.float32) + y_in[chunk].astype(jnp.float32)
+
+        @pl.when(chunk >= 2)
+        def _():
+            x_copy(chunk).wait_send()
+
+        low, high = value[:half_rows], value[half_rows:]
+        half[chunk % 2] = jnp.where(b == 0, low, high)
+        x_out[chunk % 2] = jnp.where(b == 0, high, low).astype(jnp.bfloat16)
+        x_copy(chunk).start()
+
+    def to_z(chunk):
+        x_copy(chunk).wait_recv()
+
+        @pl.when(chunk >= 2)
+        def _():
+            for k in range(1, A):
+                z_scatter(chunk, (a + k) % A, a).wait_send()
+
+        total = half[chunk % 2] + x_in[chunk].astype(jnp.float32)
+        half[chunk % 2] = total
+        own[chunk % 2] = half[chunk % 2, pl.ds(pl.multiple_of(a * piece, 8), piece)]
+        z_out[chunk % 2] = total.astype(jnp.bfloat16)
+        for k in range(1, A):
+            z_scatter(chunk, (a + k) % A, a).start()
+
+    def spread_z(chunk):
+        total = own[chunk % 2]
+        for k in range(1, A):
+            source = (a + k) % A
+            z_scatter(chunk, a, source).wait_recv()
+            total = total + z_in[chunk, source].astype(jnp.float32)
+        rows = pl.ds(pl.multiple_of(b * half_rows + a * piece, 16), piece)
+        full[chunk, rows] = total.astype(jnp.bfloat16)
+        for k in range(1, A):
+            z_gather(chunk, (a + k) % A, a).start()
+
+    def spread_x(chunk):
+        for k in range(1, A):
+            z_gather(chunk, a, (a + k) % A).wait_recv()
+        x_gather(chunk, b).start()
+
+    def finish(chunk):
+        x_gather(chunk, 1 - b).wait_recv()
+        cols = pl.ds(pl.multiple_of(chunk * W, 128), W)
+        out[:, cols] = full[chunk].astype(jnp.float32)
+
+    stages = (to_core, to_y, to_x, to_z, spread_z, spread_x, finish)
+
+    def step(t, _):
+        for delay, stage in enumerate(stages):
+            @pl.when((t >= delay) & (t < delay + chunks))
+            def _():
+                stage(t - delay)
+
+        return 0
+
+    lax.fori_loop(0, chunks + len(stages) - 1, step, 0)
+
+    for chunk in range(chunks - 2, chunks):
+        core_copy(chunk, 0).wait_send()
+        core_copy(chunk, 1).wait_send()
+        y_copy(chunk).wait_send()
+        x_copy(chunk).wait_send()
+        for k in range(1, A):
+            z_scatter(chunk, (a + k) % A, a).wait_send()
+
+    def drain(chunk, _):
+        for k in range(1, A):
+            z_gather(chunk, (a + k) % A, a).wait_send()
+        x_gather(chunk, b).wait_send()
+        return 0
+
+    lax.fori_loop(0, chunks, drain, 0)
+
+
+def reduce_call(left, right, extra):
+    D = left.shape[2]
+    width = right.shape[1]
+    W, A, B = 384, 4, 2
+    shard, chunks = D // 4, width // W
+    bf, f32 = jnp.bfloat16, jnp.float32
+    vmem = pl.BlockSpec(memory_space=pltpu.VMEM)
+    dma = pltpu.SemaphoreType.DMA
+    piece = shard // (A * B)
+    return pl.pallas_call(
+        reduce_kernel,
+        out_shape=jax.ShapeDtypeStruct((shard, width), f32),
+        in_specs=[vmem] * 3,
+        out_specs=vmem,
+        scratch_shapes=[
+            pltpu.VMEM((2, 2, shard, W), bf),
+            pltpu.VMEM((chunks, 2, shard, W), bf),
+            pltpu.VMEM((2, shard, W), bf),
+            pltpu.VMEM((chunks, shard, W), bf),
+            pltpu.VMEM((2, shard // B, W), f32),
+            pltpu.VMEM((2, shard // B, W), bf),
+            pltpu.VMEM((chunks, shard // B, W), bf),
+            pltpu.VMEM((2, piece, W), f32),
+            pltpu.VMEM((2, shard // B, W), bf),
+            pltpu.VMEM((chunks, A, piece, W), bf),
+            pltpu.VMEM((chunks, shard, W), bf),
+            dma((2, 2)), dma((chunks, 2)), dma((2,)), dma((chunks,)), dma((2,)), dma((chunks,)),
+            dma((2, A)), dma((chunks, A)), dma((chunks, A)), dma((chunks, A)), dma((chunks,)), dma((chunks,)),
+        ],
+        compiler_params=pltpu.CompilerParams(
+            collective_id=2, has_side_effects=True, vmem_limit_bytes=56 * 1024 * 1024
+        ),
+        cost_estimate=pl.CostEstimate(flops=4 * 10**9, bytes_accessed=20 * 10**6, transcendentals=0),
+        name="weight_sums",
+    )(left, right, extra)
+
+
+def front_kernel(
+    w_q, w_k, w_v, w_o, w_small, u_in,
+    all_q, all_k, all_v, all_o, all_small, u_all,
+    local_sem, core_send, y_send, pass_send, w_recv, u_up, u_down, u_across, u_recv,
+):
+    A, B = 4, 2
+    me = lax.axis_index("expert")
+    dp = lax.axis_index("dp")
+    a, b = me // B, me % B
+    y, c = dp // 2, dp % 2
+    partner_x = a * B + (1 - b)
+    core_peer = 2 * y + (1 - c)
+    y_peer = 2 * (1 - y) + c
+    far_peer = 2 * (1 - y) + 1 - c
+    shards = (w_small, w_q, w_k, w_v, w_o)
+    gathered = (all_small, all_q, all_k, all_v, all_o)
+    count = len(shards)
+
+    def copy(src, dst, send, recv, **target):
+        return pltpu.make_async_remote_copy(
+            src_ref=src, dst_ref=dst, send_sem=send, recv_sem=recv, device_id=target, device_id_type=MESH
+        )
+
+    barrier = pltpu.get_barrier_semaphore()
+    for target in [{"dp": core_peer}, {"dp": y_peer}, {"expert": partner_x}] + [
+        {"expert": (a + k) % A * B + b} for k in range(1, A)
+    ]:
+        pl.semaphore_signal(barrier, inc=1, device_id=target, device_id_type=MESH)
+    pl.semaphore_wait(barrier, 2 + A)
+
+    def to_core(i):
+        return copy(shards[i], gathered[i].at[dp], core_send.at[i], w_recv.at[i, dp], dp=core_peer)
+
+    def to_y(i):
+        return copy(shards[i], gathered[i].at[dp], y_send.at[i], w_recv.at[i, dp], dp=y_peer)
+
+    def pass_on(i):
+        return copy(gathered[i].at[y_peer], gathered[i].at[y_peer], pass_send.at[i], w_recv.at[i, y_peer], dp=core_peer)
+
+    def wait_shard(i, owner):
+        copy(shards[i], gathered[i].at[owner], core_send.at[i], w_recv.at[i, owner], dp=core_peer).wait_recv()
+
+    def keep(i):
+        return pltpu.make_async_copy(shards[i], gathered[i].at[dp], local_sem.at[i])
+
+    def u_send_up(src, s):
+        return copy(src, u_all.at[s], u_up.at[s], u_recv.at[s], expert=me + B)
+
+    def u_send_down(src, s):
+        return copy(src, u_all.at[s], u_down.at[s], u_recv.at[s], expert=me - B)
+
+    def u_send_across(src, s):
+        return copy(src, u_all.at[s], u_across.at[s], u_recv.at[s], expert=partner_x)
+
+    keep_u = pltpu.make_async_copy(u_in, u_all.at[me], local_sem.at[count])
+
+    @pl.when(a < A - 1)
+    def _():
+        u_send_up(u_in, me).start()
+
+    @pl.when(a > 0)
+    def _():
+        u_send_down(u_in, me).start()
+
+    u_send_across(u_in, me).start()
+    for i in range(count):
+        to_y(i).start()
+        to_core(i).start()
+        keep(i).start()
+    keep_u.start()
+
+    def take(row):
+        @pl.when((row >= 0) & (row < A))
+        def _():
+            s = row * B + b
+            u_send_across(u_all.at[s], s).wait_recv()
+            u_send_across(u_all.at[s], s).start()
+
+            @pl.when((row < a) & (a < A - 1))
+            def _():
+                u_send_up(u_all.at[s], s).start()
+
+            @pl.when((row > a) & (a > 0))
+            def _():
+                u_send_down(u_all.at[s], s).start()
+
+    def forward(i):
+        wait_shard(i, y_peer)
+        pass_on(i).start()
+
+    for k in range(1, A):
+        take(a - k)
+        take(a + k)
+    for i in range(count):
+        forward(i)
+
+    for row in range(A):
+        s = row * B + 1 - b
+        u_send_across(u_all.at[s], s).wait_recv()
+    for i in range(count):
+        wait_shard(i, core_peer)
+        wait_shard(i, far_peer)
+        keep(i).wait()
+        to_y(i).wait_send()
+        to_core(i).wait_send()
+        pass_on(i).wait_send()
+    keep_u.wait()
+
+    @pl.when(a < A - 1)
+    def _():
+        u_send_up(u_in, me).wait_send()
+
+    @pl.when(a > 0)
+    def _():
+        u_send_down(u_in, me).wait_send()
+
+    for row in range(A):
+        s = row * B + b
+        u_send_across(u_all.at[s], s).wait_send()
+
+        @pl.when((row < a) & (a < A - 1))
+        def _():
+            u_send_up(u_all.at[s], s).wait_send()
+
+        @pl.when((row > a) & (a > 0))
+        def _():
+            u_send_down(u_all.at[s], s).wait_send()
+
+
+def front_call(w_query, w_key, w_value, w_output, w_small, out_grad):
+    n = 8
+    bf = jnp.bfloat16
+    any_spec = pl.BlockSpec(memory_space=pl.ANY)
+    dma = pltpu.SemaphoreType.DMA
+    shards = (w_query, w_key, w_value, w_output, w_small)
+    return pl.pallas_call(
+        front_kernel,
+        out_shape=tuple(jax.ShapeDtypeStruct((4, *w.shape), bf) for w in shards)
+        + (jax.ShapeDtypeStruct((n, *out_grad.shape), bf),),
+        in_specs=[pl.BlockSpec(memory_space=pltpu.VMEM)] * 6,
+        out_specs=(any_spec,) * 6,
+        scratch_shapes=[
+            dma((6,)), dma((5,)), dma((5,)), dma((5,)), dma((5, 4)), dma((n,)), dma((n,)), dma((n,)), dma((n,)),
+        ],
+        compiler_params=pltpu.CompilerParams(collective_id=3, has_side_effects=True, vmem_limit_bytes=32 * 1024 * 1024),
+        cost_estimate=pl.CostEstimate(flops=0, bytes_accessed=40 * 10**6, transcendentals=0),
+        name="gathers",
+    )(*shards, out_grad)
+
+
 def moe_by_collectives(hidden_two, all_upstream, dense_probs, expert_gate, expert_up, expert_down):
     local_count = expert_gate.shape[0]
     all_hidden = lax.all_gather(hidden_two, "expert", axis=0, tiled=True)
@@ -576,6 +931,44 @@
     return (mix_part.astype(jnp.bfloat16), hidden_two_grad, grad_dense, expert_totals)
 
 
+def sums_by_collectives(
+    hidden_one, attended, query_grad, key_grad, value_grad, branch_grad, router_partial, gain_one_partial, gain_two_partial
+):
+    query_partial = jnp.dot(hidden_one.T, query_grad, preferred_element_type=jnp.float32)
+    key_partial = jnp.dot(hidden_one.T, key_grad, preferred_element_type=jnp.float32)
+    value_partial = jnp.dot(hidden_one.T, value_grad, preferred_element_type=jnp.float32)
+    output_partial = jnp.dot(attended.T, branch_grad, preferred_element_type=jnp.float32)
+    pieces = jax.tree.map(
+        lambda part: part.astype(jnp.float32),
+        lax.psum_scatter(
+            shortened(
+                (
+                    query_partial,
+                    key_partial,
+                    value_partial,
+                    output_partial,
+                    router_partial,
+                    gain_one_partial,
+                    gain_two_partial,
+                )
+            ),
+            "dp",
+            scatter_dimension=0,
+            tiled=True,
+        ),
+    )
+    totals = (
+        lax.psum(pieces[0].astype(jnp.bfloat16), "expert").astype(jnp.float32),
+        lax.psum(pieces[1].astype(jnp.bfloat16), "expert").astype(jnp.float32),
+        lax.psum(pieces[2].astype(jnp.bfloat16), "expert").astype(jnp.float32),
+        lax.psum(pieces[3].astype(jnp.bfloat16), "expert").astype(jnp.float32),
+        lax.psum(pieces[4].astype(jnp.bfloat16), "expert").astype(jnp.float32),
+        lax.psum(pieces[5].astype(jnp.bfloat16), "expert").astype(jnp.float32),
+        lax.psum(pieces[6].astype(jnp.bfloat16), "expert").astype(jnp.float32),
+    )
+    return totals
+
+
 def fits_fused(dp_size, group, row_count):
     return dp_size == 4 and group == 8 and row_count == 256
 
@@ -596,17 +989,24 @@
     expert_down,
     out_grad,
 ):
-    shards = (w_query, w_key, w_value, w_output, w_router, attn_gain, moe_gain)
-    gathered = (
-        lax.all_gather(shards[0], "dp", axis=0, tiled=True),
-        lax.all_gather(shards[1], "dp", axis=0, tiled=True),
-        lax.all_gather(shards[2], "dp", axis=0, tiled=True),
-        lax.all_gather(shards[3], "dp", axis=0, tiled=True),
-        lax.all_gather(shards[4], "dp", axis=0, tiled=True),
-        lax.all_gather(shards[5], "dp", axis=0, tiled=True),
-        lax.all_gather(shards[6], "dp", axis=0, tiled=True),
-    )
-    query_w, key_w, value_w, output_w, router_w, gain_one, gain_two = gathered
+    group = lax.axis_size("expert")
+    fused = fits_fused(lax.axis_size("dp"), group, tokens.shape[0])
+    if fused:
+        small = jnp.concatenate([w_router, attn_gain[:, None], moe_gain[:, None]], axis=1)
+        small = jnp.pad(small, ((0, 0), (0, 128 - small.shape[1])))
+        gathered = front_call(w_query, w_key, w_value, w_output, small, out_grad)
+        query_w, key_w, value_w, output_w, small = [
+            whole.reshape(-1, whole.shape[2]) for whole in gathered[:5]
+        ]
+        experts_all = w_router.shape[1]
+        router_w, gain_one, gain_two = small[:, :experts_all], small[:, experts_all], small[:, experts_all + 1]
+        all_upstream = gathered[5].reshape(-1, out_grad.shape[1])
+    else:
+        query_w, key_w, value_w, output_w, router_w, gain_one, gain_two = [
+            lax.all_gather(shard, "dp", axis=0, tiled=True)
+            for shard in (w_query, w_key, w_value, w_output, w_router, attn_gain, moe_gain)
+        ]
+        all_upstream = lax.all_gather(out_grad, "expert", axis=0, tiled=True)
     row_count = tokens.shape[0]
     expert_count = w_router.shape[1]
     group_size = QH // KVH
@@ -671,9 +1071,7 @@
     dense_probs = jnp.sum(route_hot * gate_probs[:, :, None], axis=1)
     upstream = out_grad.astype(jnp.float32)
     local_count = expert_gate.shape[0]
-    group = lax.axis_size("expert")
-    all_upstream = lax.all_gather(out_grad, "expert", axis=0, tiled=True)
-    if fits_fused(lax.axis_size("dp"), group, row_count):
+    if fused:
         by_owner = jnp.pad(
             dense_probs.T.reshape(group, local_count, row_count), ((0, 0), (0, 8 - local_count), (0, 0))
         )
@@ -695,7 +1093,6 @@
         )
     gate_grad = jnp.sum(route_hot * grad_dense[:, None, :], axis=-1)
     mixture = lax.psum_scatter(mix_part, "expert", scatter_dimension=0, tiled=True)
-    layer_out = (residual + mixture.astype(jnp.float32)).astype(jnp.bfloat16)
     chosen_grad = gate_probs * (gate_grad - jnp.sum(gate_probs * gate_grad, axis=-1, keepdims=True))
     logit_grad = jnp.sum(route_hot * chosen_grad[:, :, None], axis=1).astype(jnp.bfloat16)
     hidden_two_grad = hidden_two_grad + jnp.dot(
@@ -765,39 +1162,39 @@
         normed_one_grad
         - normed_one * jnp.mean(normed_one_grad * normed_one, axis=-1, keepdims=True)
     )
-    query_partial = jnp.dot(hidden_one.T, query_grad, preferred_element_type=jnp.float32)
-    key_partial = jnp.dot(hidden_one.T, key_grad, preferred_element_type=jnp.float32)
-    value_partial = jnp.dot(hidden_one.T, value_grad, preferred_element_type=jnp.float32)
-    output_partial = jnp.dot(attended.T, branch_grad, preferred_element_type=jnp.float32)
     router_partial = jnp.dot(hidden_two.T, logit_grad, preferred_element_type=jnp.float32)
-    pieces = jax.tree.map(
-        lambda part: part.astype(jnp.float32),
-        lax.psum_scatter(
-            shortened(
-                (
-                    query_partial,
-                    key_partial,
-                    value_partial,
-                    output_partial,
-                    router_partial,
-                    gain_one_partial,
-                    gain_two_partial,
-                )
-            ),
-            "dp",
-            scatter_dimension=0,
-            tiled=True,
-        ),
-    )
-    totals = (
-        lax.psum(pieces[0].astype(jnp.bfloat16), "expert").astype(jnp.float32),
-        lax.psum(pieces[1].astype(jnp.bfloat16), "expert").astype(jnp.float32),
-        lax.psum(pieces[2].astype(jnp.bfloat16), "expert").astype(jnp.float32),
-        lax.psum(pieces[3].astype(jnp.bfloat16), "expert").astype(jnp.float32),
-        lax.psum(pieces[4].astype(jnp.bfloat16), "expert").astype(jnp.float32),
-        lax.psum(pieces[5].astype(jnp.bfloat16), "expert").astype(jnp.float32),
-        lax.psum(pieces[6].astype(jnp.bfloat16), "expert").astype(jnp.float32),
-    )
+    if fused:
+        extra = jnp.concatenate(
+            [router_partial, gain_one_partial[:, None], gain_two_partial[:, None]], axis=1
+        )
+        spare = 128 - extra.shape[1]
+        extra = jnp.pad(extra, ((0, 0), (0, spare))).astype(jnp.bfloat16)
+        zero_columns = jnp.zeros((row_count, 128), jnp.bfloat16)
+        sums = reduce_call(
+            jnp.stack([attended, hidden_one]),
+            jnp.concatenate([branch_grad, query_grad, key_grad, value_grad, zero_columns], axis=1),
+            extra,
+        )
+        wide, narrow = query_w.shape[1], key_w.shape[1]
+        cuts = (0, wide, 2 * wide, 2 * wide + narrow, 2 * wide + 2 * narrow)
+        of_output, of_query, of_key, of_value = [sums[:, i:j] for i, j in zip(cuts, cuts[1:])]
+        tail = sums[:, cuts[-1] :]
+        totals = (
+            of_query,
+            of_key,
+            of_value,
+            of_output,
+            tail[:, :expert_count],
+            tail[:, expert_count],
+            tail[:, expert_count + 1],
+        )
+    else:
+        totals = sums_by_collectives(
+            hidden_one, attended, query_grad, key_grad, value_grad, branch_grad, router_partial, gain_one_partial,
+            gain_two_partial,
+        )
+    late_residual, _ = lax.optimization_barrier((residual, totals[0]))
+    layer_out = (late_residual + mixture.astype(jnp.float32)).astype(jnp.bfloat16)
     return (
         layer_out,
         in_grad,

time: 894 us -> 545 us (0.61)
  waiting for transfers between devices: 527 us -> 0.02 us
  Pallas kernels: 193 us -> 414 us
  blocking collectives: 62.1 us -> 0 us
  local copies, waits for them, and re-layouts: 20 us -> 62.1 us
  matrix products: 50.1 us -> 33.8 us
    pallas_call x0 -> x2, Pallas kernels: none -> 217 us  [the longest x1 137 us: reduce_call(): pl.pallas_call(reduce_kernel, out_shape=jax.ShapeDtypeStruct((shard, widt...]
    all_gather x5 -> x0, waiting for transfers between devices: 182 us -> none  [the longest x1 93.3 us: body(): all_upstream = lax.all_gather(out_grad, 'expert', axis=0, tiled=True)]
    reduce_scatter x4 -> x0, waiting for transfers between devices: 132 us -> none  [body(): lax.psum_scatter(shortened((query_partial, key_partial, value_partial, ou...]
    reduce_scatter x1, waiting for transfers between devices: 117 us -> 0.01 us  [body(): lax.psum_scatter(mix_part, 'expert', scatter_dimension=0, tiled=True)]
    psum x1 -> x0, waiting for transfers between devices: 76.2 us -> none  [body(): lax.psum(pieces[0].astype(jnp.bfloat16), 'expert').astype(jnp.float32)]
    psum x1 -> x0, blocking collectives: 39 us -> none  [body(): lax.psum(pieces[4].astype(jnp.bfloat16), 'expert').astype(jnp.float32)]
    unnamed x13 -> x1, waiting for transfers between devices: 20.5 us -> 0.02 us
    all_gather x3 -> x0, blocking collectives: 17 us -> none  [the longest x1 6.12 us: body(): lax.all_gather(shards[6], 'dp', axis=0, tiled=True)]
  transfers between devices with their start and end apart: 12 -> 1, of which waited for: 11 -> 0; matrix products, arithmetic and copies ran while one was open for 7% -> 10% of each run, Pallas kernels for 0% -> 25%
where the time goes in v3:
time: 545 us; the launch traced here: 543 us
  Pallas kernels  414 us (76%)
  local copies, waits for them, and re-layouts  62.1 us (11%)
  matrix products  33.8 us (6%)
  other arithmetic  18.3 us (3%)
  between operations  15 us (3%)
    pallas_call x1, Pallas kernels, moe_call(): pl.pallas_call(functools.partial(moe_kernel, comm=True), out_shape=out_sh...  197 us
    pallas_call x1, Pallas kernels, reduce_call(): pl.pallas_call(reduce_kernel, out_shape=jax.ShapeDtypeStruct((shard, widt...  137 us
    pallas_call x1, Pallas kernels, front_call(): pl.pallas_call(front_kernel, out_shape=tuple((jax.ShapeDtypeStruct((4, *w...  79.6 us
    unnamed x148, local copies, waits for them, and re-layouts  27.4 us
  transfers between devices with their start and end apart: 1, of which 0 were waited for; matrix products, arithmetic and copies ran while one was open for 10% of the time, Pallas kernels for 25%

profile of v3, /device:TPU:0, one launch (start us, length us, event | category | flops | bytes accessed | tf_op | source)
XLA Modules:
  0.0 542.9 jit_solution(9452065378273132800)
XLA Ops:
  19.4 79.6 %gathers.1 = (bf16[4,384,1536]{2,1,0:T(8,128)(2,1)S(1)}, bf16[4,384,512]{2,1,0:T(8,128)(2,1)S(1)}, bf16[4,384,512]{2,1,0:T(8,128)(2,1)S(1)}, bf16[4,384,1536]{2,...) custom-call(bf16[384,1536]{1,0:T(8,128)(2,1)S(1)} %copy-done.11, ...), custom_call_target="tpu_custom_call" | custom-call | bytes 40000000 | tf_op jit(solution)/shard_map/gathers/pallas_call | solution.py:867
  99.0 2.2 copy-done
  101.2 2.2 copy-done.5
  107.2 1.8 copy.115
  109.7 2.5 convolution_convert_fusion.2
  114.8 2.1 fusion.31
  116.9 6.7 %copy.94 = bf16[1536,1536]{1,0:T(8,128)(2,1)} copy(bf16[1536,1536]{0,1:T(8,128)(2,1)} %bitcast.112) | data formatting | bytes 9437184 | tf_op jit(solution)/shard_map/dot_general | solution.py:1025
  123.6 3.9 fusion.29
  132.5 2.0 slice-done
  139.8 196.7 %experts.1 = (bf16[8,256,1536]{2,1,0:T(8,128)(2,1)}, f32[256,1536]{1,0:T(8,128)}, f32[8,8,256]{2,1,0:T(8,128)}, f32[6,384,512]{2,1,0:T(8,128)}, bf16[2,6,384,512...) custom-call(bf16[256,1536]{1,0:T(8,128)(2,1)} %copy-done.22, bf16[8,256,1536]{2,1,0:T(8,128)(2,1)} %get-tuple-element.85.u_in, ...), custom_call_target="tpu_custom_call" | custom-call | flops 57999998976 | bytes 60000000 | tf_op jit(solution)/shard_map/experts/pallas_call | solution.py:491
  340.1 2.2 multiply_reduce_fusion
  347.1 3.9 fusion.26
  351.9 4.3 fusion
  356.3 1.6 fusion.2
  357.9 1.7 copy-done.19
  361.7 2.6 convolution_multiply_fusion
  364.9 3.9 fusion.53
  377.7 1.7 fusion.18
  380.7 137.3 %weight_sums.1 = f32[384,4224]{1,0:T(8,128)} custom-call(bf16[2,256,1536]{2,1,0:T(8,128)(2,1)} %pad_maximum_fusion.left, bf16[256,4224]{1,0:T(8,128)(2,1)} %broadcast_dynamic-update-slice_fusion.right, bf16[1536,128]{1,0:T(8,128)(2,1)} %pad.15.extra), custom_call_target="tpu_custom_call" | custom-call | flops 4000000000 | bytes 20000000 | tf_op jit(solution)/shard_map/weight_sums/pallas_call | solution.py:704
  519.6 4.9 fusion.48
  524.5 1.9 slice_reduce_fusion
  526.4 2.6 fusion.49
  529.0 4.8 fusion.50
  533.8 2.2 add_convert_fusion
  (216 shorter events, 52.7 us)
Async XLA Ops:
  7.2 7.6 %copy-start.6 = (bf16[256,1536]{1,0:T(8,128)(2,1)S(1)}, bf16[256,1536]{1,0:T(8,128)(2,1)}, u32[]{:S(2)}) copy-start(bf16[256,1536]{1,0:T(8,128)(2,1)} %u_in.1) | copy-start | bytes 2359300
  7.2 526.6 %reduce-scatter.2.cloned.1.call-start = ((), (), s32[]{:S(2)}) async-start(), calls=%async_computation.1 | async-start | bytes 7077888 | tf_op jit(solution)/shard_map/reduce_scatter | solution.py:1095
  104.5 8.7 %copy-start.1 = (bf16[4,384,512]{2,1,0:T(8,128)(2,1)}, bf16[4,384,512]{2,1,0:T(8,128)(2,1)S(1)}, u32[]{:S(2)}) copy-start(bf16[4,384,512]{2,1,0:T(8,128)(2,1)S(1)} %get-tuple-element.82) | copy-start | bytes 4718596
  104.5 32.6 %copy-start.3 = (bf16[4,384,128]{2,1,0:T(8,128)(2,1)}, bf16[4,384,128]{2,1,0:T(8,128)(2,1)S(1)}, u32[]{:S(2)}) copy-start(bf16[4,384,128]{2,1,0:T(8,128)(2,1)S(1)} %get-tuple-element.80) | copy-start | bytes 1179652
  104.5 5.2 copy-start.9
  107.1 29.1 %copy-start.48 = (f32[1536]{0:T(1024)}, f32[1536]{0:T(1024)S(1)}, u32[]{:S(2)}) copy-start(f32[1536]{0:T(1024)S(1)} %convert_reduce_fusion) | copy-start | bytes 18436
  109.6 14.0 %copy-start.54 = (f32[1536]{0:T(1024)}, f32[1536]{0:T(1024)S(1)}, u32[]{:S(2)}) copy-start(f32[1536]{0:T(1024)S(1)} %convert_reduce_fusion.1) | copy-start | bytes 18436
  113.2 17.8 %copy-start.37 = (bf16[256,512]{0,1:T(8,128)(2,1)}, bf16[256,512]{0,1:T(8,128)(2,1)S(1)}, u32[]{:S(2)}) copy-start(bf16[256,512]{0,1:T(8,128)(2,1)S(1)} %copy.92) | copy-start | bytes 786436
  123.6 3.9 copy-start.63
  123.6 3.9 copy-start.64
  131.0 3.5 slice-start
  131.1 3.6 slice-start.1
  132.5 3.6 copy-start.26
  336.6 3.5 copy-start.17
  336.6 8.3 %slice-start.2 = ((s8[4718592]{0:T(1024)(128)(4,1)}), s8[524288]{0:T(1024)(128)(4,1)S(1)}, s32[]{:S(2)}) async-start(s8[4718592]{0:T(1024)(128)(4,1)} %bitcast.104), calls=%async_computation.4 | async-start | bytes 1048576
  336.7 3.4 copy-start.4
  336.7 3.4 copy-start.49
  340.1 4.8 slice-start.3
  347.1 4.8 copy-start.38
  351.0 5.2 slice-start.4
  351.9 4.4 slice-start.5
  364.9 3.9 copy-start.2
  373.9 3.9 copy-start.29
  529.0 4.8 copy-start.18
  (48 other events, 72.9 us)
Sparse Core Ops, SparseCore 0:
  336.7 158.4 reduce-scatter.1

commit v4 on v1

--- a/solution.py
+++ b/solution.py
@@ -1,7 +1,14 @@
+import functools
+import math
+
 import jax
 import jax.numpy as jnp
 from jax import lax
+from jax.experimental import pallas as pl
+from jax.experimental.pallas import tpu as pltpu
 from jax.sharding import PartitionSpec as P
+
+MESH = pl.DeviceIdType.MESH
 
 QH = 24
 KVH = 8
@@ -340,6 +347,1195 @@
     )
 
 
+NT = (((1,), (1,)), ((), ()))
+TN = (((0,), (0,)), ((), ()))
+
+
+def dot_f32(left, right, dims=(((1,), (0,)), ((), ()))):
+    return lax.dot_general(left, right, dims, preferred_element_type=jnp.float32)
+
+
+def entry(rows, index, step):
+    value = 0
+    for place, row in enumerate(rows):
+        for column, digit in enumerate(row):
+            if digit:
+                value = jnp.where((index == place) & (step == column), digit, value)
+    return value
+
+
+BLOCK_ORDER = (
+    (0, 4, 1, 2, 5, 3, 7, 6),
+    (1, 5, 0, 2, 4, 3, 7, 6),
+    (2, 6, 3, 1, 7, 0, 4, 5),
+    (3, 7, 2, 1, 6, 0, 4, 5),
+)
+TAKE_FIRST = (
+    (15, 1, 15, 2, 5, 3, 7, 6),
+    (15, 0, 15, 3, 15, 7, 15, 6),
+    (15, 3, 15, 0, 15, 4, 15, 5),
+    (15, 2, 15, 1, 6, 0, 4, 5),
+)
+TAKE_SECOND = (
+    (15, 4, 15, 15, 15, 15, 15, 15),
+    (15, 2, 15, 4, 15, 15, 15, 15),
+    (15, 1, 15, 7, 15, 15, 15, 15),
+    (15, 7, 15, 15, 15, 15, 15, 15),
+)
+TAKE_THIRD = (
+    (15, 15, 15, 15, 15, 15, 15, 15),
+    (15, 5, 15, 15, 15, 15, 15, 15),
+    (15, 6, 15, 15, 15, 15, 15, 15),
+    (15, 15, 15, 15, 15, 15, 15, 15),
+)
+SUM_ORDER = (
+    (3, 2, 7, 7, 0),
+    (7, 3, 0, 2, 1),
+    (7, 0, 3, 1, 2),
+    (0, 1, 7, 7, 3),
+)
+HALVES = 2
+
+
+def moe_kernel(
+    h_in, u_in, p_in, wg_in, wu_in, wd_in,
+    d_out, e_out, gg_out, grads_out, core_got, y_out,
+    h_all, u_all, p_all, wg, wu, wd, act, gu, ex, ez, rx, rz, d_stage, gg_stage, tile_bf, tile_f32, got_tile,
+    load_sem, h_up, h_down, h_across, h_recv, p_send, p_recv, g_send, g_recv,
+    x_send, x_recv, z_send, z_recv, d_sem, c_send, c_recv, y_send, tile_sem, out_sem,
+    *, comm
+):
+    A, B, n = 4, 2, 8
+    R, D = h_in.shape
+    F = wg.shape[2]
+    shard = D // 4
+    me = lax.axis_index("expert")
+    dp = lax.axis_index("dp")
+    a, b = me // B, me % B
+    y, c = dp // 2, dp % 2
+    partner_x = a * B + (1 - b)
+    core_peer = 2 * y + (1 - c)
+    y_peer = 2 * (1 - y) + c
+
+    def copy(src, dst, send, recv, **target):
+        return pltpu.make_async_remote_copy(
+            src_ref=src, dst_ref=dst, send_sem=send, recv_sem=recv, device_id=target, device_id_type=MESH
+        )
+
+    loads = [
+        pltpu.make_async_copy(h_in, h_all.at[me], load_sem.at[0]),
+        pltpu.make_async_copy(u_in, u_all, load_sem.at[1]),
+        pltpu.make_async_copy(wg_in, wg, load_sem.at[2]),
+        pltpu.make_async_copy(wu_in, wu, load_sem.at[3]),
+        pltpu.make_async_copy(wd_in, wd, load_sem.at[4]),
+        pltpu.make_async_copy(p_in.at[me], p_all.at[me], load_sem.at[5]),
+    ]
+    for load in loads:
+        load.start()
+
+    barrier = pltpu.get_barrier_semaphore()
+    for k in range(1, n):
+        pl.semaphore_signal(barrier, inc=1, device_id={"expert": (me + k) % n}, device_id_type=MESH)
+    pl.semaphore_signal(barrier, inc=1, device_id={"dp": core_peer}, device_id_type=MESH)
+    pl.semaphore_wait(barrier, n)
+    loads[0].wait()
+    loads[5].wait()
+
+    def send_up(s):
+        return copy(h_all.at[s], h_all.at[s], h_up.at[s], h_recv.at[s], expert=me + B)
+
+    def send_down(s):
+        return copy(h_all.at[s], h_all.at[s], h_down.at[s], h_recv.at[s], expert=me - B)
+
+    def send_across(s):
+        return copy(h_all.at[s], h_all.at[s], h_across.at[s], h_recv.at[s], expert=partner_x)
+
+    def p_copy(peer):
+        return copy(p_in.at[peer], p_all.at[me], p_send.at[peer], p_recv.at[me], expert=peer)
+
+    @pl.when(a < A - 1)
+    def _():
+        send_up(me).start()
+
+    @pl.when(a > 0)
+    def _():
+        send_down(me).start()
+
+    send_across(me).start()
+    for k in range(1, n):
+        p_copy((me + k) % n).start()
+    for k in range(1, n):
+        s = (me + k) % n
+        copy(p_in.at[s], p_all.at[s], p_send.at[s], p_recv.at[s], expert=s).wait_recv()
+    for load in loads[1:5]:
+        load.wait()
+
+    def recv_block(s):
+        send_across(s).wait_recv()
+
+    def pass_along(row, s):
+        @pl.when((row <= a) & (a < A - 1))
+        def _():
+            send_up(s).start()
+
+        @pl.when((row >= a) & (a > 0))
+        def _():
+            send_down(s).start()
+
+    def take(code):
+        @pl.when(code < n)
+        def _():
+            across = code >= A
+            row = code % A
+            s = row * B + jnp.where(across, 1 - b, b)
+            recv_block(s)
+
+            @pl.when(jnp.logical_not(across))
+            def _():
+                pass_along(row, s)
+
+                @pl.when(((a == 0) & (row == 1)) | ((a == A - 1) & (row == A - 2)))
+                def _():
+                    send_across(s).start()
+
+            @pl.when(across & ((row == 0) | (row == A - 1)))
+            def _():
+                pass_along(row, s)
+
+                @pl.when((a > 0) & (a < A - 1) & ((row == 0) == (a == 1)))
+                def _():
+                    near = a * B + 1 - b
+
+                    @pl.when(a == 1)
+                    def _():
+                        send_up(near).start()
+
+                    @pl.when(a == A - 2)
+                    def _():
+                        send_down(near).start()
+
+            @pl.when(across & (row == 1) & (a == 2))
+            def _():
+                send_up(s).start()
+
+            @pl.when(across & (row == 2) & (a == 1))
+            def _():
+                send_down(s).start()
+
+    def d_copy(s, slot):
+        return pltpu.make_async_copy(d_stage.at[slot], d_out.at[s], d_sem.at[slot])
+
+    def g_copy(s):
+        return copy(gg_stage.at[s], gg_out.at[me], g_send.at[s], g_recv.at[me], expert=s)
+
+    def compute(step, s, row, across):
+        rows = pl.ds(pl.multiple_of(s * R, R), R)
+        probs = jnp.transpose(p_all[s])
+        grad_cols = []
+        for e in range(2):
+            gate_pre = dot_f32(h_all[s], wg[e])
+            up_pre = dot_f32(h_all[s], wu[e])
+            raw = dot_f32(u_all[s], wd[e])
+            prob = probs[:, e : e + 1]
+            sig = 1.0 / (1.0 + jnp.exp(-gate_pre))
+            gate_act = gate_pre * sig
+            activation = gate_act * up_pre
+            grad_cols.append(jnp.sum(activation * raw, axis=1, keepdims=True))
+            act[rows, e * F : (e + 1) * F] = (activation * prob).astype(jnp.bfloat16)
+            act_grad = raw * prob
+            gate_grad = act_grad * up_pre * sig * (1.0 + gate_pre * (1.0 - sig))
+            gu[rows, 2 * e * F : (2 * e + 1) * F] = gate_grad.astype(jnp.bfloat16)
+            gu[rows, (2 * e + 1) * F : (2 * e + 2) * F] = (act_grad * gate_act).astype(jnp.bfloat16)
+        column = lax.broadcasted_iota(jnp.int32, (R, 128), 1)
+        both = jnp.where(column == 0, grad_cols[0], jnp.where(column == 1, grad_cols[1], 0.0))
+        gg_stage[s] = jnp.transpose(both)[:8]
+        slot = step % 2
+
+        @pl.when(step >= 2)
+        def _():
+            d_copy(s, slot).wait()
+
+        def columns(tile, _):
+            cols = pl.ds(pl.multiple_of(tile * 512, 512), 512)
+            mixed = dot_f32(act[rows, 0:F], wd[0, cols, :], NT) + dot_f32(act[rows, F : 2 * F], wd[1, cols, :], NT)
+            d_stage[slot, :, cols] = mixed.astype(jnp.bfloat16)
+            back = dot_f32(gu[rows, 0:F], wg[0, cols, :], NT)
+            back += dot_f32(gu[rows, F : 2 * F], wu[0, cols, :], NT)
+            back += dot_f32(gu[rows, 2 * F : 3 * F], wg[1, cols, :], NT)
+            back += dot_f32(gu[rows, 3 * F : 4 * F], wu[1, cols, :], NT)
+
+            @pl.when(across)
+            def _():
+                ex[row, :, cols] = back.astype(jnp.bfloat16)
+
+            @pl.when(jnp.logical_not(across))
+            def _():
+                ez[row, :, cols] = back.astype(jnp.bfloat16)
+
+            return 0
+
+        lax.fori_loop(0, D // 512, columns, 0)
+        d_copy(s, slot).start()
+
+        @pl.when(s != me)
+        def _():
+            g_copy(s).start()
+
+        @pl.when(s == me)
+        def _():
+            pltpu.make_async_copy(gg_stage.at[s], gg_out.at[me], g_send.at[s]).start()
+
+    part_rows = R // HALVES
+
+    def part_of(part):
+        return pl.ds(pl.multiple_of(part * part_rows, 16), part_rows)
+
+    def x_copy(row, part):
+        return copy(ex.at[row, part_of(part)], rx.at[row, part_of(part)], x_send.at[row, part], x_recv.at[row, part], expert=partner_x)
+
+    def z_up(row, part):
+        return copy(ez.at[row, part_of(part)], rz.at[row + 1, part_of(part)], z_send.at[row, part], z_recv.at[row + 1, part], expert=me + B)
+
+    def z_down(row, part):
+        return copy(ez.at[row, part_of(part)], rz.at[row, part_of(part)], z_send.at[row, part], z_recv.at[row, part], expert=me - B)
+
+    def sum_part(row, part):
+        x_copy(row, part).wait_recv()
+        below = (a > 0) & (row >= a)
+        above = (a < A - 1) & (row <= a)
+
+        @pl.when(below)
+        def _():
+            z_up(row, part).wait_recv()
+
+        @pl.when(above)
+        def _():
+            z_down(row, part).wait_recv()
+
+        def chunk(index, _):
+            rows = pl.ds(pl.multiple_of(part * part_rows + index * 64, 64), 64)
+            total = ez[row, rows, :].astype(jnp.float32) + rx[row, rows, :].astype(jnp.float32)
+
+            @pl.when(row != a)
+            def _():
+                @pl.when(below)
+                def _():
+                    ez[row, rows, :] = (total + rz[row + 1, rows, :].astype(jnp.float32)).astype(jnp.bfloat16)
+
+                @pl.when(above)
+                def _():
+                    ez[row, rows, :] = (total + rz[row, rows, :].astype(jnp.float32)).astype(jnp.bfloat16)
+
+                @pl.when(jnp.logical_not(below | above))
+                def _():
+                    ez[row, rows, :] = total.astype(jnp.bfloat16)
+
+            @pl.when(row == a)
+            def _():
+                @pl.when(below & above)
+                def _():
+                    e_out[rows, :] = total + rz[row + 1, rows, :].astype(jnp.float32) + rz[row, rows, :].astype(jnp.float32)
+
+                @pl.when(below & jnp.logical_not(above))
+                def _():
+                    e_out[rows, :] = total + rz[row + 1, rows, :].astype(jnp.float32)
+
+                @pl.when(above & jnp.logical_not(below))
+                def _():
+                    e_out[rows, :] = total + rz[row, rows, :].astype(jnp.float32)
+
+            return 0
+
+        lax.fori_loop(0, part_rows // 64, chunk, 0)
+
+        @pl.when(row > a)
+        def _():
+            z_up(row, part).start()
+
+        @pl.when(row < a)
+        def _():
+            z_down(row, part).start()
+
+    def sum_parts(row):
+        def one(part, _):
+            sum_part(row, part)
+            return 0
+
+        lax.fori_loop(0, HALVES, one, 0)
+
+    def block_step(step, _):
+        @pl.when((step == n - 1) & ((a == 0) | (a == A - 1)))
+        def _():
+            sum_parts(jnp.where(a == 0, 1, A - 2))
+
+        take(entry(TAKE_FIRST, a, step))
+        take(entry(TAKE_SECOND, a, step))
+        take(entry(TAKE_THIRD, a, step))
+        code = entry(BLOCK_ORDER, a, step)
+        across = code >= A
+        row = code % A
+        s = row * B + jnp.where(across, 1 - b, b)
+        compute(step, s, row, across)
+
+        @pl.when(across)
+        def _():
+            for part in range(HALVES):
+                x_copy(row, part).start()
+
+        return 0
+
+    lax.fori_loop(0, n, block_step, 0)
+
+    def core_copy(slot, which, index):
+        return copy(tile_bf.at[slot], core_got.at[which, index], c_send.at[slot], c_recv.at[which, index], dp=core_peer)
+
+    def y_copy(slot, index):
+        return pltpu.make_async_copy(tile_bf.at[slot], y_out.at[index], y_send.at[slot])
+
+    def weight_tile(group, e, kind, left, right):
+        owner = jnp.where(group == 0, 2 * (1 - y) + 1 - c, jnp.where(group == 1, y_peer, jnp.where(group == 2, core_peer, dp)))
+        cols = pl.ds(pl.multiple_of(owner * shard, 128), shard)
+        total = dot_f32(left[:, :, cols].reshape(n * R, shard), right, TN)
+        index = kind * 2 + e
+        slot = kind
+
+        @pl.when((group == 0) | (group == 2))
+        def _():
+            @pl.when(e > 0)
+            def _():
+                core_copy(slot, 0, index).wait_send()
+
+            @pl.when((e == 0) & (group == 2))
+            def _():
+                y_copy(slot, index).wait()
+
+            tile_bf[slot] = total.astype(jnp.bfloat16)
+            core_copy(slot, group // 2, index).start()
+
+        @pl.when(group == 1)
+        def _():
+            @pl.when(e == 0)
+            def _():
+                core_copy(slot, 0, index).wait_send()
+
+            @pl.when(e > 0)
+            def _():
+                y_copy(slot, index).wait()
+
+            core_copy(slot, 0, index).wait_recv()
+            got = pltpu.make_async_copy(core_got.at[0, index], got_tile, tile_sem)
+            got.start()
+            got.wait()
+            tile_bf[slot] = (total + got_tile[...].astype(jnp.float32)).astype(jnp.bfloat16)
+            y_copy(slot, index).start()
+
+        @pl.when(group == 3)
+        def _():
+            core_copy(slot, 1, index).wait_recv()
+            got = pltpu.make_async_copy(core_got.at[1, index], got_tile, tile_sem)
+            got.start()
+            got.wait()
+            tile_f32[index] = total + got_tile[...].astype(jnp.float32)
+            pltpu.make_async_copy(tile_f32.at[index], grads_out.at[index], out_sem.at[index]).start()
+
+    def sum_step(place, _):
+        row = entry(SUM_ORDER, a, place)
+
+        @pl.when(row < A)
+        def _():
+            sum_parts(row)
+
+        @pl.when(place < 4)
+        def _():
+            def pair(e, _):
+                weight_tile(place, e, 0, h_all, gu[:, pl.ds(pl.multiple_of(2 * e * F, 128), F)])
+                weight_tile(place, e, 1, h_all, gu[:, pl.ds(pl.multiple_of((2 * e + 1) * F, 128), F)])
+                weight_tile(place, e, 2, u_all, act[:, pl.ds(pl.multiple_of(e * F, 128), F)])
+                return 0
+
+            lax.fori_loop(0, 2, pair, 0)
+
+        return 0
+
+    lax.fori_loop(0, 5, sum_step, 0)
+
+    for kind in range(3):
+        core_copy(kind, 1, 3 + kind).wait_send()
+    for row in range(A):
+        for part in range(HALVES):
+            x_copy(row, part).wait_send()
+
+            @pl.when(row != a)
+            def _():
+                z_up(row, part).wait_send()
+
+    for row in range(A):
+        s = row * B + b
+        far = row * B + 1 - b
+
+        @pl.when((row <= a) & (a < A - 1))
+        def _():
+            send_up(s).wait_send()
+
+        @pl.when((row >= a) & (a > 0))
+        def _():
+            send_down(s).wait_send()
+
+        @pl.when((row <= a) & (a < A - 1) & (row < A - 2))
+        def _():
+            send_up(far).wait_send()
+
+        @pl.when((row >= a) & (a > 0) & (row > 1))
+        def _():
+            send_down(far).wait_send()
+
+        @pl.when((row == a) | ((a == 0) & (row == 1)) | ((a == A - 1) & (row == A - 2)))
+        def _():
+            send_across(s).wait_send()
+
+    for k in range(1, n):
+        s = (me + k) % n
+        p_copy(s).wait_send()
+        g_copy(s).wait_send()
+        copy(gg_stage.at[s], gg_out.at[s], g_send.at[s], g_recv.at[s], expert=s).wait_recv()
+    pltpu.make_async_copy(gg_stage.at[me], gg_out.at[me], g_send.at[me]).wait()
+    for slot in range(2):
+        d_copy(0, slot).wait()
+    for index in range(6):
+        pltpu.make_async_copy(tile_f32.at[index], grads_out.at[index], out_sem.at[index]).wait()
+
+
+def moe_call(hidden, all_upstream, probs, expert_gate, expert_up, expert_down):
+    R, D = hidden.shape
+    F = expert_gate.shape[2]
+    A, n = 4, 8
+    shard = D // 4
+    bf, f32 = jnp.bfloat16, jnp.float32
+    any_spec = pl.BlockSpec(memory_space=pl.ANY)
+    vmem = pl.BlockSpec(memory_space=pltpu.VMEM)
+    dma = pltpu.SemaphoreType.DMA
+    out_shape = (
+        jax.ShapeDtypeStruct((n, R, D), bf),
+        jax.ShapeDtypeStruct((R, D), f32),
+        jax.ShapeDtypeStruct((n, 8, R), f32),
+        jax.ShapeDtypeStruct((6, shard, F), f32),
+        jax.ShapeDtypeStruct((2, 6, shard, F), bf),
+        jax.ShapeDtypeStruct((6, shard, F), bf),
+    )
+    return pl.pallas_call(
+        functools.partial(moe_kernel, comm=True),
+        out_shape=out_shape,
+        in_specs=[any_spec] * 6,
+        out_specs=(any_spec, vmem, any_spec, any_spec, any_spec, any_spec),
+        scratch_shapes=[
+            pltpu.VMEM((n, R, D), bf),
+            pltpu.VMEM((n, R, D), bf),
+            pltpu.VMEM((n, 8, R), f32),
+            pltpu.VMEM((2, D, F), bf),
+            pltpu.VMEM((2, D, F), bf),
+            pltpu.VMEM((2, D, F), bf),
+            pltpu.VMEM((n * R, 2 * F), bf),
+            pltpu.VMEM((n * R, 4 * F), bf),
+            pltpu.VMEM((A, R, D), bf),
+            pltpu.VMEM((A, R, D), bf),
+            pltpu.VMEM((A, R, D), bf),
+            pltpu.VMEM((A + 1, R, D), bf),
+            pltpu.VMEM((2, R, D), bf),
+            pltpu.VMEM((n, 8, R), f32),
+            pltpu.VMEM((3, shard, F), bf),
+            pltpu.VMEM((6, shard, F), f32),
+            pltpu.VMEM((shard, F), bf),
+            dma((6,)), dma((n,)), dma((n,)), dma((n,)), dma((n,)), dma((n,)), dma((n,)), dma((n,)), dma((n,)),
+            dma((A, HALVES)), dma((A, HALVES)), dma((A, HALVES)), dma((A + 1, HALVES)), dma((2,)),
+            dma((3,)), dma((2, 6)), dma((3,)), dma, dma((6,)),
+        ],
+        compiler_params=pltpu.CompilerParams(
+            collective_id=1, has_side_effects=True, vmem_limit_bytes=64 * 1024 * 1024 - 65536
+        ),
+        cost_estimate=pl.CostEstimate(flops=58 * 10**9, bytes_accessed=60 * 10**6, transcendentals=2 * 10**6),
+        name="experts",
+    )(hidden, all_upstream, probs, expert_gate, expert_up, expert_down)
+
+
+def reduce_kernel(
+    left, right, extra, out,
+    core_out, core_in, y_out, y_in, half, x_out, x_in, own, z_out, z_in, full,
+    core_send, core_recv, y_send, y_recv, x_send, x_recv, zs_send, zs_recv, zg_send, zg_recv, xg_send, xg_recv,
+):
+    A, B = 4, 2
+    W = core_out.shape[3]
+    shard = core_out.shape[2]
+    half_rows, piece = shard // B, shard // (A * B)
+    chunks = y_in.shape[0]
+    me = lax.axis_index("expert")
+    dp = lax.axis_index("dp")
+    a, b = me // B, me % B
+    y, c = dp // 2, dp % 2
+    partner_x = a * B + (1 - b)
+    core_peer = 2 * y + (1 - c)
+    y_peer = 2 * (1 - y) + c
+
+    def copy(src, dst, send, recv, **target):
+        return pltpu.make_async_remote_copy(
+            src_ref=src, dst_ref=dst, send_sem=send, recv_sem=recv, device_id=target, device_id_type=MESH
+        )
+
+    barrier = pltpu.get_barrier_semaphore()
+    for target in [{"dp": core_peer}, {"dp": y_peer}, {"expert": partner_x}] + [
+        {"expert": (a + k) % A * B + b} for k in range(1, A)
+    ]:
+        pl.semaphore_signal(barrier, inc=1, device_id=target, device_id_type=MESH)
+    pl.semaphore_wait(barrier, 2 + A)
+
+    def partial(chunk, owner):
+        rows = pl.ds(pl.multiple_of(owner * shard, 128), shard)
+        cols = pl.ds(pl.multiple_of(chunk * W, 128), W)
+        which = jnp.where(chunk < 4, 0, 1)
+        total = dot_f32(left[which, :, rows], right[:, cols], TN)
+        share = extra[pl.ds(pl.multiple_of(owner * shard, 128), shard), :].astype(jnp.float32)
+        share = jnp.where(chunk == chunks - 1, share, 0.0)
+        return jnp.concatenate([total[:, : W - 128], total[:, W - 128 :] + share], axis=1)
+
+    def core_copy(chunk, which):
+        slot = chunk % 2
+        return copy(core_out.at[slot, which], core_in.at[chunk, which], core_send.at[slot, which], core_recv.at[chunk, which], dp=core_peer)
+
+    def y_copy(chunk):
+        slot = chunk % 2
+        return copy(y_out.at[slot], y_in.at[chunk], y_send.at[slot], y_recv.at[chunk], dp=y_peer)
+
+    def x_copy(chunk):
+        slot = chunk % 2
+        return copy(x_out.at[slot], x_in.at[chunk], x_send.at[slot], x_recv.at[chunk], expert=partner_x)
+
+    def z_scatter(chunk, to, source):
+        slot = chunk % 2
+        return copy(
+            z_out.at[slot, pl.ds(pl.multiple_of(to * piece, 16), piece)], z_in.at[chunk, source],
+            zs_send.at[slot, to], zs_recv.at[chunk, source], expert=to * B + b,
+        )
+
+    def z_gather(chunk, to, source):
+        rows = pl.ds(pl.multiple_of(b * half_rows + source * piece, 16), piece)
+        return copy(full.at[chunk, rows], full.at[chunk, rows], zg_send.at[chunk, to], zg_recv.at[chunk, source], expert=to * B + b)
+
+    def x_gather(chunk, side):
+        rows = pl.ds(pl.multiple_of(side * half_rows, 16), half_rows)
+        return copy(full.at[chunk, rows], full.at[chunk, rows], xg_send.at[chunk], xg_recv.at[chunk], expert=partner_x)
+
+    def to_core(chunk):
+        for which, owner in ((0, core_peer), (1, 2 * (1 - y) + 1 - c)):
+            value = partial(chunk, owner).astype(jnp.bfloat16)
+
+            @pl.when(chunk >= 2)
+            def _():
+                core_copy(chunk, which).wait_send()
+
+            core_out[chunk % 2, which] = value
+            core_copy(chunk, which).start()
+
+    def to_y(chunk):
+        value = partial(chunk, y_peer)
+        core_copy(chunk, 1).wait_recv()
+
+        @pl.when(chunk >= 2)
+        def _():
+            y_copy(chunk).wait_send()
+
+        y_out[chunk % 2] = (value + core_in[chunk, 1].astype(jnp.float32)).astype(jnp.bfloat16)
+        y_copy(chunk).start()
+
+    def to_x(chunk):
+        value = partial(chunk, dp)
+        core_copy(chunk, 0).wait_recv()
+        y_copy(chunk).wait_recv()
+        value = value + core_in[chunk, 0].astype(jnp.float32) + y_in[chunk].astype(jnp.float32)
+
+        @pl.when(chunk >= 2)
+        def _():
+            x_copy(chunk).wait_send()
+
+        low, high = value[:half_rows], value[half_rows:]
+        half[chunk % 2] = jnp.where(b == 0, low, high)
+        x_out[chunk % 2] = jnp.where(b == 0, high, low).astype(jnp.bfloat16)
+        x_copy(chunk).start()
+
+    def to_z(chunk):
+        x_copy(chunk).wait_recv()
+
+        @pl.when(chunk >= 2)
+        def _():
+            for k in range(1, A):
+                z_scatter(chunk, (a + k) % A, a).wait_send()
+
+        total = half[chunk % 2] + x_in[chunk].astype(jnp.float32)
+        half[chunk % 2] = total
+        own[chunk % 2] = half[chunk % 2, pl.ds(pl.multiple_of(a * piece, 8), piece)]
+        z_out[chunk % 2] = total.astype(jnp.bfloat16)
+        for k in range(1, A):
+            z_scatter(chunk, (a + k) % A, a).start()
+
+    def spread_z(chunk):
+        total = own[chunk % 2]
+        for k in range(1, A):
+            source = (a + k) % A
+            z_scatter(chunk, a, source).wait_recv()
+            total = total + z_in[chunk, source].astype(jnp.float32)
+        rows = pl.ds(pl.multiple_of(b * half_rows + a * piece, 16), piece)
+        full[chunk, rows] = total.astype(jnp.bfloat16)
+        for k in range(1, A):
+            z_gather(chunk, (a + k) % A, a).start()
+
+    def spread_x(chunk):
+        for k in range(1, A):
+            z_gather(chunk, a, (a + k) % A).wait_recv()
+        x_gather(chunk, b).start()
+
+    def finish(chunk):
+        x_gather(chunk, 1 - b).wait_recv()
+        cols = pl.ds(pl.multiple_of(chunk * W, 128), W)
+        out[:, cols] = full[chunk].astype(jnp.float32)
+
+    stages = (to_core, to_y, to_x, to_z, spread_z, spread_x, finish)
+
+    def step(t, _):
+        for delay, stage in enumerate(stages):
+            @pl.when((t >= delay) & (t < delay + chunks))
+            def _():
+                stage(t - delay)
+
+        return 0
+
+    lax.fori_loop(0, chunks + len(stages) - 1, step, 0)
+
+    for chunk in range(chunks - 2, chunks):
+        core_copy(chunk, 0).wait_send()
+        core_copy(chunk, 1).wait_send()
+        y_copy(chunk).wait_send()
+        x_copy(chunk).wait_send()
+        for k in range(1, A):
+            z_scatter(chunk, (a + k) % A, a).wait_send()
+
+    def drain(chunk, _):
+        for k in range(1, A):
+            z_gather(chunk, (a + k) % A, a).wait_send()
+        x_gather(chunk, b).wait_send()
+        return 0
+
+    lax.fori_loop(0, chunks, drain, 0)
+
+
+def reduce_call(left, right, extra):
+    D = left.shape[2]
+    width = right.shape[1]
+    W, A, B = 384, 4, 2
+    shard, chunks = D // 4, width // W
+    bf, f32 = jnp.bfloat16, jnp.float32
+    vmem = pl.BlockSpec(memory_space=pltpu.VMEM)
+    dma = pltpu.SemaphoreType.DMA
+    piece = shard // (A * B)
+    return pl.pallas_call(
+        reduce_kernel,
+        out_shape=jax.ShapeDtypeStruct((shard, width), f32),
+        in_specs=[vmem] * 3,
+        out_specs=vmem,
+        scratch_shapes=[
+            pltpu.VMEM((2, 2, shard, W), bf),
+            pltpu.VMEM((chunks, 2, shard, W), bf),
+            pltpu.VMEM((2, shard, W), bf),
+            pltpu.VMEM((chunks, shard, W), bf),
+            pltpu.VMEM((2, shard // B, W), f32),
+            pltpu.VMEM((2, shard // B, W), bf),
+            pltpu.VMEM((chunks, shard // B, W), bf),
+            pltpu.VMEM((2, piece, W), f32),
+            pltpu.VMEM((2, shard // B, W), bf),
+            pltpu.VMEM((chunks, A, piece, W), bf),
+            pltpu.VMEM((chunks, shard, W), bf),
+            dma((2, 2)), dma((chunks, 2)), dma((2,)), dma((chunks,)), dma((2,)), dma((chunks,)),
+            dma((2, A)), dma((chunks, A)), dma((chunks, A)), dma((chunks, A)), dma((chunks,)), dma((chunks,)),
+        ],
+        compiler_params=pltpu.CompilerParams(
+            collective_id=2, has_side_effects=True, vmem_limit_bytes=56 * 1024 * 1024
+        ),
+        cost_estimate=pl.CostEstimate(flops=4 * 10**9, bytes_accessed=20 * 10**6, transcendentals=0),
+        name="weight_sums",
+    )(left, right, extra)
+
+
+def front_kernel(
+    lengths, tokens, routes, w_gain, w_small, w_q, w_k, w_v, w_o, u_in,
+    out_gain, out_small, out_q, out_k, out_v, out_o, u_all,
+    hidden_one, qkv, attended, log_total, cos_out, sin_out, residual, hidden_two, probs_out, by_owner,
+    all_gain, all_small, all_q, all_k, all_v, all_o, sums, q_heads, k_heads, v_heads, mixed,
+    keep_sem, core_send, y_send, pass_send, w_recv, u_keep, u_up, u_down, u_across, u_recv,
+):
+    A, B = 4, 2
+    R, D = tokens.shape
+    shard = D // 4
+    me = lax.axis_index("expert")
+    dp = lax.axis_index("dp")
+    a, b = me // B, me % B
+    y, c = dp // 2, dp % 2
+    partner_x = a * B + (1 - b)
+    core_peer = 2 * y + (1 - c)
+    y_peer = 2 * (1 - y) + c
+    far_peer = 2 * (1 - y) + 1 - c
+    shards = (w_gain, w_small, w_q, w_k, w_v, w_o)
+    landed = (all_gain, all_small, all_q, all_k, all_v, all_o)
+    kept = (out_gain, out_small, out_q, out_k, out_v, out_o)
+    count = len(shards)
+    GAIN, SMALL, QUERY, KEY, VALUE, OUTPUT = range(count)
+
+    def copy(src, dst, send, recv, **target):
+        return pltpu.make_async_remote_copy(
+            src_ref=src, dst_ref=dst, send_sem=send, recv_sem=recv, device_id=target, device_id_type=MESH
+        )
+
+    barrier = pltpu.get_barrier_semaphore()
+    for target in [{"dp": core_peer}, {"dp": y_peer}, {"expert": partner_x}] + [
+        {"expert": (a + k) % A * B + b} for k in range(1, A)
+    ]:
+        pl.semaphore_signal(barrier, inc=1, device_id=target, device_id_type=MESH)
+    pl.semaphore_wait(barrier, 2 + A)
+
+    def to_core(i):
+        return copy(shards[i], landed[i].at[dp], core_send.at[i], w_recv.at[i, dp], dp=core_peer)
+
+    def to_y(i):
+        return copy(shards[i], landed[i].at[dp], y_send.at[i], w_recv.at[i, dp], dp=y_peer)
+
+    def pass_on(i):
+        return copy(landed[i].at[y_peer], landed[i].at[y_peer], pass_send.at[i], w_recv.at[i, y_peer], dp=core_peer)
+
+    def keep_own(i):
+        return pltpu.make_async_copy(shards[i], kept[i].at[dp], keep_sem.at[i, dp])
+
+    def keep(i, owner):
+        return pltpu.make_async_copy(landed[i].at[owner], kept[i].at[owner], keep_sem.at[i, owner])
+
+    def receive(i, owner):
+        copy(shards[i], landed[i].at[owner], core_send.at[i], w_recv.at[i, owner], dp=core_peer).wait_recv()
+        keep(i, owner).start()
+
+    def forward(i):
+        receive(i, y_peer)
+        pass_on(i).start()
+
+    def u_send_up(src, s):
+        return copy(src, u_all.at[s], u_up.at[s], u_recv.at[s], expert=me + B)
+
+    def u_send_down(src, s):
+        return copy(src, u_all.at[s], u_down.at[s], u_recv.at[s], expert=me - B)
+
+    def u_send_across(src, s):
+        return copy(src, u_all.at[s], u_across.at[s], u_recv.at[s], expert=partner_x)
+
+    def take(row):
+        @pl.when((row >= 0) & (row < A))
+        def _():
+            s = row * B + b
+            u_send_across(u_all.at[s], s).wait_recv()
+            u_send_across(u_all.at[s], s).start()
+
+            @pl.when((row < a) & (a < A - 1))
+            def _():
+                u_send_up(u_all.at[s], s).start()
+
+            @pl.when((row > a) & (a > 0))
+            def _():
+                u_send_down(u_all.at[s], s).start()
+
+    keep_u = pltpu.make_async_copy(u_in, u_all.at[me], u_keep)
+
+    @pl.when(a < A - 1)
+    def _():
+        u_send_up(u_in, me).start()
+
+    @pl.when(a > 0)
+    def _():
+        u_send_down(u_in, me).start()
+
+    u_send_across(u_in, me).start()
+    for i in range(count):
+        to_y(i).start()
+        to_core(i).start()
+        keep_own(i).start()
+    keep_u.start()
+
+    row_index = lax.broadcasted_iota(jnp.int32, (R, 128), 0)
+    ends = (lengths[0, 0], lengths[0, 0] + lengths[0, 1], lengths[0, 0] + lengths[0, 1] + lengths[0, 2])
+    start = jnp.where(row_index >= ends[2], ends[2], jnp.where(row_index >= ends[1], ends[1], jnp.where(row_index >= ends[0], ends[0], 0)))
+    position = (row_index - start).astype(jnp.float32)
+    lane = lax.broadcasted_iota(jnp.int32, (R, 128), 1)
+    pair = (lane % (HD // 2)).astype(jnp.float32)
+    frequency = jnp.exp(pair * (-2.0 / HD * math.log(rope_base)))
+    angle = position * frequency
+    front = lane % HD < HD // 2
+    cos_out[...] = jnp.cos(angle)
+    sin_out[...] = jnp.where(front, -jnp.sin(angle), jnp.sin(angle))
+
+    def doc_of(index):
+        total = 0
+        for end in ends:
+            total = total + jnp.where(index >= end, 1, 0)
+        return total
+
+    rows_t = lax.broadcasted_iota(jnp.int32, (R, R), 0)
+    rows_u = lax.broadcasted_iota(jnp.int32, (R, R), 1)
+    allowed = (doc_of(rows_t) == doc_of(rows_u)) & (rows_u <= rows_t)
+
+    inputs = tokens[...].astype(jnp.float32)
+    scale_one = lax.rsqrt(jnp.mean(inputs * inputs, axis=1, keepdims=True) + eps)
+
+    forward(GAIN)
+    receive(GAIN, core_peer)
+    receive(GAIN, far_peer)
+    all_gain[dp] = w_gain[...]
+    for j in range(4):
+        cols = slice(j * shard, (j + 1) * shard)
+        gain = all_gain[j, 0:1, :].astype(jnp.float32)
+        hidden_one[:, cols] = (inputs[:, cols] * scale_one * gain).astype(jnp.bfloat16)
+
+    offsets = {QUERY: 0, KEY: D, VALUE: D + KVH * HD}
+    sums[...] = jnp.zeros_like(sums)
+
+    def product(i, owner, own=False):
+        cols = pl.ds(pl.multiple_of(owner * shard, 128), shard)
+        left = hidden_one[:, cols]
+        width = shards[i].shape[1]
+
+        def tile(t, _):
+            into = pl.ds(pl.multiple_of(offsets[i] + t * 512, 128), 512)
+            part = pl.ds(pl.multiple_of(t * 512, 128), 512)
+            weight = shards[i][:, part] if own else landed[i][owner, :, part]
+            sums[:, into] += dot_f32(left, weight)
+            return 0
+
+        lax.fori_loop(0, width // 512, tile, 0)
+
+    for i in (QUERY, KEY, VALUE):
+        product(i, dp, own=True)
+    for i in (QUERY, KEY, VALUE):
+        receive(i, core_peer)
+        product(i, core_peer)
+    take(a - 1)
+    take(a + 1)
+    forward(SMALL)
+    receive(SMALL, core_peer)
+    forward(QUERY)
+    product(QUERY, y_peer)
+    receive(QUERY, far_peer)
+    product(QUERY, far_peer)
+    take(a - 2)
+    take(a + 2)
+    forward(KEY)
+    product(KEY, y_peer)
+    receive(KEY, far_peer)
+    product(KEY, far_peer)
+    forward(VALUE)
+    product(VALUE, y_peer)
+    receive(VALUE, far_peer)
+    product(VALUE, far_peer)
+
+    def rotated(columns):
+        value = sums[:, columns]
+        other = jnp.where(front, pltpu.roll(value, 128 - HD // 2, 1), pltpu.roll(value, HD // 2, 1))
+        return (value * cos_out[...] + other * sin_out[...]).astype(jnp.bfloat16)
+
+    for pair_index in range(QH // 2):
+        columns = slice(pair_index * 128, (pair_index + 1) * 128)
+        value = rotated(columns)
+        qkv[:, columns] = value
+        q_heads[2 * pair_index] = value[:, :HD]
+        q_heads[2 * pair_index + 1] = value[:, HD:]
+    for pair_index in range(KVH // 2):
+        columns = slice(D + pair_index * 128, D + (pair_index + 1) * 128)
+        value = rotated(columns)
+        qkv[:, columns] = value
+        k_heads[2 * pair_index] = value[:, :HD]
+        k_heads[2 * pair_index + 1] = value[:, HD:]
+        columns = slice(D + KVH * HD + pair_index * 128, D + KVH * HD + (pair_index + 1) * 128)
+        value = sums[:, columns].astype(jnp.bfloat16)
+        qkv[:, columns] = value
+        v_heads[2 * pair_index] = value[:, :HD]
+        v_heads[2 * pair_index + 1] = value[:, HD:]
+    log_total[...] = jnp.zeros_like(log_total)
+
+    def group_step(g, _):
+        for k in range(QH // KVH):
+            head = g * (QH // KVH) + k
+            scores = dot_f32(q_heads[head], k_heads[g], NT) * HD**-0.5
+            scores = jnp.where(allowed, scores, masked_score)
+            top = jnp.max(scores, axis=1, keepdims=True)
+            terms = jnp.exp(scores - top)
+            total = jnp.sum(terms, axis=1, keepdims=True)
+            low = (terms / total).astype(jnp.bfloat16)
+            mixed[head] = dot_f32(low, v_heads[g]).astype(jnp.bfloat16)
+            log_total[...] += jnp.where(lane == head, top + jnp.log(total), 0.0)
+        return 0
+
+    lax.fori_loop(0, KVH, group_step, 0)
+    take(a - 3)
+    take(a + 3)
+    for pair_index in range(QH // 2):
+        attended[:, pair_index * 128 : (pair_index + 1) * 128] = jnp.concatenate(
+            [mixed[2 * pair_index], mixed[2 * pair_index + 1]], axis=1
+        )
+
+    residual[...] = inputs
+
+    def out_product(owner, own=False):
+        cols = pl.ds(pl.multiple_of(owner * shard, 128), shard)
+        left = attended[:, cols]
+
+        def tile(t, _):
+            part = pl.ds(pl.multiple_of(t * 512, 128), 512)
+            weight = w_o[:, part] if own else all_o[owner, :, part]
+            residual[:, part] += dot_f32(left, weight)
+            return 0
+
+        lax.fori_loop(0, D // 512, tile, 0)
+
+    out_product(dp, own=True)
+    receive(OUTPUT, core_peer)
+    out_product(core_peer)
+    receive(SMALL, far_peer)
+    all_small[dp] = w_small[...]
+    forward(OUTPUT)
+    out_product(y_peer)
+    receive(OUTPUT, far_peer)
+    out_product(far_peer)
+
+    whole = residual[...]
+    scale_two = lax.rsqrt(jnp.mean(whole * whole, axis=1, keepdims=True) + eps)
+    logits = jnp.zeros((R, 128), jnp.float32)
+    for j in range(4):
+        cols = slice(j * shard, (j + 1) * shard)
+        gain = all_gain[j, 1:2, :].astype(jnp.float32)
+        value = (whole[:, cols] * scale_two * gain).astype(jnp.bfloat16)
+        hidden_two[:, cols] = value
+        logits = logits + dot_f32(value, all_small[j])
+    chosen = lane == routes[:, 0:1]
+    for j in range(1, TOP):
+        chosen = chosen | (lane == routes[:, j : j + 1])
+    logits = jnp.where(chosen, logits, masked_score)
+    terms = jnp.where(chosen, jnp.exp(logits - jnp.max(logits, axis=1, keepdims=True)), 0.0)
+    probs = terms / jnp.sum(terms, axis=1, keepdims=True)
+    probs_out[...] = probs
+    turned = jnp.transpose(probs)
+    by_owner[...] = jnp.zeros_like(by_owner)
+    local = 2
+    for owner in range(A * B):
+        by_owner[owner, 0:local, :] = turned[owner * local : (owner + 1) * local]
+
+    for row in range(A):
+        s = row * B + 1 - b
+        u_send_across(u_all.at[s], s).wait_recv()
+    for i in range(count):
+        keep_own(i).wait()
+        for owner in (core_peer, y_peer, far_peer):
+            keep(i, owner).wait()
+        to_y(i).wait_send()
+        to_core(i).wait_send()
+        pass_on(i).wait_send()
+    keep_u.wait()
+
+    @pl.when(a < A - 1)
+    def _():
+        u_send_up(u_in, me).wait_send()
+
+    @pl.when(a > 0)
+    def _():
+        u_send_down(u_in, me).wait_send()
+
+    for row in range(A):
+        s = row * B + b
+        u_send_across(u_all.at[s], s).wait_send()
+
+        @pl.when((row < a) & (a < A - 1))
+        def _():
+            u_send_up(u_all.at[s], s).wait_send()
+
+        @pl.when((row > a) & (a > 0))
+        def _():
+            u_send_down(u_all.at[s], s).wait_send()
+
+
+def front_call(seq_lengths, tokens, routes, gains, small, w_query, w_key, w_value, w_output, out_grad):
+    n = 8
+    R, D = tokens.shape
+    bf, f32 = jnp.bfloat16, jnp.float32
+    any_spec = pl.BlockSpec(memory_space=pl.ANY)
+    vmem = pl.BlockSpec(memory_space=pltpu.VMEM)
+    dma = pltpu.SemaphoreType.DMA
+    shards = (gains, small, w_query, w_key, w_value, w_output)
+    whole = w_query.shape[1] + w_key.shape[1] + w_value.shape[1]
+    return pl.pallas_call(
+        front_kernel,
+        out_shape=tuple(jax.ShapeDtypeStruct((4, *w.shape), bf) for w in shards)
+        + (
+            jax.ShapeDtypeStruct((n, R, D), bf),
+            jax.ShapeDtypeStruct((R, D), bf),
+            jax.ShapeDtypeStruct((R, whole), bf),
+            jax.ShapeDtypeStruct((R, D), bf),
+            jax.ShapeDtypeStruct((R, 128), f32),
+            jax.ShapeDtypeStruct((R, 128), f32),
+            jax.ShapeDtypeStruct((R, 128), f32),
+            jax.ShapeDtypeStruct((R, D), f32),
+            jax.ShapeDtypeStruct((R, D), bf),
+            jax.ShapeDtypeStruct((R, 128), f32),
+            jax.ShapeDtypeStruct((n, 8, R), f32),
+        ),
+        in_specs=[pl.BlockSpec(memory_space=pltpu.SMEM)] + [vmem] * 9,
+        out_specs=(any_spec,) * 7 + (vmem,) * 10,
+        scratch_shapes=[pltpu.VMEM((4, *w.shape), bf) for w in shards]
+        + [
+            pltpu.VMEM((R, whole), f32),
+            pltpu.VMEM((QH, R, HD), bf),
+            pltpu.VMEM((KVH, R, HD), bf),
+            pltpu.VMEM((KVH, R, HD), bf),
+            pltpu.VMEM((QH, R, HD), bf),
+            dma((6, 4)), dma((6,)), dma((6,)), dma((6,)), dma((6, 4)), dma, dma((n,)), dma((n,)), dma((n,)), dma((n,)),
+        ],
+        compiler_params=pltpu.CompilerParams(
+            collective_id=3, has_side_effects=True, vmem_limit_bytes=60 * 1024 * 1024
+        ),
+        cost_estimate=pl.CostEstimate(flops=4 * 10**9, bytes_accessed=40 * 10**6, transcendentals=2 * 10**6),
+        name="front",
+    )(seq_lengths, tokens, routes, *shards, out_grad)
+
+
+def fused_body(
+    tokens,
+    seq_lengths,
+    routes,
+    w_query,
+    w_key,
+    w_value,
+    w_output,
+    w_router,
+    attn_gain,
+    moe_gain,
+    expert_gate,
+    expert_up,
+    expert_down,
+    out_grad,
+):
+    row_count, width = tokens.shape
+    expert_count = w_router.shape[1]
+    local_count = expert_gate.shape[0]
+    group_size = QH // KVH
+    score_scale = HD ** (-0.5)
+    gains = jnp.pad(jnp.stack([attn_gain, moe_gain]), ((0, 14), (0, 0)))
+    small = jnp.pad(w_router, ((0, 0), (0, 128 - expert_count)))
+    (
+        gains, small, query_w, key_w, value_w, output_w, all_upstream,
+        hidden_one, qkv, attended, log_total, cos_table, sin_table, residual, hidden_two, probs, by_owner,
+    ) = front_call(seq_lengths, tokens, routes, gains, small, w_query, w_key, w_value, w_output, out_grad)
+    query_w, key_w, value_w, output_w = [w.reshape(-1, w.shape[2]) for w in (query_w, key_w, value_w, output_w)]
+    gain_one, gain_two = gains[:, 0].reshape(-1), gains[:, 1].reshape(-1)
+    router_w = small.reshape(width, -1)
+
+    mix_part, row_sum, grad_rows, own_grads, _, far_grads = moe_call(
+        hidden_two, all_upstream, by_owner, expert_gate, expert_up, expert_down
+    )
+    far_grads = lax.ppermute(far_grads, "dp", [(0, 2), (1, 3), (2, 0), (3, 1)])
+    mixture = lax.psum_scatter(mix_part.reshape(-1, width), "expert", scatter_dimension=0, tiled=True)
+
+    inputs = tokens.astype(jnp.float32)
+    upstream = out_grad.astype(jnp.float32)
+    scale_one = rms_scale(inputs)
+    normed_one = inputs * scale_one
+    scale_two = rms_scale(residual)
+    normed_two = residual * scale_two
+    grad_dense = grad_rows[:, :local_count].reshape(expert_count, row_count).T
+    dense = probs[:, :expert_count]
+    logit_grad = (dense * (grad_dense - jnp.sum(dense * grad_dense, axis=-1, keepdims=True))).astype(jnp.bfloat16)
+    logit_grad = jnp.pad(logit_grad, ((0, 0), (0, 128 - expert_count)))
+    hidden_two_grad = row_sum + jnp.dot(logit_grad, router_w.T, preferred_element_type=jnp.float32)
+    gain_two_partial = jnp.sum(hidden_two_grad * normed_two, axis=0)
+    normed_two_grad = hidden_two_grad * gain_two.astype(jnp.float32)
+    residual_grad = upstream + scale_two * (
+        normed_two_grad - normed_two * jnp.mean(normed_two_grad * normed_two, axis=-1, keepdims=True)
+    )
+    branch_grad = residual_grad.astype(jnp.bfloat16)
+    attended_grad = jnp.dot(branch_grad, output_w.T, preferred_element_type=jnp.float32).astype(jnp.bfloat16)
+
+    doc_id, _ = token_layout(seq_lengths[0], row_count)
+    token_index = jnp.arange(row_count, dtype=jnp.int32)
+    allowed = (doc_id[:, None] == doc_id[None, :]) & (token_index[None, :] <= token_index[:, None])
+    query_heads = qkv[:, : QH * HD].reshape(row_count, KVH, group_size, HD)
+    key_heads = qkv[:, QH * HD : (QH + KVH) * HD].reshape(row_count, KVH, HD)
+    value_heads = qkv[:, (QH + KVH) * HD :].reshape(row_count, KVH, HD)
+    scores = jnp.einsum("tkgd,ukd->kgtu", query_heads, key_heads, preferred_element_type=jnp.float32) * score_scale
+    scores = jnp.where(allowed, scores, masked_score)
+    log_heads = log_total[:, :QH].T.reshape(KVH, group_size, row_count, 1)
+    attn_probs = jnp.exp(scores - log_heads)
+    probs_low = attn_probs.astype(jnp.bfloat16)
+    grad_heads = attended_grad.reshape(row_count, KVH, group_size, HD)
+    prob_grad = jnp.einsum("tkgd,ukd->kgtu", grad_heads, value_heads, preferred_element_type=jnp.float32)
+    score_grad = (
+        attn_probs * (prob_grad - jnp.sum(attn_probs * prob_grad, axis=-1, keepdims=True))
+    ).astype(jnp.bfloat16)
+    query_sums = (
+        jnp.einsum("kgtu,ukd->tkgd", score_grad, key_heads, preferred_element_type=jnp.float32) * score_scale
+    )
+    key_sums = (
+        jnp.einsum("kgtu,tkgd->ukd", score_grad, query_heads, preferred_element_type=jnp.float32) * score_scale
+    )
+    value_sums = jnp.einsum("kgtu,tkgd->ukd", probs_low, grad_heads, preferred_element_type=jnp.float32)
+    half_size = HD // 2
+    cosines, sines = cos_table[:, None, :half_size], sin_table[:, None, half_size:HD]
+    query_grad = unrotate(query_sums.reshape(row_count, QH * HD), cosines, sines, QH).astype(jnp.bfloat16)
+    key_grad = unrotate(key_sums.reshape(row_count, KVH * HD), cosines, sines, KVH).astype(jnp.bfloat16)
+    value_grad = value_sums.reshape(row_count, KVH * HD).astype(jnp.bfloat16)
+    hidden_one_grad = jnp.dot(query_grad, query_w.T, preferred_element_type=jnp.float32)
+    hidden_one_grad = hidden_one_grad + jnp.dot(key_grad, key_w.T, preferred_element_type=jnp.float32)
+    hidden_one_grad = hidden_one_grad + jnp.dot(value_grad, value_w.T, preferred_element_type=jnp.float32)
+    gain_one_partial = jnp.sum(hidden_one_grad * normed_one, axis=0)
+    normed_one_grad = hidden_one_grad * gain_one.astype(jnp.float32)
+    in_grad = residual_grad + scale_one * (
+        normed_one_grad - normed_one * jnp.mean(normed_one_grad * normed_one, axis=-1, keepdims=True)
+    )
+    router_partial = jnp.dot(hidden_two.T, logit_grad, preferred_element_type=jnp.float32)
+    column = jnp.arange(128, dtype=jnp.int32)[None, :]
+    extra = jnp.where(
+        column == expert_count,
+        gain_one_partial[:, None],
+        jnp.where(column == expert_count + 1, gain_two_partial[:, None], router_partial),
+    ).astype(jnp.bfloat16)
+    zero_columns = jnp.zeros((row_count, 128), jnp.bfloat16)
+    sums = reduce_call(
+        jnp.stack([attended, hidden_one]),
+        jnp.concatenate([branch_grad, query_grad, key_grad, value_grad, zero_columns], axis=1),
+        extra,
+    )
+    wide, narrow = QH * HD, KVH * HD
+    cuts = (0, wide, 2 * wide, 2 * wide + narrow, 2 * wide + 2 * narrow)
+    of_output, of_query, of_key, of_value = [sums[:, i:j] for i, j in zip(cuts, cuts[1:])]
+    tail = sums[:, cuts[-1] :]
+    far_grads, residual, _ = lax.optimization_barrier((far_grads, residual, of_query))
+    expert_grads = own_grads + far_grads.astype(jnp.float32)
+    layer_out = (residual + mixture.astype(jnp.float32)).astype(jnp.bfloat16)
+    return (
+        layer_out,
+        in_grad,
+        of_query,
+        of_key,
+        of_value,
+        of_output,
+        tail[:, :expert_count],
+        tail[:, expert_count],
+        tail[:, expert_count + 1],
+        *[expert_grads[2 * kind : 2 * kind + 2] for kind in range(3)],
+    )
+
+
+def fits_fused(mesh, tokens_shape):
+    devices = mesh.shape["dp"] * mesh.shape["expert"]
+    return mesh.shape["dp"] == 4 and mesh.shape["expert"] == 8 and tokens_shape[0] == 256 * devices
+
+
 def solution(mesh):
     placed = (
         P(("dp", "expert"), None),
@@ -357,23 +1553,29 @@
         P("expert", None, None),
         P(("dp", "expert"), None),
     )
-    return jax.shard_map(
-        body,
-        mesh=mesh,
-        in_specs=placed,
-        out_specs=(
-            P(("dp", "expert"), None),
-            P(("dp", "expert"), None),
-            P("dp", None),
-            P("dp", None),
-            P("dp", None),
-            P("dp", None),
-            P("dp", None),
-            P("dp"),
-            P("dp"),
-            P("expert", "dp", None),
-            P("expert", "dp", None),
-            P("expert", "dp", None),
-        ),
-        check_vma=False,
-    )
+    def layer(tokens, *rest):
+        return shard(fused_body if fits_fused(mesh, tokens.shape) else body)(tokens, *rest)
+
+    def shard(step):
+        return jax.shard_map(
+            step,
+            mesh=mesh,
+            in_specs=placed,
+            out_specs=(
+                P(("dp", "expert"), None),
+                P(("dp", "expert"), None),
+                P("dp", None),
+                P("dp", None),
+                P("dp", None),
+                P("dp", None),
+                P("dp", None),
+                P("dp"),
+                P("dp"),
+                P("expert", "dp", None),
+                P("expert", "dp", None),
+                P("expert", "dp", None),
+            ),
+            check_vma=False,
+        )
+
+    return layer

time: 1180 us -> 481 us (0.41)
  waiting for transfers between devices: 773 us -> 0.02 us
  Pallas kernels: 0 us -> 390 us
  matrix products: 200 us -> 23.2 us
  blocking collectives: 92.9 us -> 0 us
  other arithmetic: 47.1 us -> 16.1 us
    pallas_call x0 -> x3, Pallas kernels: none -> 390 us  [the longest x1 164 us: moe_call(): pl.pallas_call(functools.partial(moe_kernel, comm=True), out_shape=out_sh...]
    reduce_scatter x8 -> x1, waiting for transfers between devices: 354 us -> 0.01 us  [fused_body(): lax.psum_scatter(mix_part.reshape(-1, width), 'expert', scatter_dimension...]
    all_gather x6 -> x0, waiting for transfers between devices: 273 us -> none  [the longest x1 93.1 us: body(): all_hidden = lax.all_gather(hidden_two, 'expert', axis=0, tiled=True)]
    dot_general x39 -> x11, matrix products: 200 us -> 23.2 us  [the longest x1 4.46 us: fused_body(): jnp.einsum('kgtu,tkgd->ukd', probs_low, grad_heads, preferred_element_typ...]
    psum x1 -> x0, waiting for transfers between devices: 74.8 us -> none  [body(): lax.psum(pieces[0].astype(jnp.bfloat16), 'expert').astype(jnp.float32)]
    unnamed x19 -> x1, waiting for transfers between devices: 65.4 us -> 0.02 us
    all_gather x4 -> x0, blocking collectives: 47.5 us -> none  [the longest x1 30.5 us: body(): lax.all_gather(dense_probs, 'expert', axis=0, tiled=True)]
    psum x1 -> x0, blocking collectives: 39.3 us -> none  [body(): lax.psum(pieces[4].astype(jnp.bfloat16), 'expert').astype(jnp.float32)]
  transfers between devices with their start and end apart: 18 -> 2, of which waited for: 16 -> 0; matrix products, arithmetic and copies ran while one was open for 14% -> 13% of each run, Pallas kernels for 0% -> 29%
where the time goes in v4:
time: 481 us; the launch traced here: 480 us
  Pallas kernels  390 us (81%)
  local copies, waits for them, and re-layouts  35.3 us (7%)
  matrix products  23.2 us (5%)
  other arithmetic  16.1 us (3%)
  between operations  14.5 us (3%)
    pallas_call x1, Pallas kernels, moe_call(): pl.pallas_call(functools.partial(moe_kernel, comm=True), out_shape=out_sh...  164 us
    pallas_call x1, Pallas kernels, reduce_call(): pl.pallas_call(reduce_kernel, out_shape=jax.ShapeDtypeStruct((shard, widt...  137 us
    pallas_call x1, Pallas kernels, front_call(): pl.pallas_call(front_kernel, out_shape=tuple((jax.ShapeDtypeStruct((4, *w...  88.9 us
    unnamed x76, local copies, waits for them, and re-layouts  11 us
  transfers between devices with their start and end apart: 2, of which 0 were waited for; matrix products, arithmetic and copies ran while one was open for 13% of the time, Pallas kernels for 29%

profile of v4, /device:TPU:0, one launch (start us, length us, event | category | flops | bytes accessed | tf_op | source)
XLA Modules:
  0.0 479.8 jit_solution(13964580289980956498)
XLA Ops:
  7.2 1.5 copy.67.routes
  12.2 88.9 %front.1 = (bf16[4,16,384]{2,1,0:T(8,128)(2,1)}, bf16[4,384,128]{2,1,0:T(8,128)(2,1)}, bf16[4,384,1536]{2,1,0:T(8,128)(2,1)}, bf16[4,384,512]{2,1,0:T(8,128)(2,1...) custom-call(s32[1,4]{1,0:T(1,128)} %lengths.1, ...), custom_call_target="tpu_custom_call" | custom-call | flops 4000000000 | bytes 40000000 | tf_op jit(solution)/shard_map/front/pallas_call | solution.py:1373
  101.1 164.1 %experts.1 = (bf16[8,256,1536]{2,1,0:T(8,128)(2,1)}, f32[256,1536]{1,0:T(8,128)}, f32[8,8,256]{2,1,0:T(8,128)}, f32[6,384,512]{2,1,0:T(8,128)}, bf16[2,6,384,512...) custom-call(bf16[256,1536]{1,0:T(8,128)(2,1)} %get-tuple-element.36.h_in, bf16[8,256,1536]{2,1,0:T(8,128)(2,1)} %get-tuple-element.37.u_in, ...), custom_call_target="tpu_custom_call" | custom-call | flops 57999998976 | bytes 60000000 | tf_op jit(solution)/shard_map/experts/pallas_call | solution.py:825
  265.8 1.3 copy-done.16
  272.0 1.3 copy.71
  277.7 1.4 convert_dynamic-update-slice_fusion
  280.2 3.7 convolution_convert_fusion
  287.2 1.9 fusion
  289.8 1.9 fusion.2
  293.7 2.3 copy.81
  296.0 2.2 fusion.21
  299.4 4.5 fusion.25
  306.9 3.9 fusion.47
  312.2 2.1 fusion.15
  314.3 1.4 fusion.10.extra
  315.8 1.3 pad_maximum_fusion.left
  317.7 136.9 %weight_sums.1 = f32[384,4224]{1,0:T(8,128)} custom-call(bf16[2,256,1536]{2,1,0:T(8,128)(2,1)} %pad_maximum_fusion.left, bf16[256,4224]{1,0:T(8,128)(2,1)} %broadcast_dynamic-update-slice_fusion.right, bf16[1536,128]{1,0:T(8,128)(2,1)} %fusion.10.extra), custom_call_target="tpu_custom_call" | custom-call | flops 4000000000 | bytes 20000000 | tf_op jit(solution)/shard_map/weight_sums/pallas_call | solution.py:1037
  456.4 2.0 slice_reduce_fusion
  458.5 2.8 fusion.43
  461.3 1.6 fusion.18
  462.9 2.8 fusion.42
  465.7 2.7 convert_add_fusion
  468.5 2.3 fusion.44
  470.8 2.2 add_convert_fusion
  (125 shorter events, 28.1 us)
Async XLA Ops:
  7.2 463.6 %reduce-scatter.2.cloned.1.call-start = ((), (), s32[]{:S(2)}) async-start(), calls=%async_computation.1 | async-start | bytes 7077888 | tf_op jit(solution)/shard_map/reduce_scatter | solution.py:1443
  265.2 200.4 %collective-permute-start = (bf16[6,384,512]{2,1,0:T(8,128)(2,1)}, bf16[6,384,512]{2,1,0:T(8,128)(2,1)}, u32[]{:S(2)}, u32[]{:S(2)}) collective-permute-start(bf16[6,384,512]{2,1,0:T(8,128)(2,1)} %get-tuple-element.39), channel_id=1, source_target_pairs={{0,16},{8,24},{16,0},{24,8},{1,17},{9,25},{17,1},{25,9},{2,18},{10... | collective-permute-start | bytes 7077896 | tf_op jit(solution)/shard_map/ppermute | solution.py:1442
  265.8 2.1 copy-start.29
  270.5 5.7 %copy-start.1 = (f32[256,1536]{1,0:T(8,128)S(1)}, f32[256,1536]{1,0:T(8,128)}, u32[]{:S(2)}) copy-start(f32[256,1536]{1,0:T(8,128)} %get-tuple-element.56) | copy-start | bytes 4718596
  272.0 14.2 %copy-start.5 = (bf16[256,1536]{0,1:T(8,128)(2,1)}, bf16[256,1536]{0,1:T(8,128)(2,1)S(1)}, u32[]{:S(2)}) copy-start(bf16[256,1536]{0,1:T(8,128)(2,1)S(1)} %copy.70) | copy-start | bytes 2359300
  272.0 4.4 copy-start.20
  272.0 4.5 copy-start.21
  284.0 1.8 copy-start.31
  284.3 2.9 copy-start.11
  287.2 2.7 copy-start
  296.0 2.2 copy-start.24
  299.4 4.7 copy-start.10
  303.8 2.6 copy-start.4
  304.0 2.9 copy-start.9
  306.9 3.9 copy-start.13
  312.2 2.1 copy-start.26
  312.2 2.1 copy-start.30
  312.2 2.1 copy-start.32
  454.6 6.6 %copy-start.7 = (f32[256,1536]{1,0:T(8,128)S(1)}, f32[256,1536]{1,0:T(8,128)}, u32[]{:S(2)}) copy-start(f32[256,1536]{1,0:T(8,128)} %copy-done.6) | copy-start | bytes 4718596
  456.4 4.8 %copy-start.8 = (f32[256,1536]{1,0:T(8,128)S(1)}, f32[256,1536]{1,0:T(8,128)}, u32[]{:S(2)}) copy-start(f32[256,1536]{1,0:T(8,128)} %get-tuple-element.122) | copy-start | bytes 4718596
  458.5 4.4 copy-start.3
  461.3 4.4 slice-start
  462.8 2.8 slice-start.1
  468.5 2.3 copy-start.2
  (13 other events, 15.7 us)
Sparse Core Ops, SparseCore 0:
  265.9 152.2 reduce-scatter.1

commit v5 on v4

--- a/solution.py
+++ b/solution.py
@@ -364,43 +364,20 @@
     return value
 
 
-BLOCK_ORDER = (
-    (0, 4, 1, 2, 5, 3, 7, 6),
-    (1, 5, 0, 2, 4, 3, 7, 6),
-    (2, 6, 3, 1, 7, 0, 4, 5),
-    (3, 7, 2, 1, 6, 0, 4, 5),
+BLOCK_ORDER = ((0, 1, 4, 5, 6, 2, 7, 3), (1, 0, 5, 4, 6, 2, 7, 3))
+BEFORE_STEP = (
+    ((), ("W1", "X1", "W4", "A4"), (), ("W5",), ("W6",), ("W2",), ("W7",), ("W3",)),
+    ((), ("W2", "N2", "W5", "A5", "W0"), (), ("W4", "A4", "W6", "N6", "A0"), (), ("W7", "N7"), (), ("W3", "N3")),
 )
-TAKE_FIRST = (
-    (15, 1, 15, 2, 5, 3, 7, 6),
-    (15, 0, 15, 3, 15, 7, 15, 6),
-    (15, 3, 15, 0, 15, 4, 15, 5),
-    (15, 2, 15, 1, 6, 0, 4, 5),
-)
-TAKE_SECOND = (
-    (15, 4, 15, 15, 15, 15, 15, 15),
-    (15, 2, 15, 4, 15, 15, 15, 15),
-    (15, 1, 15, 7, 15, 15, 15, 15),
-    (15, 7, 15, 15, 15, 15, 15, 15),
-)
-TAKE_THIRD = (
-    (15, 15, 15, 15, 15, 15, 15, 15),
-    (15, 5, 15, 15, 15, 15, 15, 15),
-    (15, 6, 15, 15, 15, 15, 15, 15),
-    (15, 15, 15, 15, 15, 15, 15, 15),
-)
-SUM_ORDER = (
-    (3, 2, 7, 7, 0),
-    (7, 3, 0, 2, 1),
-    (7, 0, 3, 1, 2),
-    (0, 1, 7, 7, 3),
-)
+SUMS_ACROSS = (((), (), (), (), (2,), (), (3, 1, 0), ()), ((), (), (), (0,), (2,), (), (3, 1), ()))
+SUM_ORDER = ((3, 15, 15, 15, 1, 15, 15, 15, 0), (15, 15, 15, 2, 15, 3, 0, 15, 1))
 HALVES = 2
 
 
 def moe_kernel(
     h_in, u_in, p_in, wg_in, wu_in, wd_in,
     d_out, e_out, gg_out, grads_out, core_got, y_out,
-    h_all, u_all, p_all, wg, wu, wd, act, gu, ex, ez, rx, rz, d_stage, gg_stage, tile_bf, tile_f32, got_tile,
+    h_all, u_all, p_all, wg, wu, wd, act, gu, partials, rx, rz, d_stage, gg_stage, tile_bf, tile_f32, got_tile,
     load_sem, h_up, h_down, h_across, h_recv, p_send, p_recv, g_send, g_recv,
     x_send, x_recv, z_send, z_recv, d_sem, c_send, c_recv, y_send, tile_sem, out_sem,
     *, comm
@@ -409,6 +386,7 @@
     R, D = h_in.shape
     F = wg.shape[2]
     shard = D // 4
+    ez, ex = partials.at[pl.ds(0, A)], partials.at[pl.ds(A, A)]
     me = lax.axis_index("expert")
     dp = lax.axis_index("dp")
     a, b = me // B, me % B
@@ -473,54 +451,31 @@
     def recv_block(s):
         send_across(s).wait_recv()
 
-    def pass_along(row, s):
-        @pl.when((row <= a) & (a < A - 1))
+    near = jnp.where(a < A // 2, a, A - 1 - a)
+    flipped = a >= A // 2
+
+    def turned(row):
+        return jnp.where(flipped, A - 1 - row, row)
+
+    def along(s, upward):
+        @pl.when(flipped != upward)
         def _():
             send_up(s).start()
 
-        @pl.when((row >= a) & (a > 0))
+        @pl.when(flipped == upward)
         def _():
             send_down(s).start()
 
-    def take(code):
-        @pl.when(code < n)
-        def _():
-            across = code >= A
-            row = code % A
-            s = row * B + jnp.where(across, 1 - b, b)
-            recv_block(s)
-
-            @pl.when(jnp.logical_not(across))
-            def _():
-                pass_along(row, s)
-
-                @pl.when(((a == 0) & (row == 1)) | ((a == A - 1) & (row == A - 2)))
-                def _():
-                    send_across(s).start()
-
-            @pl.when(across & ((row == 0) | (row == A - 1)))
-            def _():
-                pass_along(row, s)
-
-                @pl.when((a > 0) & (a < A - 1) & ((row == 0) == (a == 1)))
-                def _():
-                    near = a * B + 1 - b
-
-                    @pl.when(a == 1)
-                    def _():
-                        send_up(near).start()
-
-                    @pl.when(a == A - 2)
-                    def _():
-                        send_down(near).start()
-
-            @pl.when(across & (row == 1) & (a == 2))
-            def _():
-                send_up(s).start()
-
-            @pl.when(across & (row == 2) & (a == 1))
-            def _():
-                send_down(s).start()
+    def move(words):
+        for word in words:
+            code = int(word[1:])
+            s = turned(code % A) * B + (1 - b if code >= A else b)
+            if word[0] == "W":
+                recv_block(s)
+            elif word[0] == "X":
+                send_across(s).start()
+            else:
+                along(s, word[0] == "A")
 
     def d_copy(s, slot):
         return pltpu.make_async_copy(d_stage.at[slot], d_out.at[s], d_sem.at[slot])
@@ -564,17 +519,10 @@
             back += dot_f32(gu[rows, 2 * F : 3 * F], wg[1, cols, :], NT)
             back += dot_f32(gu[rows, 3 * F : 4 * F], wu[1, cols, :], NT)
 
-            @pl.when(across)
-            def _():
-                ex[row, :, cols] = back.astype(jnp.bfloat16)
-
-            @pl.when(jnp.logical_not(across))
-            def _():
-                ez[row, :, cols] = back.astype(jnp.bfloat16)
-
+            partials[row + jnp.where(across, A, 0), :, cols] = back.astype(jnp.bfloat16)
             return 0
 
-        lax.fori_loop(0, D // 512, columns, 0)
+        lax.fori_loop(0, D // 512, columns, 0, unroll=True)
         d_copy(s, slot).start()
 
         @pl.when(s != me)
@@ -664,23 +612,30 @@
         lax.fori_loop(0, HALVES, one, 0)
 
     def block_step(step, _):
-        @pl.when((step == n - 1) & ((a == 0) | (a == A - 1)))
-        def _():
-            sum_parts(jnp.where(a == 0, 1, A - 2))
-
-        take(entry(TAKE_FIRST, a, step))
-        take(entry(TAKE_SECOND, a, step))
-        take(entry(TAKE_THIRD, a, step))
-        code = entry(BLOCK_ORDER, a, step)
+        for place in range(A // 2):
+            for at, words in enumerate(BEFORE_STEP[place]):
+                if words:
+                    @pl.when((near == place) & (step == at))
+                    def _():
+                        move(words)
+
+        code = entry(BLOCK_ORDER, near, step)
         across = code >= A
-        row = code % A
+        row = turned(code % A)
         s = row * B + jnp.where(across, 1 - b, b)
         compute(step, s, row, across)
-
-        @pl.when(across)
-        def _():
-            for part in range(HALVES):
-                x_copy(row, part).start()
+        for place in range(A // 2):
+            for at, rows in enumerate(SUMS_ACROSS[place]):
+                if rows:
+                    @pl.when((near == place) & (step == at))
+                    def _():
+                        for row in rows:
+                            for part in range(HALVES):
+                                x_copy(turned(row), part).start()
+
+        @pl.when((near == 0) & (step == n - 2))
+        def _():
+            sum_parts(turned(2))
 
         return 0
 
@@ -739,25 +694,22 @@
             pltpu.make_async_copy(tile_f32.at[index], grads_out.at[index], out_sem.at[index]).start()
 
     def sum_step(place, _):
-        row = entry(SUM_ORDER, a, place)
-
-        @pl.when(row < A)
-        def _():
-            sum_parts(row)
-
-        @pl.when(place < 4)
-        def _():
-            def pair(e, _):
-                weight_tile(place, e, 0, h_all, gu[:, pl.ds(pl.multiple_of(2 * e * F, 128), F)])
-                weight_tile(place, e, 1, h_all, gu[:, pl.ds(pl.multiple_of((2 * e + 1) * F, 128), F)])
-                weight_tile(place, e, 2, u_all, act[:, pl.ds(pl.multiple_of(e * F, 128), F)])
-                return 0
-
-            lax.fori_loop(0, 2, pair, 0)
+        code = entry(SUM_ORDER, near, place)
+
+        @pl.when(code < A)
+        def _():
+            sum_parts(turned(code))
+
+        @pl.when(place < 8)
+        def _():
+            group, e = place // 2, place % 2
+            weight_tile(group, e, 0, h_all, gu[:, pl.ds(pl.multiple_of(2 * e * F, 128), F)])
+            weight_tile(group, e, 1, h_all, gu[:, pl.ds(pl.multiple_of((2 * e + 1) * F, 128), F)])
+            weight_tile(group, e, 2, u_all, act[:, pl.ds(pl.multiple_of(e * F, 128), F)])
 
         return 0
 
-    lax.fori_loop(0, 5, sum_step, 0)
+    lax.fori_loop(0, 9, sum_step, 0)
 
     for kind in range(3):
         core_copy(kind, 1, 3 + kind).wait_send()
@@ -769,29 +721,31 @@
             def _():
                 z_up(row, part).wait_send()
 
-    for row in range(A):
-        s = row * B + b
-        far = row * B + 1 - b
-
-        @pl.when((row <= a) & (a < A - 1))
-        def _():
-            send_up(s).wait_send()
-
-        @pl.when((row >= a) & (a > 0))
-        def _():
-            send_down(s).wait_send()
-
-        @pl.when((row <= a) & (a < A - 1) & (row < A - 2))
-        def _():
-            send_up(far).wait_send()
-
-        @pl.when((row >= a) & (a > 0) & (row > 1))
-        def _():
-            send_down(far).wait_send()
-
-        @pl.when((row == a) | ((a == 0) & (row == 1)) | ((a == A - 1) & (row == A - 2)))
-        def _():
-            send_across(s).wait_send()
+    @pl.when(a < A - 1)
+    def _():
+        send_up(me).wait_send()
+
+    @pl.when(a > 0)
+    def _():
+        send_down(me).wait_send()
+
+    send_across(me).wait_send()
+    for place in range(A // 2):
+        @pl.when(near == place)
+        def _():
+            for word in [word for words in BEFORE_STEP[place] for word in words]:
+                code = int(word[1:])
+                s = turned(code % A) * B + (1 - b if code >= A else b)
+                if word[0] == "X":
+                    send_across(s).wait_send()
+                elif word[0] != "W":
+                    @pl.when(flipped != (word[0] == "A"))
+                    def _():
+                        send_up(s).wait_send()
+
+                    @pl.when(flipped == (word[0] == "A"))
+                    def _():
+                        send_down(s).wait_send()
 
     for k in range(1, n):
         s = (me + k) % n
@@ -836,8 +790,7 @@
             pltpu.VMEM((2, D, F), bf),
             pltpu.VMEM((n * R, 2 * F), bf),
             pltpu.VMEM((n * R, 4 * F), bf),
-            pltpu.VMEM((A, R, D), bf),
-            pltpu.VMEM((A, R, D), bf),
+            pltpu.VMEM((2 * A, R, D), bf),
             pltpu.VMEM((A, R, D), bf),
             pltpu.VMEM((A + 1, R, D), bf),
             pltpu.VMEM((2, R, D), bf),
@@ -1065,13 +1018,14 @@
 def front_kernel(
     lengths, tokens, routes, w_gain, w_small, w_q, w_k, w_v, w_o, u_in,
     out_gain, out_small, out_q, out_k, out_v, out_o, u_all,
-    hidden_one, qkv, attended, log_total, cos_out, sin_out, residual, hidden_two, probs_out, by_owner,
+    left_out, qkv, log_total, cos_out, sin_out, residual, hidden_two, probs_out, by_owner,
     all_gain, all_small, all_q, all_k, all_v, all_o, sums, q_heads, k_heads, v_heads, mixed,
     keep_sem, core_send, y_send, pass_send, w_recv, u_keep, u_up, u_down, u_across, u_recv,
 ):
     A, B = 4, 2
     R, D = tokens.shape
     shard = D // 4
+    attended, hidden_one = left_out.at[0], left_out.at[1]
     me = lax.axis_index("expert")
     dp = lax.axis_index("dp")
     a, b = me // B, me % B
@@ -1375,9 +1329,8 @@
         out_shape=tuple(jax.ShapeDtypeStruct((4, *w.shape), bf) for w in shards)
         + (
             jax.ShapeDtypeStruct((n, R, D), bf),
-            jax.ShapeDtypeStruct((R, D), bf),
+            jax.ShapeDtypeStruct((2, R, D), bf),
             jax.ShapeDtypeStruct((R, whole), bf),
-            jax.ShapeDtypeStruct((R, D), bf),
             jax.ShapeDtypeStruct((R, 128), f32),
             jax.ShapeDtypeStruct((R, 128), f32),
             jax.ShapeDtypeStruct((R, 128), f32),
@@ -1387,7 +1340,7 @@
             jax.ShapeDtypeStruct((n, 8, R), f32),
         ),
         in_specs=[pl.BlockSpec(memory_space=pltpu.SMEM)] + [vmem] * 9,
-        out_specs=(any_spec,) * 7 + (vmem,) * 10,
+        out_specs=(any_spec,) * 7 + (vmem,) * 9,
         scratch_shapes=[pltpu.VMEM((4, *w.shape), bf) for w in shards]
         + [
             pltpu.VMEM((R, whole), f32),
@@ -1403,6 +1356,177 @@
         cost_estimate=pl.CostEstimate(flops=4 * 10**9, bytes_accessed=40 * 10**6, transcendentals=2 * 10**6),
         name="front",
     )(seq_lengths, tokens, routes, *shards, out_grad)
+
+
+def back_kernel(
+    lengths, row_sum, grad_rows, probs, small, gains, tokens, out_grad, residual, hidden_two, qkv, log_total,
+    cos_table, sin_table, in_q, in_k, in_v, in_o,
+    right, extra, in_grad,
+    w_q, w_k, w_v, w_o, turned, head_grads, q_heads, k_heads, v_heads, q_sums, k_sums, v_sums, wide, load_sem,
+):
+    R, D = tokens.shape
+    shard = D // 4
+    local, groups = 2, grad_rows.shape[0]
+    expert_count = local * groups
+    loads = [
+        pltpu.make_async_copy(src, dst, load_sem.at[i])
+        for i, (src, dst) in enumerate(((in_o, w_o), (in_q, w_q), (in_k, w_k), (in_v, w_v)))
+    ]
+    for load in loads:
+        load.start()
+    lane = lax.broadcasted_iota(jnp.int32, (R, 128), 1)
+
+    turned[...] = jnp.zeros_like(turned)
+    for owner in range(groups):
+        turned[owner * local : (owner + 1) * local, :] = grad_rows[owner, 0:local, :]
+    gate_grad = jnp.transpose(turned[...])
+    dense = probs[...]
+    logit_grad = dense * (gate_grad - jnp.sum(dense * gate_grad, axis=1, keepdims=True))
+    logit_grad = logit_grad.astype(jnp.bfloat16)
+
+    whole = residual[...]
+    scale_two = lax.rsqrt(jnp.mean(whole * whole, axis=1, keepdims=True) + eps)
+    mean_two = jnp.zeros((R, 1), jnp.float32)
+    marks = [(lane == expert_count + k).astype(jnp.bfloat16) for k in range(2)]
+    for j in range(4):
+        cols = slice(j * shard, (j + 1) * shard)
+        rows = row_sum[:, cols] + dot_f32(logit_grad, small[j], NT)
+        normed = whole[:, cols] * scale_two
+        product = rows * normed
+        high = product.astype(jnp.bfloat16)
+        rest = (product - high.astype(jnp.float32)).astype(jnp.bfloat16)
+        part = dot_f32(hidden_two[:, cols], logit_grad, TN)
+        wide[:, cols] = rows
+        extra[cols, :] = (part + dot_f32(high, marks[1], TN) + dot_f32(rest, marks[1], TN)).astype(jnp.bfloat16)
+        gain = gains[j, 1:2, :].astype(jnp.float32)
+        mean_two = mean_two + jnp.sum(product * gain, axis=1, keepdims=True)
+    mean_two = mean_two * (1.0 / D)
+    for j in range(4):
+        cols = slice(j * shard, (j + 1) * shard)
+        gain = gains[j, 1:2, :].astype(jnp.float32)
+        normed = whole[:, cols] * scale_two
+        value = out_grad[:, cols].astype(jnp.float32) + scale_two * (wide[:, cols] * gain - normed * mean_two)
+        in_grad[:, cols] = value
+        right[:, cols] = value.astype(jnp.bfloat16)
+
+    loads[0].wait()
+    for j in range(4):
+        part = dot_f32(right[:, 0:D], w_o[j], NT).astype(jnp.bfloat16)
+        for k in range(shard // HD):
+            head_grads[j * (shard // HD) + k] = part[:, k * HD : (k + 1) * HD]
+    for head in range(QH):
+        q_heads[head] = qkv[:, head * HD : (head + 1) * HD]
+    for g in range(KVH):
+        k_heads[g] = qkv[:, D + g * HD : D + (g + 1) * HD]
+        v_heads[g] = qkv[:, D + (KVH + g) * HD : D + (KVH + g + 1) * HD]
+
+    ends = (lengths[0, 0], lengths[0, 0] + lengths[0, 1], lengths[0, 0] + lengths[0, 1] + lengths[0, 2])
+
+    def doc_of(index):
+        total = 0
+        for end in ends:
+            total = total + jnp.where(index >= end, 1, 0)
+        return total
+
+    rows_t = lax.broadcasted_iota(jnp.int32, (R, R), 0)
+    rows_u = lax.broadcasted_iota(jnp.int32, (R, R), 1)
+    allowed = (doc_of(rows_t) == doc_of(rows_u)) & (rows_u <= rows_t)
+    score_scale = HD**-0.5
+
+    def group_step(g, _):
+        key_total = jnp.zeros((R, HD), jnp.float32)
+        value_total = jnp.zeros((R, HD), jnp.float32)
+        for k in range(QH // KVH):
+            head = g * (QH // KVH) + k
+            scores = dot_f32(q_heads[head], k_heads[g], NT) * score_scale
+            log_head = jnp.sum(jnp.where(lane == head, log_total[...], 0.0), axis=1, keepdims=True)
+            head_probs = jnp.exp(jnp.where(allowed, scores - log_head, masked_score))
+            prob_grad = dot_f32(head_grads[head], v_heads[g], NT)
+            centre = jnp.sum(head_probs * prob_grad, axis=1, keepdims=True)
+            score_grad = (head_probs * (prob_grad - centre)).astype(jnp.bfloat16)
+            q_sums[head] = dot_f32(score_grad, k_heads[g]) * score_scale
+            key_total = key_total + dot_f32(score_grad, q_heads[head], TN)
+            value_total = value_total + dot_f32(head_probs.astype(jnp.bfloat16), head_grads[head], TN)
+        k_sums[g] = key_total * score_scale
+        v_sums[g] = value_total
+        return 0
+
+    lax.fori_loop(0, KVH, group_step, 0)
+
+    front = lane % HD < HD // 2
+
+    def turn_back(first, second):
+        value = jnp.concatenate([first, second], axis=1)
+        other = jnp.where(front, pltpu.roll(value, 128 - HD // 2, 1), pltpu.roll(value, HD // 2, 1))
+        return (value * cos_table[...] - other * sin_table[...]).astype(jnp.bfloat16)
+
+    for i in range(QH // 2):
+        right[:, D + i * 128 : D + (i + 1) * 128] = turn_back(q_sums[2 * i], q_sums[2 * i + 1])
+    key_at, value_at = D + QH * HD, D + (QH + KVH) * HD
+    for i in range(KVH // 2):
+        right[:, key_at + i * 128 : key_at + (i + 1) * 128] = turn_back(k_sums[2 * i], k_sums[2 * i + 1])
+        right[:, value_at + i * 128 : value_at + (i + 1) * 128] = jnp.concatenate(
+            [v_sums[2 * i], v_sums[2 * i + 1]], axis=1
+        ).astype(jnp.bfloat16)
+    right[:, value_at + KVH * HD :] = jnp.zeros((R, 128), jnp.bfloat16)
+
+    for load in loads[1:]:
+        load.wait()
+    inputs = tokens[...].astype(jnp.float32)
+    scale_one = lax.rsqrt(jnp.mean(inputs * inputs, axis=1, keepdims=True) + eps)
+    mean_one = jnp.zeros((R, 1), jnp.float32)
+    for j in range(4):
+        cols = slice(j * shard, (j + 1) * shard)
+        rows = dot_f32(right[:, D:key_at], w_q[j], NT)
+        rows = rows + dot_f32(right[:, key_at:value_at], w_k[j], NT)
+        rows = rows + dot_f32(right[:, value_at : value_at + KVH * HD], w_v[j], NT)
+        wide[:, cols] = rows
+        product = rows * (inputs[:, cols] * scale_one)
+        high = product.astype(jnp.bfloat16)
+        rest = (product - high.astype(jnp.float32)).astype(jnp.bfloat16)
+        part = dot_f32(high, marks[0], TN) + dot_f32(rest, marks[0], TN)
+        extra[cols, :] = (extra[cols, :].astype(jnp.float32) + part).astype(jnp.bfloat16)
+        gain = gains[j, 0:1, :].astype(jnp.float32)
+        mean_one = mean_one + jnp.sum(product * gain, axis=1, keepdims=True)
+    mean_one = mean_one * (1.0 / D)
+    for j in range(4):
+        cols = slice(j * shard, (j + 1) * shard)
+        gain = gains[j, 0:1, :].astype(jnp.float32)
+        normed = inputs[:, cols] * scale_one
+        in_grad[:, cols] = in_grad[:, cols] + scale_one * (wide[:, cols] * gain - normed * mean_one)
+
+
+def back_call(seq_lengths, row_sum, grad_rows, probs, small, gains, tokens, out_grad, residual, hidden_two, qkv, log_total, cos_table, sin_table, *weights):
+    R, D = tokens.shape
+    bf, f32 = jnp.bfloat16, jnp.float32
+    any_spec = pl.BlockSpec(memory_space=pl.ANY)
+    vmem = pl.BlockSpec(memory_space=pltpu.VMEM)
+    return pl.pallas_call(
+        back_kernel,
+        out_shape=(
+            jax.ShapeDtypeStruct((R, D + qkv.shape[1] + 128), bf),
+            jax.ShapeDtypeStruct((D, 128), bf),
+            jax.ShapeDtypeStruct((R, D), f32),
+        ),
+        in_specs=[pl.BlockSpec(memory_space=pltpu.SMEM)] + [vmem] * 13 + [any_spec] * 4,
+        out_specs=(vmem,) * 3,
+        scratch_shapes=[pltpu.VMEM(w.shape, bf) for w in weights]
+        + [
+            pltpu.VMEM((128, R), f32),
+            pltpu.VMEM((QH, R, HD), bf),
+            pltpu.VMEM((QH, R, HD), bf),
+            pltpu.VMEM((KVH, R, HD), bf),
+            pltpu.VMEM((KVH, R, HD), bf),
+            pltpu.VMEM((QH, R, HD), f32),
+            pltpu.VMEM((KVH, R, HD), f32),
+            pltpu.VMEM((KVH, R, HD), f32),
+            pltpu.VMEM((R, D), f32),
+            pltpu.SemaphoreType.DMA((4,)),
+        ],
+        compiler_params=pltpu.CompilerParams(vmem_limit_bytes=60 * 1024 * 1024),
+        cost_estimate=pl.CostEstimate(flops=6 * 10**9, bytes_accessed=30 * 10**6, transcendentals=2 * 10**6),
+        name="back",
+    )(seq_lengths, row_sum, grad_rows, probs, small, gains, tokens, out_grad, residual, hidden_two, qkv, log_total, cos_table, sin_table, *weights)
 
 
 def fused_body(
@@ -1421,95 +1545,25 @@
     expert_down,
     out_grad,
 ):
-    row_count, width = tokens.shape
+    width = tokens.shape[1]
     expert_count = w_router.shape[1]
-    local_count = expert_gate.shape[0]
-    group_size = QH // KVH
-    score_scale = HD ** (-0.5)
     gains = jnp.pad(jnp.stack([attn_gain, moe_gain]), ((0, 14), (0, 0)))
     small = jnp.pad(w_router, ((0, 0), (0, 128 - expert_count)))
     (
         gains, small, query_w, key_w, value_w, output_w, all_upstream,
-        hidden_one, qkv, attended, log_total, cos_table, sin_table, residual, hidden_two, probs, by_owner,
+        left, qkv, log_total, cos_table, sin_table, residual, hidden_two, probs, by_owner,
     ) = front_call(seq_lengths, tokens, routes, gains, small, w_query, w_key, w_value, w_output, out_grad)
-    query_w, key_w, value_w, output_w = [w.reshape(-1, w.shape[2]) for w in (query_w, key_w, value_w, output_w)]
-    gain_one, gain_two = gains[:, 0].reshape(-1), gains[:, 1].reshape(-1)
-    router_w = small.reshape(width, -1)
-
     mix_part, row_sum, grad_rows, own_grads, _, far_grads = moe_call(
         hidden_two, all_upstream, by_owner, expert_gate, expert_up, expert_down
     )
     far_grads = lax.ppermute(far_grads, "dp", [(0, 2), (1, 3), (2, 0), (3, 1)])
     mixture = lax.psum_scatter(mix_part.reshape(-1, width), "expert", scatter_dimension=0, tiled=True)
 
-    inputs = tokens.astype(jnp.float32)
-    upstream = out_grad.astype(jnp.float32)
-    scale_one = rms_scale(inputs)
-    normed_one = inputs * scale_one
-    scale_two = rms_scale(residual)
-    normed_two = residual * scale_two
-    grad_dense = grad_rows[:, :local_count].reshape(expert_count, row_count).T
-    dense = probs[:, :expert_count]
-    logit_grad = (dense * (grad_dense - jnp.sum(dense * grad_dense, axis=-1, keepdims=True))).astype(jnp.bfloat16)
-    logit_grad = jnp.pad(logit_grad, ((0, 0), (0, 128 - expert_count)))
-    hidden_two_grad = row_sum + jnp.dot(logit_grad, router_w.T, preferred_element_type=jnp.float32)
-    gain_two_partial = jnp.sum(hidden_two_grad * normed_two, axis=0)
-    normed_two_grad = hidden_two_grad * gain_two.astype(jnp.float32)
-    residual_grad = upstream + scale_two * (
-        normed_two_grad - normed_two * jnp.mean(normed_two_grad * normed_two, axis=-1, keepdims=True)
-    )
-    branch_grad = residual_grad.astype(jnp.bfloat16)
-    attended_grad = jnp.dot(branch_grad, output_w.T, preferred_element_type=jnp.float32).astype(jnp.bfloat16)
-
-    doc_id, _ = token_layout(seq_lengths[0], row_count)
-    token_index = jnp.arange(row_count, dtype=jnp.int32)
-    allowed = (doc_id[:, None] == doc_id[None, :]) & (token_index[None, :] <= token_index[:, None])
-    query_heads = qkv[:, : QH * HD].reshape(row_count, KVH, group_size, HD)
-    key_heads = qkv[:, QH * HD : (QH + KVH) * HD].reshape(row_count, KVH, HD)
-    value_heads = qkv[:, (QH + KVH) * HD :].reshape(row_count, KVH, HD)
-    scores = jnp.einsum("tkgd,ukd->kgtu", query_heads, key_heads, preferred_element_type=jnp.float32) * score_scale
-    scores = jnp.where(allowed, scores, masked_score)
-    log_heads = log_total[:, :QH].T.reshape(KVH, group_size, row_count, 1)
-    attn_probs = jnp.exp(scores - log_heads)
-    probs_low = attn_probs.astype(jnp.bfloat16)
-    grad_heads = attended_grad.reshape(row_count, KVH, group_size, HD)
-    prob_grad = jnp.einsum("tkgd,ukd->kgtu", grad_heads, value_heads, preferred_element_type=jnp.float32)
-    score_grad = (
-        attn_probs * (prob_grad - jnp.sum(attn_probs * prob_grad, axis=-1, keepdims=True))
-    ).astype(jnp.bfloat16)
-    query_sums = (
-        jnp.einsum("kgtu,ukd->tkgd", score_grad, key_heads, preferred_element_type=jnp.float32) * score_scale
-    )
-    key_sums = (
-        jnp.einsum("kgtu,tkgd->ukd", score_grad, query_heads, preferred_element_type=jnp.float32) * score_scale
-    )
-    value_sums = jnp.einsum("kgtu,tkgd->ukd", probs_low, grad_heads, preferred_element_type=jnp.float32)
-    half_size = HD // 2
-    cosines, sines = cos_table[:, None, :half_size], sin_table[:, None, half_size:HD]
-    query_grad = unrotate(query_sums.reshape(row_count, QH * HD), cosines, sines, QH).astype(jnp.bfloat16)
-    key_grad = unrotate(key_sums.reshape(row_count, KVH * HD), cosines, sines, KVH).astype(jnp.bfloat16)
-    value_grad = value_sums.reshape(row_count, KVH * HD).astype(jnp.bfloat16)
-    hidden_one_grad = jnp.dot(query_grad, query_w.T, preferred_element_type=jnp.float32)
-    hidden_one_grad = hidden_one_grad + jnp.dot(key_grad, key_w.T, preferred_element_type=jnp.float32)
-    hidden_one_grad = hidden_one_grad + jnp.dot(value_grad, value_w.T, preferred_element_type=jnp.float32)
-    gain_one_partial = jnp.sum(hidden_one_grad * normed_one, axis=0)
-    normed_one_grad = hidden_one_grad * gain_one.astype(jnp.float32)
-    in_grad = residual_grad + scale_one * (
-        normed_one_grad - normed_one * jnp.mean(normed_one_grad * normed_one, axis=-1, keepdims=True)
-    )
-    router_partial = jnp.dot(hidden_two.T, logit_grad, preferred_element_type=jnp.float32)
-    column = jnp.arange(128, dtype=jnp.int32)[None, :]
-    extra = jnp.where(
-        column == expert_count,
-        gain_one_partial[:, None],
-        jnp.where(column == expert_count + 1, gain_two_partial[:, None], router_partial),
-    ).astype(jnp.bfloat16)
-    zero_columns = jnp.zeros((row_count, 128), jnp.bfloat16)
-    sums = reduce_call(
-        jnp.stack([attended, hidden_one]),
-        jnp.concatenate([branch_grad, query_grad, key_grad, value_grad, zero_columns], axis=1),
-        extra,
-    )
+    right, extra, in_grad = back_call(
+        seq_lengths, row_sum, grad_rows, probs, small, gains, tokens, out_grad, residual, hidden_two, qkv, log_total,
+        cos_table, sin_table, query_w, key_w, value_w, output_w,
+    )
+    sums = reduce_call(left, right, extra)
     wide, narrow = QH * HD, KVH * HD
     cuts = (0, wide, 2 * wide, 2 * wide + narrow, 2 * wide + 2 * narrow)
     of_output, of_query, of_key, of_value = [sums[:, i:j] for i, j in zip(cuts, cuts[1:])]

time: 481 us -> 457 us (0.950)
  Pallas kernels: 390 us -> 420 us
  matrix products: 23.2 us -> 0 us
  local copies, waits for them, and re-layouts: 35.3 us -> 17.9 us
  other arithmetic: 16.1 us -> 3.88 us
    pallas_call x0 -> x1, Pallas kernels: none -> 27.5 us  [back_call(): pl.pallas_call(back_kernel, out_shape=(jax.ShapeDtypeStruct((R, D + qkv.s...]
    dot_general x11 -> x0, matrix products: 23.2 us -> none  [the longest x1 4.46 us: fused_body(): jnp.einsum('kgtu,tkgd->ukd', probs_low, grad_heads, preferred_element_typ...]
    pallas_call x1, Pallas kernels: 137 us -> 148 us  [reduce_call(): pl.pallas_call(reduce_kernel, out_shape=jax.ShapeDtypeStruct((shard, widt...]
    pallas_call x1, Pallas kernels: 164 us -> 155 us  [moe_call(): pl.pallas_call(functools.partial(moe_kernel, comm=True), out_shape=out_sh...]
    unnamed x76 -> x9, local copies, waits for them, and re-layouts: 11 us -> 3.04 us
    slice x9 -> x0, local copies, waits for them, and re-layouts: 5.13 us -> none  [the longest x2 1.9 us: fused_body(): value_heads = qkv[:, (QH + KVH) * HD:].reshape(row_count, KVH, HD)]
  transfers between devices with their start and end apart: 2 -> 2, of which waited for: 0 -> 0; matrix products, arithmetic and copies ran while one was open for 13% -> 3% of each run, Pallas kernels for 29% -> 39%
where the time goes in v5:
time: 457 us
  Pallas kernels  420 us (92%)
  local copies, waits for them, and re-layouts  17.9 us (4%)
  between operations  14.1 us (3%)
    pallas_call x1, Pallas kernels, moe_call(): pl.pallas_call(functools.partial(moe_kernel, comm=True), out_shape=out_sh...  155 us
    pallas_call x1, Pallas kernels, reduce_call(): pl.pallas_call(reduce_kernel, out_shape=jax.ShapeDtypeStruct((shard, widt...  148 us
    pallas_call x1, Pallas kernels, front_call(): pl.pallas_call(front_kernel, out_shape=tuple((jax.ShapeDtypeStruct((4, *w...  88.9 us
    pallas_call x1, Pallas kernels, back_call(): pl.pallas_call(back_kernel, out_shape=(jax.ShapeDtypeStruct((R, D + qkv.s...  27.5 us
  transfers between devices with their start and end apart: 2, of which 0 were waited for; matrix products, arithmetic and copies ran while one was open for 3% of the time, Pallas kernels for 39%

profile of v5, /device:TPU:0, one launch (start us, length us, event | category | flops | bytes accessed | tf_op | source)
XLA Modules:
  0.0 456.6 jit_solution(17498296846368160017)
XLA Ops:
  7.2 0.0 reduce-scatter.2.cloned.1.call-start
  7.2 0.7 stack.9
  7.9 0.7 stack.10
  8.6 0.8 copy.29
  9.4 1.5 copy.30.routes
  10.9 0.6 fusion.2.w_gain
  11.5 0.7 pad.9.w_small
  12.2 88.9 %front.1 = (bf16[4,16,384]{2,1,0:T(8,128)(2,1)}, bf16[4,384,128]{2,1,0:T(8,128)(2,1)}, bf16[4,384,1536]{2,1,0:T(8,128)(2,1)}, bf16[4,384,512]{2,1,0:T(8,128)(2,1...) custom-call(s32[1,4]{1,0:T(1,128)} %lengths.3, ...), custom_call_target="tpu_custom_call" | custom-call | flops 4000000000 | bytes 40000000 | tf_op jit(solution)/shard_map/front/pallas_call | solution.py:1327
  101.1 155.1 %experts.1 = (bf16[8,256,1536]{2,1,0:T(8,128)(2,1)}, f32[256,1536]{1,0:T(8,128)}, f32[8,8,256]{2,1,0:T(8,128)}, f32[6,384,512]{2,1,0:T(8,128)}, bf16[2,6,384,512...) custom-call(bf16[256,1536]{1,0:T(8,128)(2,1)} %get-tuple-element.38.h_in.hidden_two, ...), custom_call_target="tpu_custom_call" | custom-call | flops 57999998976 | bytes 60000000 | tf_op jit(solution)/shard_map/experts/pallas_call | solution.py:779
  256.2 0.0 reduce-scatter.2.cloned.1.call-update
  256.2 0.6 collective-permute-start
  256.8 27.5 %back.1 = (bf16[256,4224]{1,0:T(8,128)(2,1)}, bf16[1536,128]{1,0:T(8,128)(2,1)}, f32[256,1536]{1,0:T(8,128)}) custom-call(s32[1,4]{1,0:T(1,128)} %lengths.3, f32[256,1536]{1,0:T(8,128)} %get-tuple-element.44.row_sum, f32[8,8,256]{2,1,0:T(8,128)} %get-tuple-element.45.grad_rows, f32[256,128]{1,0:T(8,128)} %get-tuple-element.46.probs, ...), custom_call_target="tpu_custom_call" | custom-call | flops 6000000000 | bytes 30000000 | tf_op jit(solution)/shard_map/back/pallas_call | solution.py:1504
  284.3 148.5 %weight_sums.1 = f32[384,4224]{1,0:T(8,128)} custom-call(bf16[2,256,1536]{2,1,0:T(8,128)(2,1)} %get-tuple-element.43.left, bf16[256,4224]{1,0:T(8,128)(2,1)} %get-tuple-element.57.right, bf16[1536,128]{1,0:T(8,128)(2,1)} %get-tuple-element.58.extra), custom_call_target="tpu_custom_call" | custom-call | flops 4000000000 | bytes 20000000 | tf_op jit(solution)/shard_map/weight_sums/pallas_call | solution.py:990
  432.8 0.9 slice.38
  433.8 0.7 copy.31
  434.5 1.9 slice_reduce_fusion
  436.4 2.8 fusion.4
  439.2 4.9 %fusion.3 = (f32[384,1536]{1,0:T(8,128)}, f32[384,1536]{1,0:T(8,128)}) fusion(f32[384,4224]{1,0:T(8,128)} %weight_sums.1), kind=kLoop, calls=%fused_computation.8 | loop fusion | bytes 9437184 | tf_op jit(solution)/shard_map/slice | solution.py:1569
  444.1 0.0 collective-permute-done
  444.1 0.0 slice-done
  444.1 0.0 slice-done.1
  444.1 1.1 convert_add_fusion
  445.2 2.3 fusion.5
  447.5 2.2 add_convert_fusion
  (6 shorter events, 0.0 us)
Async XLA Ops:
  7.2 440.3 %reduce-scatter.2.cloned.1.call-start = ((), (), s32[]{:S(2)}) async-start(), calls=%async_computation.1 | async-start | bytes 7077888 | tf_op jit(solution)/shard_map/reduce_scatter | solution.py:1560
  256.2 187.9 %collective-permute-start = (bf16[6,384,512]{2,1,0:T(8,128)(2,1)}, bf16[6,384,512]{2,1,0:T(8,128)(2,1)S(1)}, u32[]{:S(2)}, u32[]{:S(2)}) collective-permute-start(bf16[6,384,512]{2,1,0:T(8,128)(2,1)} %get-tuple-element.41), channel_id=1, source_target_pairs={{0,16},{8,24},{16,0},{24,8},{1,17},{9,25},{17,1},{25,9},{2,18},{10... | collective-permute-start | bytes 7077896 | tf_op jit(solution)/shard_map/ppermute | solution.py:1559
  436.4 7.7 %slice-start = ((s8[4718592]{0:T(1024)(128)(4,1)}), s8[4194304]{0:T(1024)(128)(4,1)S(1)}, s32[]{:S(2)}) async-start(s8[4718592]{0:T(1024)(128)(4,1)} %bitcast.2), calls=%async_computation.2 | async-start | bytes 8388608
  439.2 4.9 %slice-start.1 = ((s8[4718592]{0:T(1024)(128)(4,1)}), s8[524288]{0:T(1024)(128)(4,1)S(1)}, s32[]{:S(2)}) async-start(s8[4718592]{0:T(1024)(128)(4,1)} %bitcast.2), calls=%async_computation.3 | async-start | bytes 1048576
  445.2 2.3 copy-start
Sparse Core Ops, SparseCore 0:
  256.3 156.4 reduce-scatter.1

commit v6 on v5

--- a/solution.py
+++ b/solution.py
@@ -812,8 +812,8 @@
 
 def reduce_kernel(
     left, right, extra, out,
-    core_out, core_in, y_out, y_in, half, x_out, x_in, own, z_out, z_in, full,
-    core_send, core_recv, y_send, y_recv, x_send, x_recv, zs_send, zs_recv, zg_send, zg_recv, xg_send, xg_recv,
+    core_out, core_in, y_out, y_in, half, x_out, x_in, own, z_out, z_in, full, ready,
+    core_send, core_recv, y_send, y_recv, x_send, x_recv, zs_send, zs_recv, zg_send, zg_recv, xg_send, xg_recv, ready_sem,
 ):
     A, B = 4, 2
     W = core_out.shape[3]
@@ -843,7 +843,7 @@
     def partial(chunk, owner):
         rows = pl.ds(pl.multiple_of(owner * shard, 128), shard)
         cols = pl.ds(pl.multiple_of(chunk * W, 128), W)
-        which = jnp.where(chunk < 4, 0, 1)
+        which = jnp.where(chunk < left.shape[2] // W, 0, 1)
         total = dot_f32(left[which, :, rows], right[:, cols], TN)
         share = extra[pl.ds(pl.multiple_of(owner * shard, 128), shard), :].astype(jnp.float32)
         share = jnp.where(chunk == chunks - 1, share, 0.0)
@@ -944,10 +944,19 @@
             z_gather(chunk, a, (a + k) % A).wait_recv()
         x_gather(chunk, b).start()
 
+    def written(chunk):
+        cols = pl.ds(pl.multiple_of(chunk * W, 128), W)
+        return pltpu.make_async_copy(ready.at[chunk % 2], out.at[:, cols], ready_sem.at[chunk % 2])
+
     def finish(chunk):
         x_gather(chunk, 1 - b).wait_recv()
-        cols = pl.ds(pl.multiple_of(chunk * W, 128), W)
-        out[:, cols] = full[chunk].astype(jnp.float32)
+
+        @pl.when(chunk >= 2)
+        def _():
+            written(chunk).wait()
+
+        ready[chunk % 2] = full[chunk].astype(jnp.float32)
+        written(chunk).start()
 
     stages = (to_core, to_y, to_x, to_z, spread_z, spread_x, finish)
 
@@ -962,6 +971,7 @@
     lax.fori_loop(0, chunks + len(stages) - 1, step, 0)
 
     for chunk in range(chunks - 2, chunks):
+        written(chunk).wait()
         core_copy(chunk, 0).wait_send()
         core_copy(chunk, 1).wait_send()
         y_copy(chunk).wait_send()
@@ -991,7 +1001,7 @@
         reduce_kernel,
         out_shape=jax.ShapeDtypeStruct((shard, width), f32),
         in_specs=[vmem] * 3,
-        out_specs=vmem,
+        out_specs=pl.BlockSpec(memory_space=pl.ANY),
         scratch_shapes=[
             pltpu.VMEM((2, 2, shard, W), bf),
             pltpu.VMEM((chunks, 2, shard, W), bf),
@@ -1004,8 +1014,9 @@
             pltpu.VMEM((2, shard // B, W), bf),
             pltpu.VMEM((chunks, A, piece, W), bf),
             pltpu.VMEM((chunks, shard, W), bf),
+            pltpu.VMEM((2, shard, W), f32),
             dma((2, 2)), dma((chunks, 2)), dma((2,)), dma((chunks,)), dma((2,)), dma((chunks,)),
-            dma((2, A)), dma((chunks, A)), dma((chunks, A)), dma((chunks, A)), dma((chunks,)), dma((chunks,)),
+            dma((2, A)), dma((chunks, A)), dma((chunks, A)), dma((chunks, A)), dma((chunks,)), dma((chunks,)), dma((2,)),
         ],
         compiler_params=pltpu.CompilerParams(
             collective_id=2, has_side_effects=True, vmem_limit_bytes=56 * 1024 * 1024
@@ -1015,12 +1026,16 @@
     )(left, right, extra)
 
 
+PIECES = 3
+
+
 def front_kernel(
     lengths, tokens, routes, w_gain, w_small, w_q, w_k, w_v, w_o, u_in,
     out_gain, out_small, out_q, out_k, out_v, out_o, u_all,
-    left_out, qkv, log_total, cos_out, sin_out, residual, hidden_two, probs_out, by_owner,
-    all_gain, all_small, all_q, all_k, all_v, all_o, sums, q_heads, k_heads, v_heads, mixed,
+    left_hbm, qkv_hbm, log_total, cos_out, sin_out, residual, hidden_two, probs_out, by_owner,
+    all_gain, all_small, all_q, all_k, all_v, all_o, sums, q_heads, k_heads, v_heads, mixed, left_out, qkv,
     keep_sem, core_send, y_send, pass_send, w_recv, u_keep, u_up, u_down, u_across, u_recv,
+    o_send, o_recv, o_pass, o_far, early_sem,
 ):
     A, B = 4, 2
     R, D = tokens.shape
@@ -1099,6 +1114,25 @@
             def _():
                 u_send_down(u_all.at[s], s).start()
 
+    def o_part(piece):
+        return pl.ds(piece * (shard // PIECES), shard // PIECES)
+
+    def o_to_y(piece):
+        rows = o_part(piece)
+        return copy(w_o.at[rows], all_o.at[dp, rows], o_send.at[piece], o_recv.at[piece], dp=y_peer)
+
+    def o_from_y(piece):
+        rows = o_part(piece)
+        return copy(w_o.at[rows], all_o.at[y_peer, rows], o_send.at[piece], o_recv.at[piece], dp=y_peer)
+
+    def o_pass_on(piece):
+        rows = o_part(piece)
+        return copy(all_o.at[y_peer, rows], all_o.at[y_peer, rows], o_pass.at[piece], o_far.at[piece], dp=core_peer)
+
+    def o_from_core(piece):
+        rows = o_part(piece)
+        return copy(all_o.at[far_peer, rows], all_o.at[far_peer, rows], o_pass.at[piece], o_far.at[piece], dp=core_peer)
+
     keep_u = pltpu.make_async_copy(u_in, u_all.at[me], u_keep)
 
     @pl.when(a < A - 1)
@@ -1111,7 +1145,11 @@
 
     u_send_across(u_in, me).start()
     for i in range(count):
-        to_y(i).start()
+        if i == OUTPUT:
+            for piece in range(PIECES):
+                o_to_y(piece).start()
+        else:
+            to_y(i).start()
         to_core(i).start()
         keep_own(i).start()
     keep_u.start()
@@ -1237,6 +1275,12 @@
         )
 
     residual[...] = inputs
+    early = (
+        pltpu.make_async_copy(left_out, left_hbm, early_sem.at[0]),
+        pltpu.make_async_copy(qkv, qkv_hbm, early_sem.at[1]),
+    )
+    for write in early:
+        write.start()
 
     def out_product(owner, own=False):
         cols = pl.ds(pl.multiple_of(owner * shard, 128), shard)
@@ -1255,10 +1299,25 @@
     out_product(core_peer)
     receive(SMALL, far_peer)
     all_small[dp] = w_small[...]
-    forward(OUTPUT)
-    out_product(y_peer)
-    receive(OUTPUT, far_peer)
-    out_product(far_peer)
+
+    def piece_product(owner, piece):
+        rows = o_part(piece)
+        left = attended[:, pl.ds(pl.multiple_of(owner * shard + piece * (shard // PIECES), 128), shard // PIECES)]
+        for t in range(D // 512):
+            part = slice(t * 512, (t + 1) * 512)
+            residual[:, part] += dot_f32(left, all_o[owner, rows, part])
+
+    for piece in range(PIECES):
+        o_from_y(piece).wait_recv()
+        o_pass_on(piece).start()
+        if piece:
+            o_from_core(piece - 1).wait_recv()
+            piece_product(far_peer, piece - 1)
+        piece_product(y_peer, piece)
+    keep(OUTPUT, y_peer).start()
+    o_from_core(PIECES - 1).wait_recv()
+    piece_product(far_peer, PIECES - 1)
+    keep(OUTPUT, far_peer).start()
 
     whole = residual[...]
     scale_two = lax.rsqrt(jnp.mean(whole * whole, axis=1, keepdims=True) + eps)
@@ -1289,9 +1348,15 @@
         keep_own(i).wait()
         for owner in (core_peer, y_peer, far_peer):
             keep(i, owner).wait()
-        to_y(i).wait_send()
         to_core(i).wait_send()
-        pass_on(i).wait_send()
+        if i != OUTPUT:
+            to_y(i).wait_send()
+            pass_on(i).wait_send()
+    for piece in range(PIECES):
+        o_to_y(piece).wait_send()
+        o_pass_on(piece).wait_send()
+    for write in early:
+        write.wait()
     keep_u.wait()
 
     @pl.when(a < A - 1)
@@ -1340,7 +1405,7 @@
             jax.ShapeDtypeStruct((n, 8, R), f32),
         ),
         in_specs=[pl.BlockSpec(memory_space=pltpu.SMEM)] + [vmem] * 9,
-        out_specs=(any_spec,) * 7 + (vmem,) * 9,
+        out_specs=(any_spec,) * 9 + (vmem,) * 7,
         scratch_shapes=[pltpu.VMEM((4, *w.shape), bf) for w in shards]
         + [
             pltpu.VMEM((R, whole), f32),
@@ -1348,7 +1413,10 @@
             pltpu.VMEM((KVH, R, HD), bf),
             pltpu.VMEM((KVH, R, HD), bf),
             pltpu.VMEM((QH, R, HD), bf),
+            pltpu.VMEM((2, R, D), bf),
+            pltpu.VMEM((R, whole), bf),
             dma((6, 4)), dma((6,)), dma((6,)), dma((6,)), dma((6, 4)), dma, dma((n,)), dma((n,)), dma((n,)), dma((n,)),
+            dma((PIECES,)), dma((PIECES,)), dma((PIECES,)), dma((PIECES,)), dma((2,)),
         ],
         compiler_params=pltpu.CompilerParams(
             collective_id=3, has_side_effects=True, vmem_limit_bytes=60 * 1024 * 1024

time: 457 us -> 455 us (level)
  transfers between devices with their start and end apart: 2 -> 2, of which waited for: 0 -> 0; matrix products, arithmetic and copies ran while one was open for 3% -> 3% of each run, Pallas kernels for 39% -> 38%
where the time goes in v6:
time: 455 us; the launch traced here: 454 us
  Pallas kernels  418 us (92%)
  local copies, waits for them, and re-layouts  17.9 us (4%)
  between operations  14.1 us (3%)
    pallas_call x1, Pallas kernels, moe_call(): pl.pallas_call(functools.partial(moe_kernel, comm=True), out_shape=out_sh...  155 us
    pallas_call x1, Pallas kernels, reduce_call(): pl.pallas_call(reduce_kernel, out_shape=jax.ShapeDtypeStruct((shard, widt...  147 us
    pallas_call x1, Pallas kernels, front_call(): pl.pallas_call(front_kernel, out_shape=tuple((jax.ShapeDtypeStruct((4, *w...  88.1 us
    pallas_call x1, Pallas kernels, back_call(): pl.pallas_call(back_kernel, out_shape=(jax.ShapeDtypeStruct((R, D + qkv.s...  27.5 us
  transfers between devices with their start and end apart: 2, of which 0 were waited for; matrix products, arithmetic and copies ran while one was open for 3% of the time, Pallas kernels for 38%

profile of v6, /device:TPU:0, one launch (start us, length us, event | category | flops | bytes accessed | tf_op | source)
XLA Modules:
  0.0 454.0 jit_solution(7371858145446769732)
XLA Ops:
  7.2 0.0 reduce-scatter.2.cloned.1.call-start
  7.2 0.7 stack.9
  7.9 0.7 stack.10
  8.6 0.8 copy.29
  9.4 1.5 copy.30.routes
  10.9 0.6 fusion.2.w_gain
  11.5 0.7 pad.9.w_small
  12.2 88.1 %front.1 = (bf16[4,16,384]{2,1,0:T(8,128)(2,1)}, bf16[4,384,128]{2,1,0:T(8,128)(2,1)}, bf16[4,384,1536]{2,1,0:T(8,128)(2,1)}, bf16[4,384,512]{2,1,0:T(8,128)(2,1...) custom-call(s32[1,4]{1,0:T(1,128)} %lengths.3, ...), custom_call_target="tpu_custom_call" | custom-call | flops 4000000000 | bytes 40000000 | tf_op jit(solution)/shard_map/front/pallas_call | solution.py:1392
  100.3 155.2 %experts.1 = (bf16[8,256,1536]{2,1,0:T(8,128)(2,1)}, f32[256,1536]{1,0:T(8,128)}, f32[8,8,256]{2,1,0:T(8,128)}, f32[6,384,512]{2,1,0:T(8,128)}, bf16[2,6,384,512...) custom-call(bf16[256,1536]{1,0:T(8,128)(2,1)} %get-tuple-element.38.h_in.hidden_two, ...), custom_call_target="tpu_custom_call" | custom-call | flops 57999998976 | bytes 60000000 | tf_op jit(solution)/shard_map/experts/pallas_call | solution.py:779
  255.5 0.0 reduce-scatter.2.cloned.1.call-update
  255.5 0.5 collective-permute-start
  256.0 27.5 %back.1 = (bf16[256,4224]{1,0:T(8,128)(2,1)}, bf16[1536,128]{1,0:T(8,128)(2,1)}, f32[256,1536]{1,0:T(8,128)}) custom-call(s32[1,4]{1,0:T(1,128)} %lengths.3, f32[256,1536]{1,0:T(8,128)} %get-tuple-element.44.row_sum, f32[8,8,256]{2,1,0:T(8,128)} %get-tuple-element.45.grad_rows, f32[256,128]{1,0:T(8,128)} %get-tuple-element.46.probs, ...), custom_call_target="tpu_custom_call" | custom-call | flops 6000000000 | bytes 30000000 | tf_op jit(solution)/shard_map/back/pallas_call | solution.py:1572
  283.5 146.8 %weight_sums.1 = f32[384,4224]{1,0:T(8,128)} custom-call(bf16[2,256,1536]{2,1,0:T(8,128)(2,1)} %get-tuple-element.43.left, bf16[256,4224]{1,0:T(8,128)(2,1)} %get-tuple-element.57.right, bf16[1536,128]{1,0:T(8,128)(2,1)} %get-tuple-element.58.extra), custom_call_target="tpu_custom_call" | custom-call | flops 4000000000 | bytes 20000000 | tf_op jit(solution)/shard_map/weight_sums/pallas_call | solution.py:1000
  430.3 0.9 slice.38
  431.2 0.7 copy.31
  432.0 1.9 slice_reduce_fusion
  433.9 2.8 fusion.4
  436.6 4.9 %fusion.3 = (f32[384,1536]{1,0:T(8,128)}, f32[384,1536]{1,0:T(8,128)}) fusion(f32[384,4224]{1,0:T(8,128)} %weight_sums.1), kind=kLoop, calls=%fused_computation.8 | loop fusion | bytes 9437184 | tf_op jit(solution)/shard_map/slice | solution.py:1637
  441.6 0.0 collective-permute-done
  441.6 0.0 slice-done
  441.6 0.0 slice-done.1
  441.6 1.1 convert_add_fusion
  442.7 2.3 fusion.5
  445.0 2.2 add_convert_fusion
  (6 shorter events, 0.0 us)
Async XLA Ops:
  7.2 437.8 %reduce-scatter.2.cloned.1.call-start = ((), (), s32[]{:S(2)}) async-start(), calls=%async_computation.1 | async-start | bytes 7077888 | tf_op jit(solution)/shard_map/reduce_scatter | solution.py:1628
  255.5 186.1 %collective-permute-start = (bf16[6,384,512]{2,1,0:T(8,128)(2,1)}, bf16[6,384,512]{2,1,0:T(8,128)(2,1)S(1)}, u32[]{:S(2)}, u32[]{:S(2)}) collective-permute-start(bf16[6,384,512]{2,1,0:T(8,128)(2,1)} %get-tuple-element.41), channel_id=1, source_target_pairs={{0,16},{8,24},{16,0},{24,8},{1,17},{9,25},{17,1},{25,9},{2,18},{10... | collective-permute-start | bytes 7077896 | tf_op jit(solution)/shard_map/ppermute | solution.py:1627
  433.9 7.7 %slice-start = ((s8[4718592]{0:T(1024)(128)(4,1)}), s8[4194304]{0:T(1024)(128)(4,1)S(1)}, s32[]{:S(2)}) async-start(s8[4718592]{0:T(1024)(128)(4,1)} %bitcast.2), calls=%async_computation.2 | async-start | bytes 8388608
  436.6 4.9 %slice-start.1 = ((s8[4718592]{0:T(1024)(128)(4,1)}), s8[524288]{0:T(1024)(128)(4,1)S(1)}, s32[]{:S(2)}) async-start(s8[4718592]{0:T(1024)(128)(4,1)} %bitcast.2), calls=%async_computation.3 | async-start | bytes 1048576
  442.7 2.3 copy-start
Sparse Core Ops, SparseCore 0:
  255.6 156.4 reduce-scatter.1

commit v7 on v6

--- a/solution.py
+++ b/solution.py
@@ -1427,10 +1427,10 @@
 
 
 def back_kernel(
-    lengths, row_sum, grad_rows, probs, small, gains, tokens, out_grad, residual, hidden_two, qkv, log_total,
+    lengths, row_sum, grad_rows, probs, small, gains, tokens_in, out_grad, residual, hidden_two, qkv_in, log_total,
     cos_table, sin_table, in_q, in_k, in_v, in_o,
     right, extra, in_grad,
-    w_q, w_k, w_v, w_o, turned, head_grads, q_heads, k_heads, v_heads, q_sums, k_sums, v_sums, wide, load_sem,
+    tokens, qkv, w_q, w_k, w_v, w_o, turned, head_grads, q_heads, k_heads, v_heads, q_sums, k_sums, v_sums, wide, load_sem,
 ):
     R, D = tokens.shape
     shard = D // 4
@@ -1438,7 +1438,9 @@
     expert_count = local * groups
     loads = [
         pltpu.make_async_copy(src, dst, load_sem.at[i])
-        for i, (src, dst) in enumerate(((in_o, w_o), (in_q, w_q), (in_k, w_k), (in_v, w_v)))
+        for i, (src, dst) in enumerate(
+            ((qkv_in, qkv), (in_o, w_o), (in_q, w_q), (in_k, w_k), (in_v, w_v), (tokens_in, tokens))
+        )
     ]
     for load in loads:
         load.start()
@@ -1478,6 +1480,7 @@
         right[:, cols] = value.astype(jnp.bfloat16)
 
     loads[0].wait()
+    loads[1].wait()
     for j in range(4):
         part = dot_f32(right[:, 0:D], w_o[j], NT).astype(jnp.bfloat16)
         for k in range(shard // HD):
@@ -1538,7 +1541,7 @@
         ).astype(jnp.bfloat16)
     right[:, value_at + KVH * HD :] = jnp.zeros((R, 128), jnp.bfloat16)
 
-    for load in loads[1:]:
+    for load in loads[2:]:
         load.wait()
     inputs = tokens[...].astype(jnp.float32)
     scale_one = lax.rsqrt(jnp.mean(inputs * inputs, axis=1, keepdims=True) + eps)
@@ -1576,9 +1579,11 @@
             jax.ShapeDtypeStruct((D, 128), bf),
             jax.ShapeDtypeStruct((R, D), f32),
         ),
-        in_specs=[pl.BlockSpec(memory_space=pltpu.SMEM)] + [vmem] * 13 + [any_spec] * 4,
+        in_specs=[pl.BlockSpec(memory_space=pltpu.SMEM)]
+        + [any_spec if i in (5, 9) else vmem for i in range(13)]
+        + [any_spec] * 4,
         out_specs=(vmem,) * 3,
-        scratch_shapes=[pltpu.VMEM(w.shape, bf) for w in weights]
+        scratch_shapes=[pltpu.VMEM(w.shape, bf) for w in (tokens, qkv, *weights)]
         + [
             pltpu.VMEM((128, R), f32),
             pltpu.VMEM((QH, R, HD), bf),
@@ -1589,7 +1594,7 @@
             pltpu.VMEM((KVH, R, HD), f32),
             pltpu.VMEM((KVH, R, HD), f32),
             pltpu.VMEM((R, D), f32),
-            pltpu.SemaphoreType.DMA((4,)),
+            pltpu.SemaphoreType.DMA((6,)),
         ],
         compiler_params=pltpu.CompilerParams(vmem_limit_bytes=60 * 1024 * 1024),
         cost_estimate=pl.CostEstimate(flops=6 * 10**9, bytes_accessed=30 * 10**6, transcendentals=2 * 10**6),
@@ -1615,7 +1620,9 @@
 ):
     width = tokens.shape[1]
     expert_count = w_router.shape[1]
-    gains = jnp.pad(jnp.stack([attn_gain, moe_gain]), ((0, 14), (0, 0)))
+    gain_row = lax.broadcasted_iota(jnp.int32, (16, attn_gain.shape[0]), 0)
+    gains = jnp.where(gain_row == 0, attn_gain[None, :], jnp.where(gain_row == 1, moe_gain[None, :], 0))
+    gains = gains.astype(jnp.bfloat16)
     small = jnp.pad(w_router, ((0, 0), (0, 128 - expert_count)))
     (
         gains, small, query_w, key_w, value_w, output_w, all_upstream,

time: 455 us -> 455 us (level)
  no operation moved by 1% of the time
where the time goes in v7:
time: 455 us; the launch traced here: 454 us
  Pallas kernels  418 us (92%)
  local copies, waits for them, and re-layouts  16.6 us (4%)
  between operations  14.1 us (3%)
  other arithmetic  4.65 us (1%)
    pallas_call x1, Pallas kernels, moe_call(): pl.pallas_call(functools.partial(moe_kernel, comm=True), out_shape=out_sh...  155 us
    pallas_call x1, Pallas kernels, reduce_call(): pl.pallas_call(reduce_kernel, out_shape=jax.ShapeDtypeStruct((shard, widt...  147 us
    pallas_call x1, Pallas kernels, front_call(): pl.pallas_call(front_kernel, out_shape=tuple((jax.ShapeDtypeStruct((4, *w...  88.1 us
    pallas_call x1, Pallas kernels, back_call(): pl.pallas_call(back_kernel, out_shape=(jax.ShapeDtypeStruct((R, D + qkv.s...  27.3 us
  transfers between devices with their start and end apart: 2, of which 0 were waited for; matrix products, arithmetic and copies ran while one was open for 3% of the time, Pallas kernels for 38%

profile of v7, /device:TPU:0, one launch (start us, length us, event | category | flops | bytes accessed | tf_op | source)
XLA Modules:
  0.0 453.8 jit_solution(7954075408568924544)
XLA Ops:
  7.2 0.0 reduce-scatter.2.cloned.1.call-start
  7.2 0.8 copy.29
  8.1 1.5 copy.30.routes
  9.6 0.7 pad.4.w_small
  10.2 1.4 select_select_fusion.w_gain
  11.6 88.1 %front.1 = (bf16[4,16,384]{2,1,0:T(8,128)(2,1)}, bf16[4,384,128]{2,1,0:T(8,128)(2,1)}, bf16[4,384,1536]{2,1,0:T(8,128)(2,1)}, bf16[4,384,512]{2,1,0:T(8,128)(2,1...) custom-call(s32[1,4]{1,0:T(1,128)} %lengths.3, ...), custom_call_target="tpu_custom_call" | custom-call | flops 4000000000 | bytes 40000000 | tf_op jit(solution)/shard_map/front/pallas_call | solution.py:1392
  99.7 155.1 %experts.1 = (bf16[8,256,1536]{2,1,0:T(8,128)(2,1)}, f32[256,1536]{1,0:T(8,128)}, f32[8,8,256]{2,1,0:T(8,128)}, f32[6,384,512]{2,1,0:T(8,128)}, bf16[2,6,384,512...) custom-call(bf16[256,1536]{1,0:T(8,128)(2,1)} %get-tuple-element.38.h_in.hidden_two, ...), custom_call_target="tpu_custom_call" | custom-call | flops 57999998976 | bytes 60000000 | tf_op jit(solution)/shard_map/experts/pallas_call | solution.py:779
  254.8 0.0 reduce-scatter.2.cloned.1.call-update
  254.8 0.5 collective-permute-start
  255.3 27.3 %back.1 = (bf16[256,4224]{1,0:T(8,128)(2,1)}, bf16[1536,128]{1,0:T(8,128)(2,1)}, f32[256,1536]{1,0:T(8,128)}) custom-call(s32[1,4]{1,0:T(1,128)} %lengths.3, f32[256,1536]{1,0:T(8,128)} %get-tuple-element.44.row_sum, f32[8,8,256]{2,1,0:T(8,128)} %get-tuple-element.45.grad_rows, f32[256,128]{1,0:T(8,128)} %get-tuple-element.46.probs, ...), custom_call_target="tpu_custom_call" | custom-call | flops 6000000000 | bytes 30000000 | tf_op jit(solution)/shard_map/back/pallas_call | solution.py:1575
  282.7 147.2 %weight_sums.1 = f32[384,4224]{1,0:T(8,128)} custom-call(bf16[2,256,1536]{2,1,0:T(8,128)(2,1)} %get-tuple-element.43.left, bf16[256,4224]{1,0:T(8,128)(2,1)} %get-tuple-element.57.right, bf16[1536,128]{1,0:T(8,128)(2,1)} %get-tuple-element.58.extra), custom_call_target="tpu_custom_call" | custom-call | flops 4000000000 | bytes 20000000 | tf_op jit(solution)/shard_map/weight_sums/pallas_call | solution.py:1000
  429.9 0.9 slice.38
  430.9 0.7 copy.31
  431.6 2.0 slice_reduce_fusion
  433.6 2.8 fusion.1
  436.4 4.9 %fusion = (f32[384,1536]{1,0:T(8,128)}, f32[384,1536]{1,0:T(8,128)}) fusion(f32[384,4224]{1,0:T(8,128)} %weight_sums.1), kind=kLoop, calls=%fused_computation.7 | loop fusion | bytes 9437184 | tf_op jit(solution)/shard_map/slice | solution.py:1644
  441.3 0.0 collective-permute-done
  441.3 0.0 slice-done
  441.3 0.0 slice-done.1
  441.3 1.1 convert_add_fusion
  442.4 0.0 copy-start
  442.4 2.3 fusion.2
  444.7 0.0 copy-done
  444.7 2.2 add_convert_fusion
  (5 shorter events, 0.0 us)
Async XLA Ops:
  7.2 437.5 %reduce-scatter.2.cloned.1.call-start = ((), (), s32[]{:S(2)}) async-start(), calls=%async_computation.1 | async-start | bytes 7077888 | tf_op jit(solution)/shard_map/reduce_scatter | solution.py:1635
  254.8 186.5 %collective-permute-start = (bf16[6,384,512]{2,1,0:T(8,128)(2,1)}, bf16[6,384,512]{2,1,0:T(8,128)(2,1)S(1)}, u32[]{:S(2)}, u32[]{:S(2)}) collective-permute-start(bf16[6,384,512]{2,1,0:T(8,128)(2,1)} %get-tuple-element.41), channel_id=1, source_target_pairs={{0,16},{8,24},{16,0},{24,8},{1,17},{9,25},{17,1},{25,9},{2,18},{10... | collective-permute-start | bytes 7077896 | tf_op jit(solution)/shard_map/ppermute | solution.py:1634
  433.6 7.7 %slice-start = ((s8[4718592]{0:T(1024)(128)(4,1)}), s8[4194304]{0:T(1024)(128)(4,1)S(1)}, s32[]{:S(2)}) async-start(s8[4718592]{0:T(1024)(128)(4,1)} %bitcast.2), calls=%async_computation.2 | async-start | bytes 8388608
  436.4 4.9 %slice-start.1 = ((s8[4718592]{0:T(1024)(128)(4,1)}), s8[524288]{0:T(1024)(128)(4,1)S(1)}, s32[]{:S(2)}) async-start(s8[4718592]{0:T(1024)(128)(4,1)} %bitcast.2), calls=%async_computation.3 | async-start | bytes 1048576
  442.4 2.3 copy-start
Sparse Core Ops, SparseCore 0:
  255.0 156.4 reduce-scatter.1
